TPU v7x, 32 devices: a whole 2x2x4 slice. The times are simulated.
32 devices in a mesh: seq: 8 (over z, x), head: 4 (over y, core).
Axes of the slice: x: 2, y: 2, z: 4, core: 2. Of those that a mesh axis runs over, the one named last changes fastest.
Arguments:
- q_raw: bfloat16 [4096, 2560], P('seq', 'head'), may hold values from -48 to 48
- k_raw: bfloat16 [4096, 2560], P('seq', 'head'), may hold values from -48 to 48
- values: bfloat16 [4096, 2560], P('seq', 'head'), may hold values from -24 to 24
- q_tangent: bfloat16 [4096, 2560], P('seq', 'head'), may hold values from -6 to 6
- k_tangent: bfloat16 [4096, 2560], P('seq', 'head'), may hold values from -6 to 6
- v_tangent: bfloat16 [4096, 2560], P('seq', 'head'), may hold values from -24 to 24
- out_cotangent: bfloat16 [4096, 2560], P('seq', 'head'), may hold values from -24 to 24
- q_gain: float32 [2560], P('head'), may hold values from 0.1 to 1.9
- k_gain: float32 [2560], P('head'), may hold values from 0.1 to 1.9
- tile_at_slot: int32 [32], replicated, may hold values from 0 to 31, as said below
- key_tiles: int32 [32, 6], replicated, may hold values from 0 to 31, as said below
Outputs:
- output: bfloat16 [4096, 2560], P('seq', 'head')
- output_tangent: bfloat16 [4096, 2560], P('seq', 'head')
- grad_q: bfloat16 [4096, 2560], P('seq', 'head')
- grad_k: bfloat16 [4096, 2560], P('seq', 'head')
- grad_v: bfloat16 [4096, 2560], P('seq', 'head')
Inputs may be any that keep to these rules, and one draw needn't show every extreme that they name: `tile_at_slot`: a permutation of the tiles. `key_tiles`: row g lists 6 distinct tiles in this order: g itself, 3 other tiles whose slots lie on the same index of seq as g's slot, then 2 tiles whose slots lie on the index just before or just after it. The query tiles of one index of seq name at most 2 distinct tiles of each neighbouring index, and exactly 2 of every neighbour that exists.
All inputs are finite; a program needn't handle non-finite values.
Results may differ from a plain program's by a relative error of at most 0.014.
The roundings to bfloat16 on the way count: a program that leaves them out, or rounds other values in their place, can miss the bound.
Values may be sent and summed in bfloat16 or wider, within the bound.
A program may use at most 192 MiB of HBM per device.

v0:
```python
import jax
import jax.numpy as jnp
from jax import lax
from jax.sharding import PartitionSpec as P

HEADS = 20
HEAD_DIM = 128
TILE = 128
NEED = 2
KSEL = 6


NORM_EPS = 1e-06


def shifted(value, axis, steps):
    count = lax.axis_size(axis)
    leading, last = (max(0, -steps), min(count, count - steps))
    return lax.ppermute(value, axis, [(source, source + steps) for source in range(leading, last)])


def product(form, left, right):
    return jnp.einsum(form, left, right, preferred_element_type=jnp.float32)


def attend(
    queries, query_tangent, cotangent, keys, key_values, key_tangent, value_tangent, score_scale
):
    scores = product("gqhe,gkhe->ghqk", queries, keys) * score_scale
    highest = jnp.max(scores, axis=-1, keepdims=True)
    weights = jnp.exp(scores - highest)
    probs = weights / jnp.sum(weights, axis=-1, keepdims=True)
    probs_half = probs.astype(jnp.bfloat16)
    output = product("ghqk,gkhe->gqhe", probs_half, key_values).astype(jnp.bfloat16)
    score_tangent = (
        product("gqhe,gkhe->ghqk", query_tangent, keys)
        + product("gqhe,gkhe->ghqk", queries, key_tangent)
    ) * score_scale
    centre = jnp.sum(probs * score_tangent, axis=-1, keepdims=True)
    prob_tangent = (probs * (score_tangent - centre)).astype(jnp.bfloat16)
    output_tangent = (
        product("ghqk,gkhe->gqhe", prob_tangent, key_values)
        + product("ghqk,gkhe->gqhe", probs_half, value_tangent)
    ).astype(jnp.bfloat16)
    prob_grad = product("gqhe,gkhe->ghqk", cotangent, key_values)
    delta = product("gqhe,gqhe->ghq", cotangent, output)
    score_grad = (probs * (prob_grad - delta[..., None])).astype(jnp.bfloat16)
    query_grad = product("ghqk,gkhe->gqhe", score_grad, keys) * score_scale
    key_grad = product("ghqk,gqhe->gkhe", score_grad, queries) * score_scale
    value_grad = product("ghqk,gqhe->gkhe", probs_half, cotangent)
    return (output, output_tangent, query_grad, key_grad, value_grad)


def per_device(
    q_raw,
    k_raw,
    values,
    q_tangent,
    k_tangent,
    v_tangent,
    out_cotangent,
    q_gain,
    k_gain,
    tile_at_slot,
    key_tiles,
):
    row_count, lane_width = q_raw.shape
    head_count = lane_width // HEAD_DIM
    tiles_here = row_count // TILE
    seq_devices = lax.axis_size("seq")
    position = lax.axis_index("seq")
    full_width = HEADS * HEAD_DIM
    score_scale = HEAD_DIM ** (-0.5)
    q_float = q_raw.astype(jnp.float32)
    k_float = k_raw.astype(jnp.float32)
    q_moving = q_tangent.astype(jnp.float32)
    k_moving = k_tangent.astype(jnp.float32)
    totals = lax.psum(
        (
            jnp.sum(q_float * q_float, axis=1),
            jnp.sum(q_float * q_moving, axis=1),
            jnp.sum(k_float * k_float, axis=1),
            jnp.sum(k_float * k_moving, axis=1),
        ),
        "head",
    )
    q_inverse = lax.rsqrt(totals[0][:, None] / full_width + NORM_EPS)
    k_inverse = lax.rsqrt(totals[2][:, None] / full_width + NORM_EPS)
    q_drift = totals[1][:, None] / full_width
    k_drift = totals[3][:, None] / full_width
    q_normed = (q_float * q_inverse * q_gain).astype(jnp.bfloat16)
    k_normed = (k_float * k_inverse * k_gain).astype(jnp.bfloat16)
    q_normed_tangent = (
        q_gain * (q_moving * q_inverse - q_float * q_inverse**3 * q_drift)
    ).astype(jnp.bfloat16)
    k_normed_tangent = (
        k_gain * (k_moving * k_inverse - k_float * k_inverse**3 * k_drift)
    ).astype(jnp.bfloat16)
    key_stack = jnp.stack([k_normed, values, k_normed_tangent, v_tangent], 0).reshape(
        4, tiles_here, TILE, lane_width
    )
    slot_of = jnp.argsort(tile_at_slot)
    key_slots = slot_of[key_tiles[tile_at_slot]]
    wanted_here = lax.dynamic_slice_in_dim(key_slots, position * tiles_here, tiles_here, 0)
    key_device = wanted_here // tiles_here
    key_offset = wanted_here % tiles_here
    tile_range = jnp.arange(tiles_here, dtype=jnp.int32)

    def named_tiles(listing, device):
        return jnp.any(
            listing.reshape(-1)[:, None] == device * tiles_here + tile_range[None, :], axis=0
        )

    send_orders = []
    pieces = [key_stack]
    for offset in (1, -1):
        receiver = jnp.clip(position + offset, 0, seq_devices - 1)
        listing = lax.dynamic_slice_in_dim(key_slots, receiver * tiles_here, tiles_here, 0)
        named_flags = named_tiles(listing, position).astype(jnp.int32)
        packet_order = jnp.argsort(1 - named_flags)[:NEED]
        send_orders.append(packet_order)
        packet = jnp.take(key_stack, packet_order, axis=1)
        pieces.append(shifted(packet, "seq", offset))
    below_rank = jnp.cumsum(named_tiles(wanted_here, position - 1).astype(jnp.int32)) - 1
    above_rank = jnp.cumsum(named_tiles(wanted_here, position + 1).astype(jnp.int32)) - 1
    slot_index = jnp.where(
        key_device == position,
        key_offset,
        jnp.where(
            key_device == position - 1,
            tiles_here + below_rank[key_offset],
            tiles_here + NEED + above_rank[key_offset],
        ),
    )
    buffer = jnp.concatenate(pieces, 1)
    buffer_tiles = buffer.shape[1]
    group_size = 4
    group_count = tiles_here // group_size

    def grouped(array):
        return array.reshape(group_count, group_size, TILE, head_count, HEAD_DIM)

    def group_step(grad_sums, group_item):
        queries, query_tangent, cotangent, indices = group_item
        picked = jnp.take(buffer, indices.reshape(-1), axis=1).reshape(
            4, group_size, KSEL * TILE, head_count, HEAD_DIM
        )
        output, output_tangent, query_grad, key_grad, value_grad = attend(
            queries,
            query_tangent,
            cotangent,
            picked[0],
            picked[1],
            picked[2],
            picked[3],
            score_scale,
        )
        both_grads = jnp.stack(
            [
                key_grad.reshape(group_size * KSEL, TILE, lane_width),
                value_grad.reshape(group_size * KSEL, TILE, lane_width),
            ],
            0,
        )
        grad_sums = grad_sums.at[:, indices.reshape(-1)].add(both_grads)
        return (grad_sums, (output, output_tangent, query_grad))

    start_sums = jnp.zeros((2, buffer_tiles, TILE, lane_width), jnp.float32)
    grad_sums, (output, output_tangent, query_grad) = lax.scan(
        group_step,
        start_sums,
        (
            grouped(q_normed),
            grouped(q_normed_tangent),
            grouped(out_cotangent),
            slot_index.reshape(group_count, group_size, KSEL),
        ),
    )
    partial_sums = grad_sums.astype(jnp.bfloat16)
    collected = partial_sums[:, :tiles_here].astype(jnp.float32)
    for offset, first, packet_order in (
        (-1, tiles_here, send_orders[0]),
        (1, tiles_here + NEED, send_orders[1]),
    ):
        returned = shifted(partial_sums[:, first : first + NEED], "seq", offset)
        collected = collected.at[:, packet_order].add(returned.astype(jnp.float32))
    key_total = collected[0].reshape(row_count, lane_width)
    value_total = collected[1].reshape(row_count, lane_width)
    q_weighted = q_gain * query_grad.reshape(row_count, lane_width)
    k_weighted = k_gain * key_total
    back_totals = lax.psum(
        (jnp.sum(q_float * q_weighted, axis=1), jnp.sum(k_float * k_weighted, axis=1)), "head"
    )
    grad_q = (
        q_inverse * q_weighted - q_float * q_inverse**3 * (back_totals[0][:, None] / full_width)
    ).astype(jnp.bfloat16)
    grad_k = (
        k_inverse * k_weighted - k_float * k_inverse**3 * (back_totals[1][:, None] / full_width)
    ).astype(jnp.bfloat16)
    return (
        output.reshape(row_count, lane_width),
        output_tangent.reshape(row_count, lane_width),
        grad_q,
        grad_k,
        value_total.astype(jnp.bfloat16),
    )


def solution(mesh):
    in_specs = (
        P("seq", "head"),
        P("seq", "head"),
        P("seq", "head"),
        P("seq", "head"),
        P("seq", "head"),
        P("seq", "head"),
        P("seq", "head"),
        P("head"),
        P("head"),
        P(),
        P(),
    )
    out_specs = (
        P("seq", "head"),
        P("seq", "head"),
        P("seq", "head"),
        P("seq", "head"),
        P("seq", "head"),
    )
    return jax.shard_map(
        per_device, mesh=mesh, in_specs=in_specs, out_specs=out_specs, check_vma=False
    )
```

profile of v0, /device:TPU:25, one launch (start us, length us, event | category | flops | bytes accessed | tf_op | source)
XLA Modules:
  0.0 399.0 jit_solution(13907506691538227989)
XLA Ops:
  2.8 2.3 sort.48
  9.5 5.7 %all-reduce.1 = (f32[512]{0:T(512)S(1)}, f32[512]{0:T(512)S(1)}, f32[512]{0:T(512)S(1)}) all-reduce(f32[512]{0:T(512)S(1)} %get-tuple-element.55, f32[512]{0:T(512)S(1)} %get-tuple-element.54, f32[512]{0:T(512)S(1)} %fusion.40), channel_id=1, replica_groups=mesh['seq'=8,'head'=4] {'head'}, use_global_device_ids=true, to_apply=%region_8.0 | all-reduce | flops 1536 | bytes 12288 | tf_op jit(solution)/shard_map/psum | solution.py:78
  21.0 2.6 select_bitcast_fusion.1
  23.6 3.1 collective-permute-start
  28.5 2.6 fusion.45
  31.1 3.1 collective-permute-start.1
  37.8 2.1 squeeze.33
  39.9 2.4 copy.85
  42.3 2.3 squeeze.38
  44.6 2.2 copy.87
  46.7 2.2 copy.75
  49.0 6.0 %collective-permute-done = bf16[4,2,128,640]{3,2,0,1:T(8,128)(2,1)} collective-permute-done((bf16[4,2,128,640]{3,2,0,1:T(8,128)(2,1)}, bf16[4,2,128,640]{3,2,0,1:T(8,128)(2,1)}, u32[]{:S(2)}, u32[]{:S(2)}) %collective-permute-start) | collective-permute-done | bytes 1310752 | tf_op jit(solution)/shard_map/ppermute | solution.py:19
  55.0 30.5 %collective-permute-done.1 = bf16[4,2,128,640]{3,2,1,0:T(8,128)(2,1)} collective-permute-done((bf16[4,2,128,640]{3,2,1,0:T(8,128)(2,1)}, bf16[4,2,128,640]{3,2,1,0:T(8,128)(2,1)}, u32[]{:S(2)}, u32[]{:S(2)}) %collective-permute-start.1) | collective-permute-done | bytes 1310752 | tf_op jit(solution)/shard_map/ppermute | solution.py:19
  85.5 5.1 %pad_maximum_fusion = bf16[4,8,128,640]{3,2,1,0:T(8,128)(2,1)} fusion(bf16[4,2,128,640]{3,2,1,0:T(8,128)(2,1)} %collective-permute-done.1, bf16[1,4,128,640]{3,2,1,0:T(8,128)(2,1)} %bitcast.117, bf16[1,4,128,640]{3,2,1,0:T(8,128)(2,1)S(1)} %bitcast.113, bf16[1,4,128,640]{3,2,1,0:T(8,128)(2,1)} %bitcast.119, bf16[1,4,128,640]{3,2,1,0:T(8,128)(2,1)S(1)} %bitcast.111, ...), kind=kLoop, calls=%fused_computation.22 | loop fusion | flops 31457280 | bytes 10485760 | tf_op jit(solution)/shard_map/concatenate | solution.py:135
  90.6 9.8 %gather_fusion.4 = bf16[24,4,128,640]{3,2,1,0:T(8,128)(2,1)} fusion(bf16[4,8,128,640]{3,2,1,0:T(8,128)(2,1)} %pad_maximum_fusion, s32[1024]{0:T(1024)S(1)} %pad_clamp_fusion), kind=kCustom, calls=%fused_computation.6 | custom fusion | bytes 31457376 | tf_op jit(solution)/shard_map/while/body/eval_jaxpr/jit(_take)/gather | solution.py:145
  100.4 8.3 %select_bitcast_fusion = bf16[4,24,128,640]{3,2,0,1:T(8,128)(2,1)S(1)} fusion(bf16[24,4,128,640]{3,2,1,0:T(8,128)(2,1)} %gather_fusion.4, pred[24]{0:T(512)(128)(4,1)S(1)} %compare_and_fusion.2), kind=kLoop, calls=%fused_computation.12 | loop fusion | flops 7864320 | bytes 31457304 | tf_op jit(solution)/shard_map/while/body/eval_jaxpr/jit(_take)/select_n | solution.py:145
  108.7 5.8 %fusion.80 = (bf16[1,24,128,640]{3,2,0,1:T(8,128)(2,1)}, bf16[1,24,128,640]{3,2,0,1:T(8,128)(2,1)}, bf16[1,24,128,640]{3,2,0,1:T(8,128)(2,1)}, bf16[1,24,128,640]{3,2,0,1:T(8,128)(2,1)}) fusion(bf16[4,24,128,640]{3,2,0,1:T(8,128)(2,1)S(1)} %select_bitcast_fusion), kind=kLoop, calls=%fused_computation.152 | loop fusion | bytes 31457280 | tf_op jit(solution)/shard_map/while/body/eval_jaxpr/slice | solution.py:155
  114.5 9.5 %reshape.338 = bf16[4,768,5,128]{3,2,1,0:T(8,128)(2,1)} reshape(bf16[1,24,128,640]{3,2,0,1:T(8,128)(2,1)} %get-tuple-element.74) | data formatting | bytes 7864320 | tf_op jit(solution)/shard_map/while/body/eval_jaxpr/squeeze | solution.py:152
  124.1 8.1 %copy.89 = bf16[4,768,5,128]{1,3,2,0:T(8,128)(2,1)} copy(bf16[4,768,5,128]{3,2,1,0:T(8,128)(2,1)} %reshape.338) | data formatting | bytes 7864320 | tf_op jit(solution)/shard_map/while/body/eval_jaxpr/squeeze | solution.py:152
  132.1 3.3 fusion.55
  135.5 4.6 %fusion.82 = (f32[4,5,128]{2,1,0:T(8,128)S(1)}, f32[4,5,128,768]{3,2,1,0:T(8,128)}) fusion(f32[4,5,128,768]{3,2,1,0:T(8,128)S(1)} %fusion.55), kind=kOutput, calls=%fused_computation.154 | output fusion | flops 7865087 | bytes 15738880 | tf_op jit(solution)/shard_map/while/body/eval_jaxpr/sub | solution.py:31
  140.9 13.3 %convolution_bitcast_fusion = f32[4,768,5,128]{3,1,2,0:T(8,128)} fusion(bf16[4,128,5,128]{3,1,2,0:T(8,128)(2,1)S(1)} %copy-done.21, f32[4,5,128]{2,1,0:T(8,128)S(1)} %get-tuple-element.88, f32[4,5,128,768]{3,2,1,0:T(8,128)} %copy-done.1), kind=kOutput, calls=%fused_computation.31 | convolution fusion | flops 513150208 | bytes 16394240 | tf_op jit(solution)/shard_map/while/body/eval_jaxpr/ghqk,gqhe->gkhe/dot_general | solution.py:23
  154.2 10.5 %copy.95 = f32[4,768,5,128]{1,0,3,2:T(4,128)} copy(f32[4,768,5,128]{3,1,2,0:T(8,128)} %convolution_bitcast_fusion) | data formatting | bytes 15728640 | tf_op jit(solution)/shard_map/while/body/eval_jaxpr/ghqk,gqhe->gkhe/transpose | solution.py:23
  164.7 10.1 %reshape.229 = f32[1,24,128,640]{2,1,3,0:T(8,128)} reshape(f32[4,768,5,128]{1,0,3,2:T(4,128)} %copy.95) | data formatting | bytes 15728640 | tf_op jit(solution)/shard_map/while/body/eval_jaxpr/stack;while/body/eval_jaxpr/reshape | solution.py:158
  174.8 9.7 %reshape.337 = bf16[4,768,5,128]{3,2,1,0:T(8,128)(2,1)} reshape(bf16[1,24,128,640]{3,2,0,1:T(8,128)(2,1)} %get-tuple-element.75) | data formatting | bytes 7864320 | tf_op jit(solution)/shard_map/while/body/eval_jaxpr/squeeze | solution.py:153
  184.6 14.9 %bitcast_convert_fusion = (f32[4,5,128,128]{2,3,1,0:T(8,128)}, bf16[4,5,128,128]{3,2,1,0:T(8,128)(2,1)}) fusion(f32[4,5,128]{2,1,0:T(8,128)S(1)} %get-tuple-element.88, f32[4,5,128,768]{3,2,1,0:T(8,128)} %copy-done.1, bf16[4,768,5,128]{3,2,1,0:T(8,128)(2,1)} %reshape.337), kind=kOutput, calls=%fused_computation.87 | convolution fusion | flops 513805568 | bytes 13772800 | tf_op jit(solution)/shard_map/while/body/eval_jaxpr/ghqk,gkhe->gqhe/dot_general | solution.py:23
  199.4 2.5 multiply_reduce_fusion.2
  201.9 8.4 %fusion.1 = bf16[4,5,128,768]{3,2,1,0:T(8,128)(2,1)S(1)} fusion(f32[4,5,128]{2,1,0:T(8,128)S(1)} %copy.109, bf16[4,128,5,128]{3,1,2,0:T(8,128)(2,1)S(1)} %copy-done.21, bf16[4,768,5,128]{3,2,1,0:T(8,128)(2,1)} %reshape.337, f32[4,5,128,768]{3,2,1,0:T(8,128)} %get-tuple-element.89, f32[4,5,128]{2,1,0:T(8,128)S(1)} %get-tuple-element.88), kind=kOutput, calls=%fused_computation.14 | convolution fusion | flops 511180800 | bytes 16404480 | tf_op jit(solution)/shard_map/while/body/eval_jaxpr/gqhe,gkhe->ghqk/dot_general | solution.py:23
  210.3 1.9 copy-done.2
  213.4 8.1 %copy.92 = f32[4,768,5,128]{1,0,3,2:T(4,128)} copy(f32[4,768,5,128]{1,3,2,0:T(8,128)S(1)} %multiply_bitcast_fusion) | data formatting | bytes 15728640 | tf_op jit(solution)/shard_map/while/body/eval_jaxpr/mul | solution.py:49
  221.5 10.1 %reshape.228 = f32[1,24,128,640]{2,1,3,0:T(8,128)} reshape(f32[4,768,5,128]{1,0,3,2:T(4,128)} %copy.92) | data formatting | bytes 15728640 | tf_op jit(solution)/shard_map/while/body/eval_jaxpr/stack;while/body/eval_jaxpr/reshape | solution.py:158
  231.6 12.0 %maximum_bitcast_fusion = f32[24,2,128,640]{2,0,3,1:T(8,128)} fusion(f32[1,24,128,640]{2,1,3,0:T(8,128)} %reshape.229, f32[1,24,128,640]{2,1,3,0:T(8,128)} %reshape.228), kind=kLoop, calls=%fused_computation.11 | loop fusion | flops 3932160 | bytes 31457280 | tf_op jit(solution)/shard_map/while/body/eval_jaxpr/stack | solution.py:158
  243.6 15.7 %copy.96 = f32[24,2,128,640]{3,2,1,0:T(8,128)} copy(f32[24,2,128,640]{2,0,3,1:T(8,128)} %maximum_bitcast_fusion) | data formatting | bytes 31457280 | tf_op jit(solution)/shard_map/while/body/eval_jaxpr/stack | solution.py:158
  259.3 2.9 broadcast_in_dim.77
  262.2 31.3 %scatter_fusion = f32[2,8,128,640]{3,2,1,0:T(8,128)} fusion(f32[2,8,128,640]{3,2,1,0:T(8,128)} %broadcast_in_dim.77, s32[24]{0:T(128)S(1)} %fusion.59, f32[24,2,128,640]{3,2,1,0:T(8,128)} %copy.96), kind=kCustom, calls=%fused_computation.7 | custom fusion | flops 3932160 | bytes 47186016 | tf_op jit(solution)/shard_map/while/body/eval_jaxpr/scatter-add | solution.py:165
  293.5 3.0 convert_element_type.126
  297.6 2.2 collective-permute-start.2
  301.0 4.4 %collective-permute-start.3 = (bf16[2,2,128,640]{3,2,1,0:T(8,128)(2,1)}, bf16[2,2,128,640]{3,2,1,0:T(8,128)(2,1)}, u32[]{:S(2)}, u32[]{:S(2)}) collective-permute-start(bf16[2,2,128,640]{3,2,1,0:T(8,128)(2,1)} %get-tuple-element.76), channel_id=1, source_target_pairs={{0,4},{4,8},{8,12},{12,16},{16,20},{20,24},{24,28},{1,5},{5,9},{9,... | collective-permute-start | bytes 1966088 | tf_op jit(solution)/shard_map/ppermute | solution.py:19
  307.7 9.6 %reshape.334 = bf16[4,768,5,128]{3,2,1,0:T(8,128)(2,1)} reshape(bf16[1,24,128,640]{3,2,0,1:T(8,128)(2,1)} %get-tuple-element.73) | data formatting | bytes 7864320 | tf_op jit(solution)/shard_map/while/body/eval_jaxpr/squeeze | solution.py:154
  317.2 9.6 %reshape.335 = bf16[4,768,5,128]{3,2,1,0:T(8,128)(2,1)} reshape(bf16[1,24,128,640]{3,2,0,1:T(8,128)(2,1)} %get-tuple-element.72) | data formatting | bytes 7864320 | tf_op jit(solution)/shard_map/while/body/eval_jaxpr/squeeze | solution.py:155
  334.7 2.4 scatter_fusion.1
  337.1 2.4 scatter_fusion.2
  341.2 6.4 %all-reduce = (f32[512]{0:T(512)S(1)}, f32[512]{0:T(512)S(1)}, f32[512]{0:T(512)S(1)}) all-reduce(f32[512]{0:T(512)S(1)} %get-tuple-element.53, f32[512]{0:T(512)S(1)} %get-tuple-element.52, f32[512]{0:T(512)S(1)} %fusion.39), channel_id=1, replica_groups=mesh['seq'=8,'head'=4] {'head'}, use_global_device_ids=true, to_apply=%region_18.20 | all-reduce | flops 1536 | bytes 12288 | tf_op jit(solution)/shard_map/psum | solution.py:78
  347.7 2.7 fusion.34
  353.4 3.4 fusion.49
  356.9 8.4 %multiply_reduce_fusion = (f32[4,5,128]{2,1,0:T(8,128)S(1)}, f32[4,5,128,768]{3,2,1,0:T(8,128)}) fusion(f32[4,5,128,768]{3,2,1,0:T(8,128)} %get-tuple-element.89, f32[4,5,128]{2,1,0:T(8,128)S(1)} %get-tuple-element.88, f32[4,5,128,768]{3,2,1,0:T(8,128)S(1)} %fusion.49, bf16[4,768,5,128]{3,2,1,0:T(8,128)(2,1)} %reshape.334, ...), kind=kOutput, calls=%fused_computation.17 | convolution fusion | flops 513144320 | bytes 28200960 | tf_op jit(solution)/shard_map/while/body/eval_jaxpr/gqhe,gkhe->ghqk/dot_general | solution.py:23
  365.2 17.1 %fusion.5 = f32[4,5,128,128]{3,2,1,0:T(8,128)} fusion(f32[4,5,128,768]{3,2,1,0:T(8,128)} %get-tuple-element.93, f32[4,5,128]{2,1,0:T(8,128)S(1)} %get-tuple-element.92, bf16[4,768,5,128]{3,2,1,0:T(8,128)(2,1)} %reshape.337, f32[4,5,128]{2,1,0:T(8,128)S(1)} %get-tuple-element.88, f32[4,5,128,768]{3,2,1,0:T(8,128)} %copy-done.1), kind=kOutput, calls=%fused_computation.23 | convolution fusion | flops 517082368 | bytes 20992000 | tf_op jit(solution)/shard_map/while/body/eval_jaxpr/ghqk,gkhe->gqhe/dot_general | solution.py:23
  382.3 13.8 %fusion.46 = bf16[4,128,5,128]{1,3,2,0:T(8,128)(2,1)S(1)} fusion(f32[4,5,128,128]{3,2,1,0:T(8,128)} %fusion.5, bf16[4,768,5,128]{3,2,1,0:T(8,128)(2,1)} %reshape.335, f32[4,5,128]{2,1,0:T(8,128)S(1)} %get-tuple-element.88, f32[4,5,128,768]{3,2,1,0:T(8,128)} %copy-done.1), kind=kOutput, calls=%fused_computation.84 | convolution fusion | flops 513805568 | bytes 13772800 | tf_op jit(solution)/shard_map/while/body/eval_jaxpr/ghqk,gkhe->gqhe/dot_general | solution.py:23
  (156 shorter events, 39.4 us)
Async XLA Ops:
  5.1 3.6 copy-start.20
  5.1 4.1 %copy-start.7 = (bf16[512,640]{1,0:T(8,128)(2,1)S(1)}, bf16[512,640]{1,0:T(8,128)(2,1)}, u32[]{:S(2)}) copy-start(bf16[512,640]{1,0:T(8,128)(2,1)} %param.14) | copy-start | bytes 1966084
  5.1 4.1 %copy-start.19 = (bf16[512,640]{1,0:T(8,128)(2,1)S(1)}, bf16[512,640]{1,0:T(8,128)(2,1)}, u32[]{:S(2)}) copy-start(bf16[512,640]{1,0:T(8,128)(2,1)} %param.17) | copy-start | bytes 1966084
  5.1 10.8 %copy-start.23 = (f32[640]{0:T(1024)S(1)}, f32[640]{0:T(1024)}, u32[]{:S(2)}) copy-start(f32[640]{0:T(1024)} %param.21) | copy-start | bytes 7684
  8.7 7.8 %copy-start.35 = (s32[2]{0:T(128)}, s32[2]{0:T(128)S(1)}, u32[]{:S(2)}) copy-start(s32[2]{0:T(128)S(1)} %get-tuple-element.97) | copy-start | bytes 28
  8.7 18.0 %copy-start.33 = (s32[2]{0:T(128)}, s32[2]{0:T(128)S(1)}, u32[]{:S(2)}) copy-start(s32[2]{0:T(128)S(1)} %get-tuple-element.71) | copy-start | bytes 28
  15.9 0.6 copy-start.30
  15.9 3.3 copy-start.28
  15.9 20.9 %copy-start.26 = (f32[512]{0:T(512)}, f32[512]{0:T(512)S(1)}, u32[]{:S(2)}) copy-start(f32[512]{0:T(512)S(1)} %get-tuple-element.85) | copy-start | bytes 6148
  16.4 0.8 copy-start.12
  16.4 1.0 copy-start.14
  23.6 31.4 %collective-permute-start = (bf16[4,2,128,640]{3,2,0,1:T(8,128)(2,1)}, bf16[4,2,128,640]{3,2,0,1:T(8,128)(2,1)}, u32[]{:S(2)}, u32[]{:S(2)}) collective-permute-start(bf16[4,2,128,640]{3,2,0,1:T(8,128)(2,1)} %select_bitcast_fusion.1), channel_id=1, source_target_pairs={{0,4},{4,8},{8,12},{12,16},{16,20},{20,24},{24,28},{1,5},{5,9},{9,... | collective-permute-start | bytes 3932168 | tf_op jit(solution)/shard_map/ppermute | solution.py:19
  28.5 8.2 %copy-start.25 = (f32[640]{0:T(1024)S(1)}, f32[640]{0:T(1024)}, u32[]{:S(2)}) copy-start(f32[640]{0:T(1024)} %param.20) | copy-start | bytes 7684
  31.1 54.3 %collective-permute-start.1 = (bf16[4,2,128,640]{3,2,1,0:T(8,128)(2,1)}, bf16[4,2,128,640]{3,2,1,0:T(8,128)(2,1)}, u32[]{:S(2)}, u32[]{:S(2)}) collective-permute-start(bf16[4,2,128,640]{3,2,1,0:T(8,128)(2,1)} %fusion.45), channel_id=1, source_target_pairs={{4,0},{8,4},{12,8},{16,12},{20,16},{24,20},{28,24},{5,1},{9,5},{13... | collective-permute-start | bytes 3932168 | tf_op jit(solution)/shard_map/ppermute | solution.py:19
  36.7 48.7 %copy-start.13 = (bf16[512,640]{1,0:T(8,128)(2,1)S(1)}, bf16[512,640]{1,0:T(8,128)(2,1)}, u32[]{:S(2)}) copy-start(bf16[512,640]{1,0:T(8,128)(2,1)} %copy-done.12) | copy-start | bytes 1966084
  36.8 48.7 %copy-start.15 = (bf16[512,640]{1,0:T(8,128)(2,1)S(1)}, bf16[512,640]{1,0:T(8,128)(2,1)}, u32[]{:S(2)}) copy-start(bf16[512,640]{1,0:T(8,128)(2,1)} %copy-done.14) | copy-start | bytes 1966084
  39.9 170.4 %copy-start.10 = (bf16[4,128,5,128]{1,0,3,2:T(4,128)(2,1)}, bf16[4,128,5,128]{1,0,3,2:T(4,128)(2,1)S(1)}, u32[]{:S(2)}) copy-start(bf16[4,128,5,128]{1,0,3,2:T(4,128)(2,1)S(1)} %squeeze.33) | copy-start | bytes 1966084
  135.5 5.4 %copy-start.1 = (f32[4,5,128,768]{3,2,1,0:T(8,128)}, f32[4,5,128,768]{3,2,1,0:T(8,128)S(1)}, u32[]{:S(2)}) copy-start(f32[4,5,128,768]{3,2,1,0:T(8,128)S(1)} %fusion.55) | copy-start | bytes 23592964
  135.5 5.4 %copy-start.21 = (bf16[4,128,5,128]{3,1,2,0:T(8,128)(2,1)S(1)}, bf16[4,128,5,128]{3,1,2,0:T(8,128)(2,1)}, u32[]{:S(2)}) copy-start(bf16[4,128,5,128]{3,1,2,0:T(8,128)(2,1)} %copy.87) | copy-start | bytes 1966084
  184.6 14.9 %copy-start.18 = (bf16[4,128,5,128]{1,0,3,2:T(4,128)(2,1)S(1)}, bf16[4,128,5,128]{1,0,3,2:T(4,128)(2,1)}, u32[]{:S(2)}) copy-start(bf16[4,128,5,128]{1,0,3,2:T(4,128)(2,1)} %squeeze.38) | copy-start | bytes 1966084
  210.3 1.9 copy-start.2
  293.5 6.3 %copy-start = (bf16[4,768,5,128]{1,3,2,0:T(8,128)(2,1)S(1)}, bf16[4,768,5,128]{1,3,2,0:T(8,128)(2,1)}, u32[]{:S(2)}) copy-start(bf16[4,768,5,128]{1,3,2,0:T(8,128)(2,1)} %copy.89) | copy-start | bytes 11796484
  293.5 6.3 %copy-start.3 = (bf16[4,5,128,768]{3,2,1,0:T(8,128)(2,1)S(1)}, bf16[4,5,128,768]{3,2,1,0:T(8,128)(2,1)}, u32[]{:S(2)}) copy-start(bf16[4,5,128,768]{3,2,1,0:T(8,128)(2,1)} %copy-done.2) | copy-start | bytes 11796484
  296.4 4.6 %copy-start.9 = (bf16[2,8,128,640]{3,2,1,0:T(8,128)(2,1)}, bf16[2,8,128,640]{3,2,1,0:T(8,128)(2,1)S(1)}, u32[]{:S(2)}) copy-start(bf16[2,8,128,640]{3,2,1,0:T(8,128)(2,1)S(1)} %convert_element_type.126) | copy-start | bytes 7864324
  297.6 9.7 %copy-start.16 = (bf16[512,640]{0,1:T(8,128)(2,1)S(1)}, bf16[512,640]{0,1:T(8,128)(2,1)}, u32[]{:S(2)}) copy-start(bf16[512,640]{0,1:T(8,128)(2,1)} %copy.75) | copy-start | bytes 1966084
  297.6 32.4 %collective-permute-start.2 = (bf16[2,2,128,640]{3,2,1,0:T(8,128)(2,1)}, bf16[2,2,128,640]{3,2,1,0:T(8,128)(2,1)}, u32[]{:S(2)}, u32[]{:S(2)}) collective-permute-start(bf16[2,2,128,640]{3,2,1,0:T(8,128)(2,1)} %get-tuple-element.77), channel_id=1, source_target_pairs={{4,0},{8,4},{12,8},{16,12},{20,16},{24,20},{28,24},{5,1},{9,5},{13... | collective-permute-start | bytes 1966088 | tf_op jit(solution)/shard_map/ppermute | solution.py:19
  301.0 31.4 %collective-permute-start.3 = (bf16[2,2,128,640]{3,2,1,0:T(8,128)(2,1)}, bf16[2,2,128,640]{3,2,1,0:T(8,128)(2,1)}, u32[]{:S(2)}, u32[]{:S(2)}) collective-permute-start(bf16[2,2,128,640]{3,2,1,0:T(8,128)(2,1)} %get-tuple-element.76), channel_id=1, source_target_pairs={{0,4},{4,8},{8,12},{12,16},{16,20},{20,24},{24,28},{1,5},{5,9},{9,... | collective-permute-start | bytes 1966088 | tf_op jit(solution)/shard_map/ppermute | solution.py:19
  306.2 1.1 copy-start.4
  317.2 9.6 %copy-start.22 = (bf16[4,5,128,128]{3,2,1,0:T(8,128)(2,1)S(1)}, bf16[4,5,128,128]{3,2,1,0:T(8,128)(2,1)}, u32[]{:S(2)}) copy-start(bf16[4,5,128,128]{3,2,1,0:T(8,128)(2,1)} %get-tuple-element.91) | copy-start | bytes 1966084
  331.2 3.5 copy-start.36
  332.4 4.7 %copy-start.34 = (s32[2]{0:T(128)S(1)}, s32[2]{0:T(128)}, u32[]{:S(2)}) copy-start(s32[2]{0:T(128)} %copy-done.33) | copy-start | bytes 28
  337.1 3.8 copy-start.24
  339.5 1.4 copy-start.8
  339.5 8.1 %copy-start.29 = (f32[512]{0:T(512)S(1)}, f32[512]{0:T(512)}, u32[]{:S(2)}) copy-start(f32[512]{0:T(512)} %copy-done.28) | copy-start | bytes 6148
  339.5 8.1 %copy-start.31 = (f32[512]{0:T(512)S(1)}, f32[512]{0:T(512)}, u32[]{:S(2)}) copy-start(f32[512]{0:T(512)} %copy-done.30) | copy-start | bytes 6148
  339.5 10.8 %copy-start.27 = (f32[512]{0:T(512)S(1)}, f32[512]{0:T(512)}, u32[]{:S(2)}) copy-start(f32[512]{0:T(512)} %copy-done.26) | copy-start | bytes 6148
  339.6 10.8 %copy-start.32 = (f32[512]{0:T(512)S(1)}, f32[512]{0:T(512)}, u32[]{:S(2)}) copy-start(f32[512]{0:T(512)} %get-tuple-element.84) | copy-start | bytes 6148
  339.7 1.3 copy-start.6
  340.9 9.4 %copy-start.5 = (f32[4,128,5,128]{1,0,3,2:T(4,128)S(1)}, f32[4,128,5,128]{1,0,3,2:T(4,128)}, u32[]{:S(2)}) copy-start(f32[4,128,5,128]{1,0,3,2:T(4,128)} %copy-done.4) | copy-start | bytes 3932164
  340.9 9.5 %copy-start.17 = (bf16[512,640]{0,1:T(8,128)(2,1)S(1)}, bf16[512,640]{0,1:T(8,128)(2,1)}, u32[]{:S(2)}) copy-start(bf16[512,640]{0,1:T(8,128)(2,1)} %copy.75) | copy-start | bytes 1966084
  353.4 3.4 copy-start.11
where the time goes:
time: 406 us; the launch traced here: 399 us
  local copies, waits for them, and re-layouts  156 us (38%)
  other arithmetic  94.9 us (23%)
  matrix products  84.8 us (21%)
  waiting for transfers between devices  36.5 us (9%)
  starting transfers between devices  12.7 us (3%)
  blocking collectives  12.2 us (3%)
    dot_general x10, matrix products, product(): return jnp.einsum(form, left, right, preferred_element_type=jnp.float32)  84.8 us
    ppermute x4, waiting for transfers between devices, shifted(): lax.ppermute(value, axis, [(source, source + steps) for source in range(l...  36.5 us
    scatter-add x1, other arithmetic, group_step(): grad_sums = grad_sums.at[:, indices.reshape(-1)].add(both_grads)  31.3 us
    reshape x2, local copies, waits for them, and re-layouts, group_step(): jnp.stack([key_grad.reshape(group_size * KSEL, TILE, lane_width), value_g...  20.2 us
    squeeze x2, local copies, waits for them, and re-layouts, group_step(): picked[0]  17.6 us
    another operation x1, local copies, waits for them, and re-layouts, group_step(): jnp.stack([key_grad.reshape(group_size * KSEL, TILE, lane_width), value_g...  15.7 us
    unnamed x83, local copies, waits for them, and re-layouts  15.3 us
    ppermute x4, starting transfers between devices, shifted(): lax.ppermute(value, axis, [(source, source + steps) for source in range(l...  12.7 us
  transfers between devices with their start and end apart: 4, of which 2 were waited for; matrix products, arithmetic and copies ran while one was open for 12% of the time, Pallas kernels for 0%

commit v1 on v0

v1 whole, which is shorter than its diff:
```python
import functools

import jax
import jax.numpy as jnp
from jax import lax
from jax.experimental import pallas as pl
from jax.experimental.pallas import tpu as pltpu
from jax.sharding import PartitionSpec as P

HEADS = 20
HEAD_DIM = 128
TILE = 128
NEED = 2
KSEL = 6
FULL_WIDTH = HEADS * HEAD_DIM
NORM_EPS = 1e-06
SCALE = HEAD_DIM ** (-0.5)
PACK = NEED * TILE
VMEM_BYTES = 48 * 1024 * 1024
CHUNKS = (2, 2, 1)

VMEM = pl.BlockSpec(memory_space=pltpu.VMEM)
SMEM = pl.BlockSpec(memory_space=pltpu.SMEM)
F32 = jnp.float32
BF16 = jnp.bfloat16


def params():
    return pltpu.CompilerParams(vmem_limit_bytes=VMEM_BYTES)


def shifted(value, axis, steps):
    count = lax.axis_size(axis)
    leading, last = (max(0, -steps), min(count, count - steps))
    return lax.ppermute(value, axis, [(source, source + steps) for source in range(leading, last)])


def chunk_bounds(head_count):
    sizes = CHUNKS if sum(CHUNKS) == head_count else (1,) * head_count
    starts = [sum(sizes[:index]) for index in range(len(sizes))]
    return list(zip(starts, sizes))


def to_rows(columns):
    rows = columns[0].shape[0]
    lane = lax.broadcasted_iota(jnp.int32, (rows, 128), 1)
    packed = jnp.zeros((rows, 128), F32)
    for index, column in enumerate(columns):
        packed = jnp.where(lane == index, column, packed)
    return packed.T[:8]


def to_columns(rows, count):
    padded = jnp.concatenate([rows, jnp.zeros((120, rows.shape[1]), F32)], axis=0).T
    return [padded[:, index : index + 1] for index in range(count)]


def prepare_kernel(
    devices,
    tiles_here,
    position_ref,
    tile_at_slot,
    key_tiles,
    q_ref,
    k_ref,
    qt_ref,
    kt_ref,
    v_ref,
    vt_ref,
    plan_ref,
    up_ref,
    down_ref,
    sums_ref,
    slot_of,
):
    position = position_ref[0]

    def invert(slot, carry):
        slot_of[tile_at_slot[slot]] = slot
        return carry

    lax.fori_loop(0, devices * tiles_here, invert, 0)

    def remote_slots(device):
        return [
            slot_of[key_tiles[tile_at_slot[device * tiles_here + tile], column]]
            for tile in range(tiles_here)
            for column in range(tiles_here, KSEL)
        ]

    def first_last(slots, device):
        first = jnp.int32(tiles_here - 1)
        last = jnp.int32(0)
        for slot in slots:
            offset = slot - device * tiles_here
            inside = (offset >= 0) & (offset < tiles_here)
            first = jnp.where(inside, jnp.minimum(first, offset), first)
            last = jnp.where(inside, jnp.maximum(last, offset), last)
        return first, last

    above = remote_slots(jnp.minimum(position + 1, devices - 1))
    below = remote_slots(jnp.maximum(position - 1, 0))
    here = remote_slots(position)
    up_order = first_last(above, position)
    down_order = first_last(below, position)
    from_below, _ = first_last(here, position - 1)
    from_above, _ = first_last(here, position + 1)
    plan_ref[0], plan_ref[1] = up_order
    plan_ref[2], plan_ref[3] = down_order
    for index, slot in enumerate(here):
        low = jnp.where(slot == (position - 1) * tiles_here + from_below, 0, 1)
        high = jnp.where(slot == (position + 1) * tiles_here + from_above, 2, 3)
        plan_ref[4 + index] = jnp.where(slot < position * tiles_here, low, high)
    for order, packet in ((up_order, up_ref), (down_order, down_ref)):
        for rank in range(NEED):
            source = pl.ds(pl.multiple_of(order[rank] * TILE, TILE), TILE)
            packet[rank * TILE : (rank + 1) * TILE, :] = v_ref[source, :]
            packet[PACK + rank * TILE : PACK + (rank + 1) * TILE, :] = vt_ref[source, :]
    columns = []
    for raw_ref, moving_ref in ((q_ref, qt_ref), (k_ref, kt_ref)):
        raw = raw_ref[...].astype(F32)
        moving = moving_ref[...].astype(F32)
        columns.append(jnp.sum(raw * raw, axis=1, keepdims=True))
        columns.append(jnp.sum(raw * moving, axis=1, keepdims=True))
    sums_ref[...] = to_rows(columns)


def norm_kernel(
    bounds,
    plan,
    totals_ref,
    q_ref,
    k_ref,
    qt_ref,
    kt_ref,
    q_gain_ref,
    k_gain_ref,
    qn_ref,
    qnt_ref,
    kn_ref,
    knt_ref,
    *packets,
):
    totals = to_columns(totals_ref[...], 4)
    for first, raw_ref, moving_ref, gain_ref, normed_ref, tangent_ref in (
        (2, k_ref, kt_ref, k_gain_ref, kn_ref, knt_ref),
        (0, q_ref, qt_ref, q_gain_ref, qn_ref, qnt_ref),
    ):
        inverse = lax.rsqrt(totals[first] / FULL_WIDTH + NORM_EPS)
        drift = totals[first + 1] / FULL_WIDTH
        raw = raw_ref[...].astype(F32)
        moving = moving_ref[...].astype(F32)
        gain = gain_ref[...]
        normed_ref[...] = (raw * inverse * gain).astype(BF16)
        tangent_ref[...] = (
            gain * (moving * inverse - raw * (inverse * inverse * inverse * drift))
        ).astype(BF16)
    for index, (start, size) in enumerate(bounds):
        lanes = slice(start * HEAD_DIM, (start + size) * HEAD_DIM)
        for side in range(2):
            packet = packets[2 * index + side]
            for rank in range(NEED):
                source = pl.ds(pl.multiple_of(plan[2 * side + rank] * TILE, TILE), TILE)
                packet[rank * TILE : (rank + 1) * TILE, :] = kn_ref[source, lanes]
                packet[PACK + rank * TILE : PACK + (rank + 1) * TILE, :] = knt_ref[source, lanes]


def dot(left, right, left_axis, right_axis):
    return lax.dot_general(
        left, right, (((left_axis,), (right_axis,)), ((), ())), preferred_element_type=F32
    )


def attend_kernel(
    tiles_here,
    plan,
    q_ref,
    qt_ref,
    co_ref,
    k_ref,
    kt_ref,
    v_ref,
    vt_ref,
    kb_ref,
    ka_ref,
    vb_ref,
    va_ref,
    out_ref,
    ot_ref,
    qg_ref,
    local_ref,
    below_ref,
    above_ref,
    remote,
    remote_sum,
    local_sum,
):
    rows = tiles_here * TILE
    for base, kp_ref, vp_ref in ((0, kb_ref, vb_ref), (PACK, ka_ref, va_ref)):
        remote[base : base + PACK, 0:128] = kp_ref[:PACK, :]
        remote[base : base + PACK, 128:256] = kp_ref[PACK:, :]
        remote[base : base + PACK, 256:384] = vp_ref[:PACK, :]
        remote[base : base + PACK, 384:512] = vp_ref[PACK:, :]
    remote_sum[...] = jnp.zeros_like(remote_sum)
    k_local = jnp.concatenate([k_ref[...], kt_ref[...]], axis=1)
    v_local = jnp.concatenate([v_ref[...], vt_ref[...]], axis=1)
    for tile in range(tiles_here):
        here = slice(tile * TILE, (tile + 1) * TILE)
        places = [
            pl.ds(pl.multiple_of(plan[4 + tile * 2 + column] * TILE, TILE), TILE)
            for column in range(2)
        ]
        keys = jnp.concatenate([k_local] + [remote[place, 0:256] for place in places], axis=0)
        vals = jnp.concatenate([v_local] + [remote[place, 256:512] for place in places], axis=0)
        query, moving, cotangent = q_ref[here, :], qt_ref[here, :], co_ref[here, :]
        scores = dot(query, keys[:, :128], 1, 1)
        highest = jnp.max(scores, axis=1, keepdims=True)
        weights = jnp.exp((scores - highest) * SCALE)
        probs = weights * (1.0 / jnp.sum(weights, axis=1, keepdims=True))
        probs_half = probs.astype(BF16)
        both = dot(probs_half, vals, 1, 0)
        output = both[:, :128].astype(BF16)
        out_ref[here, :] = output
        score_tangent = dot(jnp.concatenate([moving, query], axis=1), keys, 1, 1) * SCALE
        centre = jnp.sum(probs * score_tangent, axis=1, keepdims=True)
        prob_tangent = (probs * (score_tangent - centre)).astype(BF16)
        ot_ref[here, :] = (dot(prob_tangent, vals[:, :128], 1, 0) + both[:, 128:]).astype(BF16)
        prob_grad = dot(cotangent, vals[:, :128], 1, 1)
        delta = jnp.sum(cotangent.astype(F32) * output.astype(F32), axis=1, keepdims=True)
        score_grad = (probs * (prob_grad - delta)).astype(BF16)
        qg_ref[here, :] = dot(score_grad, keys[:, :128], 1, 0) * SCALE
        key_grad = dot(score_grad, query, 0, 0)
        value_grad = dot(probs_half, cotangent, 0, 0)
        if tile == 0:
            local_sum[:, :128] = key_grad[:rows]
            local_sum[:, 128:] = value_grad[:rows]
        else:
            local_sum[:, :128] += key_grad[:rows]
            local_sum[:, 128:] += value_grad[:rows]
        for column, place in enumerate(places):
            piece = slice(rows + column * TILE, rows + (column + 1) * TILE)
            remote_sum[place, :128] += key_grad[piece]
            remote_sum[place, 128:] += value_grad[piece]
    local_ref[:rows, :] = (local_sum[:, :128] * SCALE).astype(BF16)
    local_ref[rows:, :] = local_sum[:, 128:].astype(BF16)
    for base, part_ref in ((0, below_ref), (PACK, above_ref)):
        part_ref[:PACK, :] = (remote_sum[base : base + PACK, :128] * SCALE).astype(BF16)
        part_ref[PACK:, :] = remote_sum[base : base + PACK, 128:].astype(BF16)


def merge_kernel(bounds, plan, q_ref, k_ref, q_gain_ref, k_gain_ref, *refs):
    count = len(bounds)
    qg, local, from_above, from_below = (refs[index * count : (index + 1) * count] for index in range(4))
    grad_v_ref, key_ref, sums_ref, value_ref = refs[4 * count :]
    rows = q_ref.shape[0]
    q_sum = jnp.zeros((rows, 1), F32)
    for index, (start, size) in enumerate(bounds):
        lanes = slice(start * HEAD_DIM, (start + size) * HEAD_DIM)
        key_ref[:, lanes] = local[index][:rows, :].astype(F32)
        value_ref[:, lanes] = local[index][rows:, :].astype(F32)
        for side, returned in enumerate((from_above[index], from_below[index])):
            for rank in range(NEED):
                place = pl.ds(pl.multiple_of(plan[2 * side + rank] * TILE, TILE), TILE)
                piece = slice(rank * TILE, (rank + 1) * TILE)
                key_ref[place, lanes] += returned[piece, :].astype(F32)
                piece = slice(PACK + rank * TILE, PACK + (rank + 1) * TILE)
                value_ref[place, lanes] += returned[piece, :].astype(F32)
        q_sum += jnp.sum(
            q_ref[:, lanes].astype(F32) * (q_gain_ref[:, lanes] * qg[index][...]),
            axis=1,
            keepdims=True,
        )
    grad_v_ref[...] = value_ref[...].astype(BF16)
    k_sum = jnp.sum(
        k_ref[...].astype(F32) * (k_gain_ref[...] * key_ref[...]), axis=1, keepdims=True
    )
    sums_ref[...] = to_rows([q_sum, k_sum])


def final_kernel(
    bounds, totals_ref, back_ref, q_ref, k_ref, q_gain_ref, k_gain_ref, key_ref, *refs
):
    count = len(bounds)
    qg, (grad_q_ref, grad_k_ref) = refs[:count], refs[count:]
    totals = to_columns(totals_ref[...], 4)
    back = to_columns(back_ref[...], 2)
    q_inverse = lax.rsqrt(totals[0] / FULL_WIDTH + NORM_EPS)
    k_inverse = lax.rsqrt(totals[2] / FULL_WIDTH + NORM_EPS)
    q_pull = q_inverse * q_inverse * q_inverse * (back[0] / FULL_WIDTH)
    k_pull = k_inverse * k_inverse * k_inverse * (back[1] / FULL_WIDTH)
    for index, (start, size) in enumerate(bounds):
        lanes = slice(start * HEAD_DIM, (start + size) * HEAD_DIM)
        grad_q_ref[:, lanes] = (
            q_inverse * (q_gain_ref[:, lanes] * qg[index][...])
            - q_ref[:, lanes].astype(F32) * q_pull
        ).astype(BF16)
    grad_k_ref[...] = (
        k_inverse * (k_gain_ref[...] * key_ref[...]) - k_ref[...].astype(F32) * k_pull
    ).astype(BF16)


def per_device(
    q_raw,
    k_raw,
    values,
    q_tangent,
    k_tangent,
    v_tangent,
    out_cotangent,
    q_gain,
    k_gain,
    tile_at_slot,
    key_tiles,
):
    rows, width = q_raw.shape
    head_count = width // HEAD_DIM
    tiles_here = rows // TILE
    devices = lax.axis_size("seq")
    bounds = chunk_bounds(head_count)
    position = lax.axis_index("seq").astype(jnp.int32).reshape(1)
    q_gain = q_gain.reshape(1, width)
    k_gain = k_gain.reshape(1, width)
    struct = jax.ShapeDtypeStruct

    plan, v_up, v_down, sums = pl.pallas_call(
        functools.partial(prepare_kernel, devices, tiles_here),
        out_shape=[
            struct((16,), jnp.int32),
            struct((2 * PACK, width), BF16),
            struct((2 * PACK, width), BF16),
            struct((8, rows), F32),
        ],
        in_specs=[SMEM] * 3 + [VMEM] * 6,
        out_specs=[SMEM] + [VMEM] * 3,
        scratch_shapes=[pltpu.SMEM((devices * tiles_here,), jnp.int32)],
        compiler_params=params(),
        name="prepare",
    )(position, tile_at_slot, key_tiles, q_raw, k_raw, q_tangent, k_tangent, values, v_tangent)
    v_below = shifted(v_up, "seq", 1)
    v_above = shifted(v_down, "seq", -1)
    totals = lax.psum(sums, "head")
    packet_shapes = [
        struct((2 * PACK, size * HEAD_DIM), BF16) for _, size in bounds for _ in range(2)
    ]
    qn, qnt, kn, knt, *packets = pl.pallas_call(
        functools.partial(norm_kernel, bounds),
        out_shape=[struct((rows, width), BF16)] * 4 + packet_shapes,
        in_specs=[SMEM] + [VMEM] * 7,
        out_specs=[VMEM] * (4 + len(packet_shapes)),
        compiler_params=params(),
        name="norm",
    )(plan, totals, q_raw, k_raw, q_tangent, k_tangent, q_gain, k_gain)
    k_below = [shifted(packet, "seq", 1) for packet in packets[0::2]]
    k_above = [shifted(packet, "seq", -1) for packet in packets[1::2]]

    results = []
    for index, (start, size) in enumerate(bounds):
        def whole(head, plan_ref, start=start):
            return (0, start + head)

        def part(head, plan_ref):
            return (0, head)

        full_spec = pl.BlockSpec((rows, HEAD_DIM), whole)
        results.append(
            pl.pallas_call(
                functools.partial(attend_kernel, tiles_here),
                grid_spec=pltpu.PrefetchScalarGridSpec(
                    num_scalar_prefetch=1,
                    grid=(size,),
                    in_specs=[full_spec] * 7
                    + [pl.BlockSpec((2 * PACK, HEAD_DIM), part)] * 2
                    + [pl.BlockSpec((2 * PACK, HEAD_DIM), whole)] * 2,
                    out_specs=[pl.BlockSpec((rows, HEAD_DIM), part)] * 3
                    + [pl.BlockSpec((2 * rows, HEAD_DIM), part)]
                    + [pl.BlockSpec((2 * PACK, HEAD_DIM), part)] * 2,
                    scratch_shapes=[
                        pltpu.VMEM((2 * PACK, 4 * HEAD_DIM), BF16),
                        pltpu.VMEM((2 * PACK, 2 * HEAD_DIM), F32),
                        pltpu.VMEM((rows, 2 * HEAD_DIM), F32),
                    ],
                ),
                out_shape=[
                    struct((rows, size * HEAD_DIM), BF16),
                    struct((rows, size * HEAD_DIM), BF16),
                    struct((rows, size * HEAD_DIM), F32),
                    struct((2 * rows, size * HEAD_DIM), BF16),
                    struct((2 * PACK, size * HEAD_DIM), BF16),
                    struct((2 * PACK, size * HEAD_DIM), BF16),
                ],
                cost_estimate=pl.CostEstimate(
                    flops=20 * size * rows * KSEL * TILE * HEAD_DIM,
                    bytes_accessed=24 * size * rows * HEAD_DIM,
                    transcendentals=size * rows * KSEL * TILE,
                ),
                compiler_params=params(),
                name="attend",
            )(
                plan, qn, qnt, out_cotangent, kn, knt, values, v_tangent,
                k_below[index], k_above[index], v_below, v_above,
            )
        )
    outs, tangents, query_grads, locals_, to_below, to_above = zip(*results)
    from_above = [shifted(packet, "seq", -1) for packet in to_below]
    from_below = [shifted(packet, "seq", 1) for packet in to_above]
    count = len(bounds)
    grad_v, key_total, back_sums = pl.pallas_call(
        functools.partial(merge_kernel, bounds),
        out_shape=[
            struct((rows, width), BF16), struct((rows, width), F32), struct((8, rows), F32)
        ],
        in_specs=[SMEM] + [VMEM] * (4 + 4 * count),
        out_specs=[VMEM] * 3,
        scratch_shapes=[pltpu.VMEM((rows, width), F32)],
        compiler_params=params(),
        name="merge",
    )(plan, q_raw, k_raw, q_gain, k_gain, *query_grads, *locals_, *from_above, *from_below)
    back = lax.psum(back_sums, "head")
    grad_q, grad_k = pl.pallas_call(
        functools.partial(final_kernel, bounds),
        out_shape=[struct((rows, width), BF16)] * 2,
        in_specs=[VMEM] * (7 + count),
        out_specs=[VMEM] * 2,
        compiler_params=params(),
        name="final",
    )(totals, back, q_raw, k_raw, q_gain, k_gain, key_total, *query_grads)
    return (
        jnp.concatenate(outs, axis=1),
        jnp.concatenate(tangents, axis=1),
        grad_q,
        grad_k,
        grad_v,
    )


def solution(mesh):
    rows, lanes, copied = P("seq", "head"), P("head"), P()
    return jax.shard_map(
        per_device,
        mesh=mesh,
        in_specs=(rows,) * 7 + (lanes,) * 2 + (copied,) * 2,
        out_specs=(rows,) * 5,
        check_vma=False,
    )
```

time: 406 us -> 142 us (0.35); the launches traced: 399 us -> 140 us
  local copies, waits for them, and re-layouts: 156 us -> 9.31 us
  other arithmetic: 94.9 us -> 1.17 us
  matrix products: 84.8 us -> 0 us
  starting transfers between devices: 12.7 us -> 54.9 us
  Pallas kernels: 0 us -> 38.2 us
  waiting for transfers between devices: 36.5 us -> 15.1 us
  blocking collectives: 12.2 us -> 20.3 us
    dot_general x10 -> x0, matrix products: 84.8 us -> none  [product(): return jnp.einsum(form, left, right, preferred_element_type=jnp.float32)]
    squeeze x9 -> x0, local copies, waits for them, and re-layouts: 54.7 us -> none  [the longest x2 17.6 us: group_step(): picked[0]]
    ppermute x4 -> x14, starting transfers between devices: 12.7 us -> 54.9 us  [shifted(): lax.ppermute(value, axis, [(source, source + steps) for source in range(l...]
    pallas_call x0 -> x7, Pallas kernels: none -> 38.2 us  [the longest x3 28.8 us: per_device(): pl.pallas_call(functools.partial(attend_kernel, tiles_here), grid_spec=pl...]
    scatter-add x3 -> x0, other arithmetic: 36 us -> none  [the longest x1 31.3 us: group_step(): grad_sums = grad_sums.at[:, indices.reshape(-1)].add(both_grads)]
    ppermute x4 -> x14, waiting for transfers between devices: 36.5 us -> 15.1 us  [shifted(): lax.ppermute(value, axis, [(source, source + steps) for source in range(l...]
    reshape x4 -> x2, local copies, waits for them, and re-layouts: 20.4 us -> 0.01 us  [the longest x1 0.01 us: per_device(): q_gain = q_gain.reshape(1, width)]
    gather x8 -> x0, local copies, waits for them, and re-layouts: 17 us -> none  [the longest x1 9.79 us: group_step(): jnp.take(buffer, indices.reshape(-1), axis=1)]
  transfers between devices with their start and end apart: 4 -> 14, of which waited for: 2 -> 4; matrix products, arithmetic and copies ran while one was open for 12% -> 1% of each run, Pallas kernels for 0% -> 22%
where the time goes in v1:
time: 142 us; the launch traced here: 140 us
  starting transfers between devices  54.9 us (39%)
  Pallas kernels  38.2 us (27%)
  blocking collectives  20.3 us (14%)
  waiting for transfers between devices  15.1 us (11%)
  local copies, waits for them, and re-layouts  9.31 us (7%)
    ppermute x14, starting transfers between devices, shifted(): lax.ppermute(value, axis, [(source, source + steps) for source in range(l...  54.9 us
    pallas_call x3, Pallas kernels, per_device(): pl.pallas_call(functools.partial(attend_kernel, tiles_here), grid_spec=pl...  28.8 us
    ppermute x14, waiting for transfers between devices, shifted(): lax.ppermute(value, axis, [(source, source + steps) for source in range(l...  15.1 us
    psum x1, blocking collectives, per_device(): totals = lax.psum(sums, 'head')  10.8 us
    psum x1, blocking collectives, per_device(): back = lax.psum(back_sums, 'head')  9.53 us
    unnamed x35, local copies, waits for them, and re-layouts  9.3 us
  transfers between devices with their start and end apart: 14, of which 4 were waited for; matrix products, arithmetic and copies ran while one was open for 1% of the time, Pallas kernels for 22%

profile of v1, /device:TPU:25, one launch (start us, length us, event | category | flops | bytes accessed | tf_op | source)
XLA Modules:
  0.0 139.9 jit_solution(9568770394353244247)
XLA Ops:
  0.6 0.8 copy.16.key_tiles
  1.4 1.1 copy-done
  2.5 1.1 copy-done.2
  3.6 1.1 copy-done.4
  4.7 1.1 copy-done.6
  5.8 1.1 copy-done.8
  6.8 1.1 copy-done.10
  7.9 0.7 copy-done.13
  8.6 2.7 %prepare.1 = (s32[16]{0:T(128)S(1)}, bf16[512,640]{1,0:T(8,128)(2,1)}, bf16[512,640]{1,0:T(8,128)(2,1)S(1)}, f32[8,512]{1,0:T(8,128)S(1)}) custom-call(s32[1]{0:T(128)} %bitcast.position_ref, s32[32]{0:T(128)S(1)} %copy-done.13, s32[32,6]{1,0:T(8,128)S(1)} %copy.16.key_tiles, bf16[512,640]{1,0:T(8,128)(2,1)S(1)} %copy-done, bf16[512,640]{1,0:T(8,128)(2,1)S(1)} %copy-done.2, ...), custom_call_target="tpu_custom_call" | custom-call | tf_op jit(solution)/shard_map/prepare/pallas_call | solution.py:325
  11.3 3.1 %collective-permute-start.2 = (bf16[512,640]{1,0:T(8,128)(2,1)}, bf16[512,640]{1,0:T(8,128)(2,1)S(1)}, u32[]{:S(2)}, u32[]{:S(2)}) collective-permute-start(bf16[512,640]{1,0:T(8,128)(2,1)} %get-tuple-element.50), channel_id=1, source_target_pairs={{0,4},{4,8},{8,12},{12,16},{16,20},{20,24},{24,28},{1,5},{5,9},{9,... | collective-permute-start | bytes 1966088 | tf_op jit(solution)/shard_map/ppermute | solution.py:35
  14.5 3.1 %collective-permute-start.3 = (bf16[512,640]{1,0:T(8,128)(2,1)S(1)}, bf16[512,640]{1,0:T(8,128)(2,1)}, u32[]{:S(2)}, u32[]{:S(2)}) collective-permute-start(bf16[512,640]{1,0:T(8,128)(2,1)S(1)} %get-tuple-element.51), channel_id=1, source_target_pairs={{4,0},{8,4},{12,8},{16,12},{20,16},{24,20},{28,24},{5,1},{9,5},{13... | collective-permute-start | bytes 1966088 | tf_op jit(solution)/shard_map/ppermute | solution.py:35
  17.6 10.8 %psum.14.totals_ref = f32[8,512]{1,0:T(8,128)S(1)} all-reduce(f32[8,512]{1,0:T(8,128)S(1)} %get-tuple-element.43), channel_id=1, replica_groups=mesh['seq'=8,'head'=4] {'head'}, use_global_device_ids=true, to_apply=%region_0.0 | all-reduce | flops 4096 | bytes 32768 | tf_op jit(solution)/shard_map/psum | solution.py:341
  28.4 0.0 copy-start.12
  28.4 2.4 %norm.1 = (bf16[512,640]{1,0:T(8,128)(2,1)S(1)}, bf16[512,640]{1,0:T(8,128)(2,1)S(1)}, bf16[512,640]{1,0:T(8,128)(2,1)S(1)}, bf16[512,640]{1,0:T(8,128)(2,1)S(1)...) custom-call(s32[16]{0:T(128)S(1)} %get-tuple-element.42.plan, ...), custom_call_target="tpu_custom_call" | custom-call | tf_op jit(solution)/shard_map/norm/pallas_call | solution.py:345
  30.8 3.0 %collective-permute-start = (bf16[512,256]{1,0:T(8,128)(2,1)S(1)}, bf16[512,256]{1,0:T(8,128)(2,1)S(1)}, u32[]{:S(2)}, u32[]{:S(2)}) collective-permute-start(bf16[512,256]{1,0:T(8,128)(2,1)S(1)} %get-tuple-element.48), channel_id=1, source_target_pairs={{0,4},{4,8},{8,12},{12,16},{16,20},{20,24},{24,28},{1,5},{5,9},{9,... | collective-permute-start | bytes 786440 | tf_op jit(solution)/shard_map/ppermute | solution.py:35
  33.8 3.2 %collective-permute-start.1 = (bf16[512,256]{1,0:T(8,128)(2,1)S(1)}, bf16[512,256]{1,0:T(8,128)(2,1)S(1)}, u32[]{:S(2)}, u32[]{:S(2)}) collective-permute-start(bf16[512,256]{1,0:T(8,128)(2,1)S(1)} %get-tuple-element.49), channel_id=1, source_target_pairs={{4,0},{8,4},{12,8},{16,12},{20,16},{24,20},{28,24},{5,1},{9,5},{13... | collective-permute-start | bytes 786440 | tf_op jit(solution)/shard_map/ppermute | solution.py:35
  37.0 2.1 %collective-permute-start.4 = (bf16[512,256]{1,0:T(8,128)(2,1)S(1)}, bf16[512,256]{1,0:T(8,128)(2,1)S(1)}, u32[]{:S(2)}, u32[]{:S(2)}) collective-permute-start(bf16[512,256]{1,0:T(8,128)(2,1)S(1)} %get-tuple-element.53), channel_id=1, source_target_pairs={{0,4},{4,8},{8,12},{12,16},{16,20},{20,24},{24,28},{1,5},{5,9},{9,... | collective-permute-start | bytes 786440 | tf_op jit(solution)/shard_map/ppermute | solution.py:35
  39.1 0.9 collective-permute-done.kb_ref
  40.1 17.2 %collective-permute-start.5 = (bf16[512,256]{1,0:T(8,128)(2,1)S(1)}, bf16[512,256]{1,0:T(8,128)(2,1)S(1)}, u32[]{:S(2)}, u32[]{:S(2)}) collective-permute-start(bf16[512,256]{1,0:T(8,128)(2,1)S(1)} %get-tuple-element.54), channel_id=1, source_target_pairs={{4,0},{8,4},{12,8},{16,12},{20,16},{24,20},{28,24},{5,1},{9,5},{13... | collective-permute-start | bytes 786440 | tf_op jit(solution)/shard_map/ppermute | solution.py:35
  57.3 4.6 %collective-permute-done.1.ka_ref = bf16[512,256]{1,0:T(8,128)(2,1)S(1)} collective-permute-done((bf16[512,256]{1,0:T(8,128)(2,1)S(1)}, bf16[512,256]{1,0:T(8,128)(2,1)S(1)}, u32[]{:S(2)}, u32[]{:S(2)}) %collective-permute-start.1) | collective-permute-done | bytes 262176 | tf_op jit(solution)/shard_map/ppermute | solution.py:35
  61.9 1.9 %collective-permute-start.6 = (bf16[512,128]{1,0:T(8,128)(2,1)S(1)}, bf16[512,128]{1,0:T(8,128)(2,1)S(1)}, u32[]{:S(2)}, u32[]{:S(2)}) collective-permute-start(bf16[512,128]{1,0:T(8,128)(2,1)S(1)} %get-tuple-element.56), channel_id=1, source_target_pairs={{0,4},{4,8},{8,12},{12,16},{16,20},{20,24},{24,28},{1,5},{5,9},{9,... | collective-permute-start | bytes 393224 | tf_op jit(solution)/shard_map/ppermute | solution.py:35
  63.8 0.0 collective-permute-done.2.vb_ref
  63.8 0.0 copy-start.14
  63.8 4.3 %collective-permute-start.7 = (bf16[512,128]{1,0:T(8,128)(2,1)S(1)}, bf16[512,128]{1,0:T(8,128)(2,1)S(1)}, u32[]{:S(2)}, u32[]{:S(2)}) collective-permute-start(bf16[512,128]{1,0:T(8,128)(2,1)S(1)} %get-tuple-element.57), channel_id=1, source_target_pairs={{4,0},{8,4},{12,8},{16,12},{20,16},{24,20},{28,24},{5,1},{9,5},{13... | collective-permute-start | bytes 393224 | tf_op jit(solution)/shard_map/ppermute | solution.py:35
  68.1 0.0 collective-permute-done.3.va_ref
  68.1 0.0 copy-start.5
  68.1 0.0 copy-start.7
  68.2 11.3 %attend.3 = (bf16[512,256]{1,0:T(8,128)(2,1)S(1)}, bf16[512,256]{1,0:T(8,128)(2,1)S(1)}, f32[512,256]{1,0:T(8,128)S(1)}, bf16[1024,256]{1,0:T(8,128)(2,1)S(1)}, ...) custom-call(s32[16]{0:T(128)S(1)} %get-tuple-element.42.plan, bf16[512,640]{1,0:T(8,128)(2,1)S(1)} %get-tuple-element.44.q_ref, ...), custom_call_target="tpu_custom_call" | custom-call | flops 2013265920 | bytes 3145728 | tf_op jit(solution)/shard_map/attend/pallas_call | solution.py:366
  79.4 1.9 %collective-permute-start.11 = (bf16[512,256]{1,0:T(8,128)(2,1)S(1)}, bf16[512,256]{1,0:T(8,128)(2,1)S(1)}, u32[]{:S(2)}, u32[]{:S(2)}) collective-permute-start(bf16[512,256]{1,0:T(8,128)(2,1)S(1)} %get-tuple-element.71), channel_id=1, source_target_pairs={{0,4},{4,8},{8,12},{12,16},{16,20},{20,24},{24,28},{1,5},{5,9},{9,... | collective-permute-start | bytes 786440 | tf_op jit(solution)/shard_map/ppermute | solution.py:35
  81.4 0.0 collective-permute-done.6.kb_ref
  81.4 4.3 %collective-permute-start.8 = (bf16[512,256]{1,0:T(8,128)(2,1)S(1)}, bf16[512,256]{1,0:T(8,128)(2,1)S(1)}, u32[]{:S(2)}, u32[]{:S(2)}) collective-permute-start(bf16[512,256]{1,0:T(8,128)(2,1)S(1)} %get-tuple-element.68), channel_id=1, source_target_pairs={{4,0},{8,4},{12,8},{16,12},{20,16},{24,20},{28,24},{5,1},{9,5},{13... | collective-permute-start | bytes 786440 | tf_op jit(solution)/shard_map/ppermute | solution.py:35
  85.6 0.0 collective-permute-done.7.ka_ref
  85.7 6.2 %attend.5 = (bf16[512,128]{1,0:T(8,128)(2,1)S(1)}, bf16[512,128]{1,0:T(8,128)(2,1)S(1)}, f32[512,128]{1,0:T(8,128)S(1)}, bf16[1024,128]{1,0:T(8,128)(2,1)S(1)}, ...) custom-call(s32[16]{0:T(128)S(1)} %get-tuple-element.42.plan, bf16[512,640]{1,0:T(8,128)(2,1)S(1)} %get-tuple-element.44.q_ref, ...), custom_call_target="tpu_custom_call" | custom-call | flops 1006632960 | bytes 1572864 | tf_op jit(solution)/shard_map/attend/pallas_call | solution.py:366
  91.9 2.1 %collective-permute-start.10 = (bf16[512,128]{1,0:T(8,128)(2,1)S(1)}, bf16[512,128]{1,0:T(8,128)(2,1)S(1)}, u32[]{:S(2)}, u32[]{:S(2)}) collective-permute-start(bf16[512,128]{1,0:T(8,128)(2,1)S(1)} %get-tuple-element.70), channel_id=1, source_target_pairs={{4,0},{8,4},{12,8},{16,12},{20,16},{24,20},{28,24},{5,1},{9,5},{13... | collective-permute-start | bytes 393224 | tf_op jit(solution)/shard_map/ppermute | solution.py:35
  94.0 11.3 %attend.4 = (bf16[512,256]{1,0:T(8,128)(2,1)S(1)}, bf16[512,256]{1,0:T(8,128)(2,1)S(1)}, f32[512,256]{1,0:T(8,128)S(1)}, bf16[1024,256]{1,0:T(8,128)(2,1)S(1)}, ...) custom-call(s32[16]{0:T(128)S(1)} %get-tuple-element.42.plan, bf16[512,640]{1,0:T(8,128)(2,1)S(1)} %get-tuple-element.44.q_ref, ...), custom_call_target="tpu_custom_call" | custom-call | flops 2013265920 | bytes 3145728 | tf_op jit(solution)/shard_map/attend/pallas_call | solution.py:366
  105.3 3.4 %collective-permute-start.12 = (bf16[512,256]{1,0:T(8,128)(2,1)S(1)}, bf16[512,256]{1,0:T(8,128)(2,1)S(1)}, u32[]{:S(2)}, u32[]{:S(2)}) collective-permute-start(bf16[512,256]{1,0:T(8,128)(2,1)S(1)} %get-tuple-element.72), channel_id=1, source_target_pairs={{0,4},{4,8},{8,12},{12,16},{16,20},{20,24},{24,28},{1,5},{5,9},{9,... | collective-permute-start | bytes 786440 | tf_op jit(solution)/shard_map/ppermute | solution.py:35
  108.7 2.8 %collective-permute-start.9 = (bf16[512,256]{1,0:T(8,128)(2,1)S(1)}, bf16[512,256]{1,0:T(8,128)(2,1)S(1)}, u32[]{:S(2)}, u32[]{:S(2)}) collective-permute-start(bf16[512,256]{1,0:T(8,128)(2,1)S(1)} %get-tuple-element.69), channel_id=1, source_target_pairs={{4,0},{8,4},{12,8},{16,12},{20,16},{24,20},{28,24},{5,1},{9,5},{13... | collective-permute-start | bytes 786440 | tf_op jit(solution)/shard_map/ppermute | solution.py:35
  111.5 0.0 collective-permute-done.10.refs_8_
  111.5 2.5 %collective-permute-start.13 = (bf16[512,128]{1,0:T(8,128)(2,1)S(1)}, bf16[512,128]{1,0:T(8,128)(2,1)S(1)}, u32[]{:S(2)}, u32[]{:S(2)}) collective-permute-start(bf16[512,128]{1,0:T(8,128)(2,1)S(1)} %get-tuple-element.73), channel_id=1, source_target_pairs={{0,4},{4,8},{8,12},{12,16},{16,20},{20,24},{24,28},{1,5},{5,9},{9,... | collective-permute-start | bytes 393224 | tf_op jit(solution)/shard_map/ppermute | solution.py:35
  114.0 1.2 pad_maximum_fusion
  115.2 3.1 %collective-permute-done.13.refs_11_ = bf16[512,128]{1,0:T(8,128)(2,1)S(1)} collective-permute-done((bf16[512,128]{1,0:T(8,128)(2,1)S(1)}, bf16[512,128]{1,0:T(8,128)(2,1)S(1)}, u32[]{:S(2)}, u32[]{:S(2)}) %collective-permute-start.13) | collective-permute-done | bytes 131104 | tf_op jit(solution)/shard_map/ppermute | solution.py:35
  118.2 0.0 collective-permute-done.11.refs_9_
  118.2 0.0 collective-permute-done.8.refs_6_
  118.3 6.5 %collective-permute-done.9.refs_7_ = bf16[512,256]{1,0:T(8,128)(2,1)S(1)} collective-permute-done((bf16[512,256]{1,0:T(8,128)(2,1)S(1)}, bf16[512,256]{1,0:T(8,128)(2,1)S(1)}, u32[]{:S(2)}, u32[]{:S(2)}) %collective-permute-start.9) | collective-permute-done | bytes 262176 | tf_op jit(solution)/shard_map/ppermute | solution.py:35
  124.8 2.6 %merge.1 = (bf16[512,640]{1,0:T(8,128)(2,1)}, f32[512,640]{1,0:T(8,128)}, f32[8,512]{1,0:T(8,128)S(1)}) custom-call(s32[16]{0:T(128)S(1)} %get-tuple-element.42.plan, bf16[512,640]{1,0:T(8,128)(2,1)S(1)} %copy-done.1, bf16[512,640]{1,0:T(8,128)(2,1)S(1)} %copy-done.3, f32[1,640]{1,0:T(1,128)S(1)} %reshape.20.q_gain_ref, f32[1,640]{1,0:T(1,128)S(1)} %reshape.21.k_gain_ref, ...), custom_call_target="tpu_custom_call" | custom-call | tf_op jit(solution)/shard_map/merge/pallas_call | solution.py:407
  127.4 9.5 %psum.15.back_ref = f32[8,512]{1,0:T(8,128)S(1)} all-reduce(f32[8,512]{1,0:T(8,128)S(1)} %get-tuple-element.74), channel_id=1, replica_groups=mesh['seq'=8,'head'=4] {'head'}, use_global_device_ids=true, to_apply=%region_1.0 | all-reduce | flops 4096 | bytes 32768 | tf_op jit(solution)/shard_map/psum | solution.py:418
  136.9 1.3 copy-done.11
  138.2 1.7 %final.1 = (bf16[512,640]{1,0:T(8,128)(2,1)}, bf16[512,640]{1,0:T(8,128)(2,1)}) custom-call(f32[8,512]{1,0:T(8,128)S(1)} %psum.14.totals_ref, f32[8,512]{1,0:T(8,128)S(1)} %psum.15.back_ref, bf16[512,640]{1,0:T(8,128)(2,1)S(1)} %copy-done.1, bf16[512,640]{1,0:T(8,128)(2,1)S(1)} %copy-done.3, f32[1,640]{1,0:T(1,128)S(1)} %reshape.20.q_gain_ref, ...), custom_call_target="tpu_custom_call" | custom-call | tf_op jit(solution)/shard_map/final/pallas_call | solution.py:419
  (27 shorter events, 0.1 us)
Async XLA Ops:
  1.4 1.1 copy-start
  2.5 1.1 copy-start.2
  3.6 1.1 copy-start.4
  4.7 1.1 copy-start.6
  5.8 1.1 copy-start.8
  6.8 1.1 copy-start.10
  7.9 0.7 copy-start.13
  8.6 8.9 %copy-start.15 = (f32[640]{0:T(1024)S(1)}, f32[640]{0:T(1024)}, u32[]{:S(2)}) copy-start(f32[640]{0:T(1024)} %param.18) | copy-start | bytes 7684
  8.6 9.0 %copy-start.16 = (f32[640]{0:T(1024)S(1)}, f32[640]{0:T(1024)}, u32[]{:S(2)}) copy-start(f32[640]{0:T(1024)} %param.19) | copy-start | bytes 7684
  8.6 19.8 %copy-start.1 = (bf16[512,640]{1,0:T(8,128)(2,1)S(1)}, bf16[512,640]{1,0:T(8,128)(2,1)}, u32[]{:S(2)}) copy-start(bf16[512,640]{1,0:T(8,128)(2,1)} %q_ref.7) | copy-start | bytes 1966084
  8.6 19.8 %copy-start.3 = (bf16[512,640]{1,0:T(8,128)(2,1)S(1)}, bf16[512,640]{1,0:T(8,128)(2,1)}, u32[]{:S(2)}) copy-start(bf16[512,640]{1,0:T(8,128)(2,1)} %k_ref.7) | copy-start | bytes 1966084
  8.6 19.8 %copy-start.9 = (bf16[512,640]{1,0:T(8,128)(2,1)S(1)}, bf16[512,640]{1,0:T(8,128)(2,1)}, u32[]{:S(2)}) copy-start(bf16[512,640]{1,0:T(8,128)(2,1)} %qt_ref.3) | copy-start | bytes 1966084
  11.3 52.5 %collective-permute-start.2 = (bf16[512,640]{1,0:T(8,128)(2,1)}, bf16[512,640]{1,0:T(8,128)(2,1)S(1)}, u32[]{:S(2)}, u32[]{:S(2)}) collective-permute-start(bf16[512,640]{1,0:T(8,128)(2,1)} %get-tuple-element.50), channel_id=1, source_target_pairs={{0,4},{4,8},{8,12},{12,16},{16,20},{20,24},{24,28},{1,5},{5,9},{9,... | collective-permute-start | bytes 1966088 | tf_op jit(solution)/shard_map/ppermute | solution.py:35
  14.5 53.6 %collective-permute-start.3 = (bf16[512,640]{1,0:T(8,128)(2,1)S(1)}, bf16[512,640]{1,0:T(8,128)(2,1)}, u32[]{:S(2)}, u32[]{:S(2)}) collective-permute-start(bf16[512,640]{1,0:T(8,128)(2,1)S(1)} %get-tuple-element.51), channel_id=1, source_target_pairs={{4,0},{8,4},{12,8},{16,12},{20,16},{24,20},{28,24},{5,1},{9,5},{13... | collective-permute-start | bytes 1966088 | tf_op jit(solution)/shard_map/ppermute | solution.py:35
  28.4 39.7 %copy-start.12 = (bf16[512,640]{1,0:T(8,128)(2,1)S(1)}, bf16[512,640]{1,0:T(8,128)(2,1)}, u32[]{:S(2)}) copy-start(bf16[512,640]{1,0:T(8,128)(2,1)} %co_ref.5) | copy-start | bytes 1966084
  30.8 9.3 %collective-permute-start = (bf16[512,256]{1,0:T(8,128)(2,1)S(1)}, bf16[512,256]{1,0:T(8,128)(2,1)S(1)}, u32[]{:S(2)}, u32[]{:S(2)}) collective-permute-start(bf16[512,256]{1,0:T(8,128)(2,1)S(1)} %get-tuple-element.48), channel_id=1, source_target_pairs={{0,4},{4,8},{8,12},{12,16},{16,20},{20,24},{24,28},{1,5},{5,9},{9,... | collective-permute-start | bytes 786440 | tf_op jit(solution)/shard_map/ppermute | solution.py:35
  33.8 28.1 %collective-permute-start.1 = (bf16[512,256]{1,0:T(8,128)(2,1)S(1)}, bf16[512,256]{1,0:T(8,128)(2,1)S(1)}, u32[]{:S(2)}, u32[]{:S(2)}) collective-permute-start(bf16[512,256]{1,0:T(8,128)(2,1)S(1)} %get-tuple-element.49), channel_id=1, source_target_pairs={{4,0},{8,4},{12,8},{16,12},{20,16},{24,20},{28,24},{5,1},{9,5},{13... | collective-permute-start | bytes 786440 | tf_op jit(solution)/shard_map/ppermute | solution.py:35
  37.0 57.0 %collective-permute-start.4 = (bf16[512,256]{1,0:T(8,128)(2,1)S(1)}, bf16[512,256]{1,0:T(8,128)(2,1)S(1)}, u32[]{:S(2)}, u32[]{:S(2)}) collective-permute-start(bf16[512,256]{1,0:T(8,128)(2,1)S(1)} %get-tuple-element.53), channel_id=1, source_target_pairs={{0,4},{4,8},{8,12},{12,16},{16,20},{20,24},{24,28},{1,5},{5,9},{9,... | collective-permute-start | bytes 786440 | tf_op jit(solution)/shard_map/ppermute | solution.py:35
  40.1 54.0 %collective-permute-start.5 = (bf16[512,256]{1,0:T(8,128)(2,1)S(1)}, bf16[512,256]{1,0:T(8,128)(2,1)S(1)}, u32[]{:S(2)}, u32[]{:S(2)}) collective-permute-start(bf16[512,256]{1,0:T(8,128)(2,1)S(1)} %get-tuple-element.54), channel_id=1, source_target_pairs={{4,0},{8,4},{12,8},{16,12},{20,16},{24,20},{28,24},{5,1},{9,5},{13... | collective-permute-start | bytes 786440 | tf_op jit(solution)/shard_map/ppermute | solution.py:35
  61.9 19.5 %collective-permute-start.6 = (bf16[512,128]{1,0:T(8,128)(2,1)S(1)}, bf16[512,128]{1,0:T(8,128)(2,1)S(1)}, u32[]{:S(2)}, u32[]{:S(2)}) collective-permute-start(bf16[512,128]{1,0:T(8,128)(2,1)S(1)} %get-tuple-element.56), channel_id=1, source_target_pairs={{0,4},{4,8},{8,12},{12,16},{16,20},{20,24},{24,28},{1,5},{5,9},{9,... | collective-permute-start | bytes 393224 | tf_op jit(solution)/shard_map/ppermute | solution.py:35
  63.8 4.3 %copy-start.14 = (bf16[512,640]{1,0:T(8,128)(2,1)}, bf16[512,640]{1,0:T(8,128)(2,1)S(1)}, u32[]{:S(2)}) copy-start(bf16[512,640]{1,0:T(8,128)(2,1)S(1)} %collective-permute-done.2.vb_ref) | copy-start | bytes 1966084
  63.8 21.8 %collective-permute-start.7 = (bf16[512,128]{1,0:T(8,128)(2,1)S(1)}, bf16[512,128]{1,0:T(8,128)(2,1)S(1)}, u32[]{:S(2)}, u32[]{:S(2)}) collective-permute-start(bf16[512,128]{1,0:T(8,128)(2,1)S(1)} %get-tuple-element.57), channel_id=1, source_target_pairs={{4,0},{8,4},{12,8},{16,12},{20,16},{24,20},{28,24},{5,1},{9,5},{13... | collective-permute-start | bytes 393224 | tf_op jit(solution)/shard_map/ppermute | solution.py:35
  68.1 17.5 %copy-start.5 = (bf16[512,640]{1,0:T(8,128)(2,1)S(1)}, bf16[512,640]{1,0:T(8,128)(2,1)}, u32[]{:S(2)}) copy-start(bf16[512,640]{1,0:T(8,128)(2,1)} %v_ref.7) | copy-start | bytes 1966084
  68.1 17.5 %copy-start.7 = (bf16[512,640]{1,0:T(8,128)(2,1)S(1)}, bf16[512,640]{1,0:T(8,128)(2,1)}, u32[]{:S(2)}) copy-start(bf16[512,640]{1,0:T(8,128)(2,1)} %vt_ref.7) | copy-start | bytes 1966084
  79.4 38.8 %collective-permute-start.11 = (bf16[512,256]{1,0:T(8,128)(2,1)S(1)}, bf16[512,256]{1,0:T(8,128)(2,1)S(1)}, u32[]{:S(2)}, u32[]{:S(2)}) collective-permute-start(bf16[512,256]{1,0:T(8,128)(2,1)S(1)} %get-tuple-element.71), channel_id=1, source_target_pairs={{0,4},{4,8},{8,12},{12,16},{16,20},{20,24},{24,28},{1,5},{5,9},{9,... | collective-permute-start | bytes 786440 | tf_op jit(solution)/shard_map/ppermute | solution.py:35
  81.4 36.9 %collective-permute-start.8 = (bf16[512,256]{1,0:T(8,128)(2,1)S(1)}, bf16[512,256]{1,0:T(8,128)(2,1)S(1)}, u32[]{:S(2)}, u32[]{:S(2)}) collective-permute-start(bf16[512,256]{1,0:T(8,128)(2,1)S(1)} %get-tuple-element.68), channel_id=1, source_target_pairs={{4,0},{8,4},{12,8},{16,12},{20,16},{24,20},{28,24},{5,1},{9,5},{13... | collective-permute-start | bytes 786440 | tf_op jit(solution)/shard_map/ppermute | solution.py:35
  91.9 19.6 %collective-permute-start.10 = (bf16[512,128]{1,0:T(8,128)(2,1)S(1)}, bf16[512,128]{1,0:T(8,128)(2,1)S(1)}, u32[]{:S(2)}, u32[]{:S(2)}) collective-permute-start(bf16[512,128]{1,0:T(8,128)(2,1)S(1)} %get-tuple-element.70), channel_id=1, source_target_pairs={{4,0},{8,4},{12,8},{16,12},{20,16},{24,20},{28,24},{5,1},{9,5},{13... | collective-permute-start | bytes 393224 | tf_op jit(solution)/shard_map/ppermute | solution.py:35
  105.3 12.9 %collective-permute-start.12 = (bf16[512,256]{1,0:T(8,128)(2,1)S(1)}, bf16[512,256]{1,0:T(8,128)(2,1)S(1)}, u32[]{:S(2)}, u32[]{:S(2)}) collective-permute-start(bf16[512,256]{1,0:T(8,128)(2,1)S(1)} %get-tuple-element.72), channel_id=1, source_target_pairs={{0,4},{4,8},{8,12},{12,16},{16,20},{20,24},{24,28},{1,5},{5,9},{9,... | collective-permute-start | bytes 786440 | tf_op jit(solution)/shard_map/ppermute | solution.py:35
  108.7 16.1 %collective-permute-start.9 = (bf16[512,256]{1,0:T(8,128)(2,1)S(1)}, bf16[512,256]{1,0:T(8,128)(2,1)S(1)}, u32[]{:S(2)}, u32[]{:S(2)}) collective-permute-start(bf16[512,256]{1,0:T(8,128)(2,1)S(1)} %get-tuple-element.69), channel_id=1, source_target_pairs={{4,0},{8,4},{12,8},{16,12},{20,16},{24,20},{28,24},{5,1},{9,5},{13... | collective-permute-start | bytes 786440 | tf_op jit(solution)/shard_map/ppermute | solution.py:35
  111.5 6.7 %collective-permute-start.13 = (bf16[512,128]{1,0:T(8,128)(2,1)S(1)}, bf16[512,128]{1,0:T(8,128)(2,1)S(1)}, u32[]{:S(2)}, u32[]{:S(2)}) collective-permute-start(bf16[512,128]{1,0:T(8,128)(2,1)S(1)} %get-tuple-element.73), channel_id=1, source_target_pairs={{0,4},{4,8},{8,12},{12,16},{16,20},{20,24},{24,28},{1,5},{5,9},{9,... | collective-permute-start | bytes 393224 | tf_op jit(solution)/shard_map/ppermute | solution.py:35
  136.9 1.3 copy-start.11

commit v2 on v1

--- a/solution.py
+++ b/solution.py
@@ -21,6 +21,7 @@
 
 VMEM = pl.BlockSpec(memory_space=pltpu.VMEM)
 SMEM = pl.BlockSpec(memory_space=pltpu.SMEM)
+HBM = pl.BlockSpec(memory_space=pltpu.HBM)
 F32 = jnp.float32
 BF16 = jnp.bfloat16
 
@@ -61,17 +62,13 @@
     position_ref,
     tile_at_slot,
     key_tiles,
-    q_ref,
-    k_ref,
-    qt_ref,
-    kt_ref,
     v_ref,
     vt_ref,
     plan_ref,
     up_ref,
     down_ref,
-    sums_ref,
     slot_of,
+    copy_sem,
 ):
     position = position_ref[0]
 
@@ -111,11 +108,25 @@
         low = jnp.where(slot == (position - 1) * tiles_here + from_below, 0, 1)
         high = jnp.where(slot == (position + 1) * tiles_here + from_above, 2, 3)
         plan_ref[4 + index] = jnp.where(slot < position * tiles_here, low, high)
+    copies = []
     for order, packet in ((up_order, up_ref), (down_order, down_ref)):
         for rank in range(NEED):
             source = pl.ds(pl.multiple_of(order[rank] * TILE, TILE), TILE)
-            packet[rank * TILE : (rank + 1) * TILE, :] = v_ref[source, :]
-            packet[PACK + rank * TILE : PACK + (rank + 1) * TILE, :] = vt_ref[source, :]
+            for base, array_ref in ((0, v_ref), (PACK, vt_ref)):
+                copies.append(
+                    pltpu.make_async_copy(
+                        array_ref.at[source, :],
+                        packet.at[pl.ds(base + rank * TILE, TILE), :],
+                        copy_sem.at[len(copies)],
+                    )
+                )
+    for copy in copies:
+        copy.start()
+    for copy in copies:
+        copy.wait()
+
+
+def sums_kernel(q_ref, k_ref, qt_ref, kt_ref, sums_ref):
     columns = []
     for raw_ref, moving_ref in ((q_ref, qt_ref), (k_ref, kt_ref)):
         raw = raw_ref[...].astype(F32)
@@ -123,6 +134,57 @@
         columns.append(jnp.sum(raw * raw, axis=1, keepdims=True))
         columns.append(jnp.sum(raw * moving, axis=1, keepdims=True))
     sums_ref[...] = to_rows(columns)
+
+
+def exchange_kernel(count, part_ref, total_ref, arrived, send_sem, recv_sem):
+    me = lax.axis_index("head")
+    barrier = pltpu.get_barrier_semaphore()
+    for step in range(1, count):
+        pl.semaphore_signal(
+            barrier,
+            inc=1,
+            device_id={"head": lax.rem(me + step, count)},
+            device_id_type=pl.DeviceIdType.MESH,
+        )
+    pl.semaphore_wait(barrier, count - 1)
+    copies = [
+        pltpu.make_async_remote_copy(
+            src_ref=part_ref,
+            dst_ref=arrived.at[step - 1],
+            send_sem=send_sem.at[step - 1],
+            recv_sem=recv_sem.at[step - 1],
+            device_id={"head": lax.rem(me + step, count)},
+            device_id_type=pl.DeviceIdType.MESH,
+        )
+        for step in range(1, count)
+    ]
+    for copy in copies:
+        copy.start()
+    for copy in copies:
+        copy.wait()
+    total = part_ref[...]
+    for step in range(1, count):
+        total += arrived[step - 1]
+    total_ref[...] = total
+
+
+def head_total(part, collective_id):
+    count = lax.axis_size("head")
+    return pl.pallas_call(
+        functools.partial(exchange_kernel, count),
+        out_shape=jax.ShapeDtypeStruct(part.shape, F32),
+        in_specs=[VMEM],
+        out_specs=VMEM,
+        scratch_shapes=[
+            pltpu.VMEM((count - 1,) + part.shape, F32),
+            pltpu.SemaphoreType.DMA((count - 1,)),
+            pltpu.SemaphoreType.DMA((count - 1,)),
+        ],
+        compiler_params=pltpu.CompilerParams(
+            collective_id=collective_id, has_side_effects=True
+        ),
+        name="exchange",
+    )(part)
 
 
 def norm_kernel(
@@ -322,23 +384,33 @@
     k_gain = k_gain.reshape(1, width)
     struct = jax.ShapeDtypeStruct
 
-    plan, v_up, v_down, sums = pl.pallas_call(
+    plan, v_up, v_down = pl.pallas_call(
         functools.partial(prepare_kernel, devices, tiles_here),
         out_shape=[
             struct((16,), jnp.int32),
             struct((2 * PACK, width), BF16),
             struct((2 * PACK, width), BF16),
-            struct((8, rows), F32),
         ],
-        in_specs=[SMEM] * 3 + [VMEM] * 6,
-        out_specs=[SMEM] + [VMEM] * 3,
-        scratch_shapes=[pltpu.SMEM((devices * tiles_here,), jnp.int32)],
+        in_specs=[SMEM] * 3 + [HBM] * 2,
+        out_specs=[SMEM] + [HBM] * 2,
+        scratch_shapes=[
+            pltpu.SMEM((devices * tiles_here,), jnp.int32),
+            pltpu.SemaphoreType.DMA((4 * NEED,)),
+        ],
         compiler_params=params(),
         name="prepare",
-    )(position, tile_at_slot, key_tiles, q_raw, k_raw, q_tangent, k_tangent, values, v_tangent)
+    )(position, tile_at_slot, key_tiles, values, v_tangent)
     v_below = shifted(v_up, "seq", 1)
     v_above = shifted(v_down, "seq", -1)
-    totals = lax.psum(sums, "head")
+    sums = pl.pallas_call(
+        sums_kernel,
+        out_shape=struct((8, rows), F32),
+        in_specs=[VMEM] * 4,
+        out_specs=VMEM,
+        compiler_params=params(),
+        name="sums",
+    )(q_raw, k_raw, q_tangent, k_tangent)
+    totals = head_total(sums, 0)
     packet_shapes = [
         struct((2 * PACK, size * HEAD_DIM), BF16) for _, size in bounds for _ in range(2)
     ]
@@ -415,7 +487,7 @@
         compiler_params=params(),
         name="merge",
     )(plan, q_raw, k_raw, q_gain, k_gain, *query_grads, *locals_, *from_above, *from_below)
-    back = lax.psum(back_sums, "head")
+    back = head_total(back_sums, 1)
     grad_q, grad_k = pl.pallas_call(
         functools.partial(final_kernel, bounds),
         out_shape=[struct((rows, width), BF16)] * 2,

time: 142 us -> 135 us (0.951)
  blocking collectives: 20.3 us -> 0 us
  Pallas kernels: 38.2 us -> 51.5 us
    psum x2 -> x0, blocking collectives: 20.3 us -> none  [the longest x1 10.8 us: per_device(): totals = lax.psum(sums, 'head')]
    pallas_call x0 -> x3, Pallas kernels: none -> 12 us  [the longest x2 11.4 us: head_total(): pl.pallas_call(functools.partial(exchange_kernel, count), out_shape=jax.S...]
    unnamed x35 -> x39, local copies, waits for them, and re-layouts: 9.3 us -> 9.86 us
  transfers between devices with their start and end apart: 14 -> 14, of which waited for: 4 -> 4; matrix products, arithmetic and copies ran while one was open for 1% -> 1% of each run, Pallas kernels for 22% -> 28%
where the time goes in v2:
time: 135 us; the launch traced here: 134 us
  starting transfers between devices  53.8 us (40%)
  Pallas kernels  51.5 us (38%)
  waiting for transfers between devices  16.4 us (12%)
  local copies, waits for them, and re-layouts  9.87 us (7%)
    ppermute x14, starting transfers between devices, shifted(): lax.ppermute(value, axis, [(source, source + steps) for source in range(l...  53.8 us
    pallas_call x3, Pallas kernels, per_device(): pl.pallas_call(functools.partial(attend_kernel, tiles_here), grid_spec=pl...  28.8 us
    ppermute x14, waiting for transfers between devices, shifted(): lax.ppermute(value, axis, [(source, source + steps) for source in range(l...  16.4 us
    pallas_call x2, Pallas kernels, head_total(): pl.pallas_call(functools.partial(exchange_kernel, count), out_shape=jax.S...  11.4 us
    unnamed x39, local copies, waits for them, and re-layouts  9.86 us
    pallas_call x1, Pallas kernels, per_device(): pl.pallas_call(functools.partial(prepare_kernel, devices, tiles_here), ou...  3.96 us
  transfers between devices with their start and end apart: 14, of which 4 were waited for; matrix products, arithmetic and copies ran while one was open for 1% of the time, Pallas kernels for 28%

profile of v2, /device:TPU:25, one launch (start us, length us, event | category | flops | bytes accessed | tf_op | source)
XLA Modules:
  0.0 133.8 jit_solution(10296742393557613132)
XLA Ops:
  0.7 0.9 copy.16.key_tiles
  1.5 1.1 copy-done.2
  2.6 1.1 copy-done.4
  3.7 0.7 copy-done.16
  4.4 4.0 %prepare.1 = (s32[16]{0:T(128)S(1)}, bf16[512,640]{1,0:T(8,128)(2,1)S(1)}, bf16[512,640]{1,0:T(8,128)(2,1)S(1)}) custom-call(s32[1]{0:T(128)} %bitcast.position_ref, s32[32]{0:T(128)S(1)} %copy-done.16, s32[32,6]{1,0:T(8,128)S(1)} %copy.16.key_tiles, bf16[512,640]{1,0:T(8,128)(2,1)S(1)} %copy-done.2, bf16[512,640]{1,0:T(8,128)(2,1)S(1)} %copy-done.4), custom_call_target="tpu_custom_call" | custom-call | tf_op jit(solution)/shard_map/prepare/pallas_call | solution.py:387
  8.3 3.1 %collective-permute-start.2 = (bf16[512,640]{1,0:T(8,128)(2,1)S(1)}, bf16[512,640]{1,0:T(8,128)(2,1)}, u32[]{:S(2)}, u32[]{:S(2)}) collective-permute-start(bf16[512,640]{1,0:T(8,128)(2,1)S(1)} %get-tuple-element.48), channel_id=1, source_target_pairs={{0,4},{4,8},{8,12},{12,16},{16,20},{20,24},{24,28},{1,5},{5,9},{9,... | collective-permute-start | bytes 1966088 | tf_op jit(solution)/shard_map/ppermute | solution.py:36
  11.5 3.1 %collective-permute-start.3 = (bf16[512,640]{1,0:T(8,128)(2,1)S(1)}, bf16[512,640]{1,0:T(8,128)(2,1)}, u32[]{:S(2)}, u32[]{:S(2)}) collective-permute-start(bf16[512,640]{1,0:T(8,128)(2,1)S(1)} %get-tuple-element.49), channel_id=1, source_target_pairs={{4,0},{8,4},{12,8},{16,12},{20,16},{24,20},{28,24},{5,1},{9,5},{13... | collective-permute-start | bytes 1966088 | tf_op jit(solution)/shard_map/ppermute | solution.py:36
  14.6 0.0 copy-start.6
  14.6 1.1 copy-done.6
  15.7 1.1 copy-done.8
  16.8 0.6 sums.1.part_ref
  17.4 0.6 copy-done.14
  18.0 6.2 %exchange.2.totals_ref = f32[8,512]{1,0:T(8,128)} custom-call(f32[8,512]{1,0:T(8,128)} %copy-done.14), custom_call_target="tpu_custom_call" | custom-call | tf_op jit(solution)/shard_map/exchange/pallas_call | solution.py:173
  24.2 0.7 copy-done.11
  25.0 2.4 %norm.1 = (bf16[512,640]{1,0:T(8,128)(2,1)S(1)}, bf16[512,640]{1,0:T(8,128)(2,1)S(1)}, bf16[512,640]{1,0:T(8,128)(2,1)S(1)}, bf16[512,640]{1,0:T(8,128)(2,1)S(1)...) custom-call(s32[16]{0:T(128)S(1)} %get-tuple-element.41.plan, ...), custom_call_target="tpu_custom_call" | custom-call | tf_op jit(solution)/shard_map/norm/pallas_call | solution.py:417
  27.4 3.0 %collective-permute-start = (bf16[512,256]{1,0:T(8,128)(2,1)S(1)}, bf16[512,256]{1,0:T(8,128)(2,1)S(1)}, u32[]{:S(2)}, u32[]{:S(2)}) collective-permute-start(bf16[512,256]{1,0:T(8,128)(2,1)S(1)} %get-tuple-element.46), channel_id=1, source_target_pairs={{0,4},{4,8},{8,12},{12,16},{16,20},{20,24},{24,28},{1,5},{5,9},{9,... | collective-permute-start | bytes 786440 | tf_op jit(solution)/shard_map/ppermute | solution.py:36
  30.4 3.1 %collective-permute-start.1 = (bf16[512,256]{1,0:T(8,128)(2,1)S(1)}, bf16[512,256]{1,0:T(8,128)(2,1)S(1)}, u32[]{:S(2)}, u32[]{:S(2)}) collective-permute-start(bf16[512,256]{1,0:T(8,128)(2,1)S(1)} %get-tuple-element.47), channel_id=1, source_target_pairs={{4,0},{8,4},{12,8},{16,12},{20,16},{24,20},{28,24},{5,1},{9,5},{13... | collective-permute-start | bytes 786440 | tf_op jit(solution)/shard_map/ppermute | solution.py:36
  33.5 2.2 %collective-permute-start.4 = (bf16[512,256]{1,0:T(8,128)(2,1)S(1)}, bf16[512,256]{1,0:T(8,128)(2,1)S(1)}, u32[]{:S(2)}, u32[]{:S(2)}) collective-permute-start(bf16[512,256]{1,0:T(8,128)(2,1)S(1)} %get-tuple-element.51), channel_id=1, source_target_pairs={{0,4},{4,8},{8,12},{12,16},{16,20},{20,24},{24,28},{1,5},{5,9},{9,... | collective-permute-start | bytes 786440 | tf_op jit(solution)/shard_map/ppermute | solution.py:36
  35.7 2.2 %collective-permute-done.kb_ref = bf16[512,256]{1,0:T(8,128)(2,1)S(1)} collective-permute-done((bf16[512,256]{1,0:T(8,128)(2,1)S(1)}, bf16[512,256]{1,0:T(8,128)(2,1)S(1)}, u32[]{:S(2)}, u32[]{:S(2)}) %collective-permute-start) | collective-permute-done | bytes 262176 | tf_op jit(solution)/shard_map/ppermute | solution.py:36
  38.0 16.1 %collective-permute-start.5 = (bf16[512,256]{1,0:T(8,128)(2,1)S(1)}, bf16[512,256]{1,0:T(8,128)(2,1)S(1)}, u32[]{:S(2)}, u32[]{:S(2)}) collective-permute-start(bf16[512,256]{1,0:T(8,128)(2,1)S(1)} %get-tuple-element.52), channel_id=1, source_target_pairs={{4,0},{8,4},{12,8},{16,12},{20,16},{24,20},{28,24},{5,1},{9,5},{13... | collective-permute-start | bytes 786440 | tf_op jit(solution)/shard_map/ppermute | solution.py:36
  54.1 4.6 %collective-permute-done.1.ka_ref = bf16[512,256]{1,0:T(8,128)(2,1)S(1)} collective-permute-done((bf16[512,256]{1,0:T(8,128)(2,1)S(1)}, bf16[512,256]{1,0:T(8,128)(2,1)S(1)}, u32[]{:S(2)}, u32[]{:S(2)}) %collective-permute-start.1) | collective-permute-done | bytes 262176 | tf_op jit(solution)/shard_map/ppermute | solution.py:36
  58.7 1.9 %collective-permute-start.6 = (bf16[512,128]{1,0:T(8,128)(2,1)S(1)}, bf16[512,128]{1,0:T(8,128)(2,1)S(1)}, u32[]{:S(2)}, u32[]{:S(2)}) collective-permute-start(bf16[512,128]{1,0:T(8,128)(2,1)S(1)} %get-tuple-element.54), channel_id=1, source_target_pairs={{0,4},{4,8},{8,12},{12,16},{16,20},{20,24},{24,28},{1,5},{5,9},{9,... | collective-permute-start | bytes 393224 | tf_op jit(solution)/shard_map/ppermute | solution.py:36
  60.6 0.0 collective-permute-done.2.vb_ref
  60.6 4.3 %collective-permute-start.7 = (bf16[512,128]{1,0:T(8,128)(2,1)S(1)}, bf16[512,128]{1,0:T(8,128)(2,1)S(1)}, u32[]{:S(2)}, u32[]{:S(2)}) collective-permute-start(bf16[512,128]{1,0:T(8,128)(2,1)S(1)} %get-tuple-element.55), channel_id=1, source_target_pairs={{4,0},{8,4},{12,8},{16,12},{20,16},{24,20},{28,24},{5,1},{9,5},{13... | collective-permute-start | bytes 393224 | tf_op jit(solution)/shard_map/ppermute | solution.py:36
  64.9 0.0 collective-permute-done.3.va_ref
  64.9 0.0 copy-start.3
  64.9 0.0 copy-start.5
  64.9 11.3 %attend.3 = (bf16[512,256]{1,0:T(8,128)(2,1)S(1)}, bf16[512,256]{1,0:T(8,128)(2,1)S(1)}, f32[512,256]{1,0:T(8,128)S(1)}, bf16[1024,256]{1,0:T(8,128)(2,1)S(1)}, ...) custom-call(s32[16]{0:T(128)S(1)} %get-tuple-element.41.plan, bf16[512,640]{1,0:T(8,128)(2,1)S(1)} %get-tuple-element.42.q_ref, ...), custom_call_target="tpu_custom_call" | custom-call | flops 2013265920 | bytes 3145728 | tf_op jit(solution)/shard_map/attend/pallas_call | solution.py:438
  76.2 1.9 %collective-permute-start.11 = (bf16[512,256]{1,0:T(8,128)(2,1)S(1)}, bf16[512,256]{1,0:T(8,128)(2,1)S(1)}, u32[]{:S(2)}, u32[]{:S(2)}) collective-permute-start(bf16[512,256]{1,0:T(8,128)(2,1)S(1)} %get-tuple-element.69), channel_id=1, source_target_pairs={{0,4},{4,8},{8,12},{12,16},{16,20},{20,24},{24,28},{1,5},{5,9},{9,... | collective-permute-start | bytes 786440 | tf_op jit(solution)/shard_map/ppermute | solution.py:36
  78.2 4.3 %collective-permute-start.8 = (bf16[512,256]{1,0:T(8,128)(2,1)S(1)}, bf16[512,256]{1,0:T(8,128)(2,1)S(1)}, u32[]{:S(2)}, u32[]{:S(2)}) collective-permute-start(bf16[512,256]{1,0:T(8,128)(2,1)S(1)} %get-tuple-element.66), channel_id=1, source_target_pairs={{4,0},{8,4},{12,8},{16,12},{20,16},{24,20},{28,24},{5,1},{9,5},{13... | collective-permute-start | bytes 786440 | tf_op jit(solution)/shard_map/ppermute | solution.py:36
  82.5 6.2 %attend.5 = (bf16[512,128]{1,0:T(8,128)(2,1)S(1)}, bf16[512,128]{1,0:T(8,128)(2,1)S(1)}, f32[512,128]{1,0:T(8,128)S(1)}, bf16[1024,128]{1,0:T(8,128)(2,1)S(1)}, ...) custom-call(s32[16]{0:T(128)S(1)} %get-tuple-element.41.plan, bf16[512,640]{1,0:T(8,128)(2,1)S(1)} %get-tuple-element.42.q_ref, ...), custom_call_target="tpu_custom_call" | custom-call | flops 1006632960 | bytes 1572864 | tf_op jit(solution)/shard_map/attend/pallas_call | solution.py:438
  88.7 2.1 %collective-permute-start.10 = (bf16[512,128]{1,0:T(8,128)(2,1)S(1)}, bf16[512,128]{1,0:T(8,128)(2,1)S(1)}, u32[]{:S(2)}, u32[]{:S(2)}) collective-permute-start(bf16[512,128]{1,0:T(8,128)(2,1)S(1)} %get-tuple-element.68), channel_id=1, source_target_pairs={{4,0},{8,4},{12,8},{16,12},{20,16},{24,20},{28,24},{5,1},{9,5},{13... | collective-permute-start | bytes 393224 | tf_op jit(solution)/shard_map/ppermute | solution.py:36
  90.8 0.0 collective-permute-done.4.kb_ref
  90.8 0.0 collective-permute-done.5.ka_ref
  90.8 11.3 %attend.4 = (bf16[512,256]{1,0:T(8,128)(2,1)S(1)}, bf16[512,256]{1,0:T(8,128)(2,1)S(1)}, f32[512,256]{1,0:T(8,128)S(1)}, bf16[1024,256]{1,0:T(8,128)(2,1)S(1)}, ...) custom-call(s32[16]{0:T(128)S(1)} %get-tuple-element.41.plan, bf16[512,640]{1,0:T(8,128)(2,1)S(1)} %get-tuple-element.42.q_ref, ...), custom_call_target="tpu_custom_call" | custom-call | flops 2013265920 | bytes 3145728 | tf_op jit(solution)/shard_map/attend/pallas_call | solution.py:438
  102.1 3.4 %collective-permute-start.12 = (bf16[512,256]{1,0:T(8,128)(2,1)S(1)}, bf16[512,256]{1,0:T(8,128)(2,1)S(1)}, u32[]{:S(2)}, u32[]{:S(2)}) collective-permute-start(bf16[512,256]{1,0:T(8,128)(2,1)S(1)} %get-tuple-element.70), channel_id=1, source_target_pairs={{0,4},{4,8},{8,12},{12,16},{16,20},{20,24},{24,28},{1,5},{5,9},{9,... | collective-permute-start | bytes 786440 | tf_op jit(solution)/shard_map/ppermute | solution.py:36
  105.5 2.8 %collective-permute-start.9 = (bf16[512,256]{1,0:T(8,128)(2,1)S(1)}, bf16[512,256]{1,0:T(8,128)(2,1)S(1)}, u32[]{:S(2)}, u32[]{:S(2)}) collective-permute-start(bf16[512,256]{1,0:T(8,128)(2,1)S(1)} %get-tuple-element.67), channel_id=1, source_target_pairs={{4,0},{8,4},{12,8},{16,12},{20,16},{24,20},{28,24},{5,1},{9,5},{13... | collective-permute-start | bytes 786440 | tf_op jit(solution)/shard_map/ppermute | solution.py:36
  108.3 2.5 %collective-permute-start.13 = (bf16[512,128]{1,0:T(8,128)(2,1)S(1)}, bf16[512,128]{1,0:T(8,128)(2,1)S(1)}, u32[]{:S(2)}, u32[]{:S(2)}) collective-permute-start(bf16[512,128]{1,0:T(8,128)(2,1)S(1)} %get-tuple-element.71), channel_id=1, source_target_pairs={{0,4},{4,8},{8,12},{12,16},{16,20},{20,24},{24,28},{1,5},{5,9},{9,... | collective-permute-start | bytes 393224 | tf_op jit(solution)/shard_map/ppermute | solution.py:36
  110.8 1.2 pad_maximum_fusion
  112.0 3.1 %collective-permute-done.13.refs_11_ = bf16[512,128]{1,0:T(8,128)(2,1)S(1)} collective-permute-done((bf16[512,128]{1,0:T(8,128)(2,1)S(1)}, bf16[512,128]{1,0:T(8,128)(2,1)S(1)}, u32[]{:S(2)}, u32[]{:S(2)}) %collective-permute-start.13) | collective-permute-done | bytes 131104 | tf_op jit(solution)/shard_map/ppermute | solution.py:36
  115.0 0.0 collective-permute-done.11.refs_9_
  115.1 6.5 %collective-permute-done.9.refs_7_ = bf16[512,256]{1,0:T(8,128)(2,1)S(1)} collective-permute-done((bf16[512,256]{1,0:T(8,128)(2,1)S(1)}, bf16[512,256]{1,0:T(8,128)(2,1)S(1)}, u32[]{:S(2)}, u32[]{:S(2)}) %collective-permute-start.9) | collective-permute-done | bytes 262176 | tf_op jit(solution)/shard_map/ppermute | solution.py:36
  121.6 2.6 %merge.1 = (bf16[512,640]{1,0:T(8,128)(2,1)}, f32[512,640]{1,0:T(8,128)}, f32[8,512]{1,0:T(8,128)S(1)}) custom-call(s32[16]{0:T(128)S(1)} %get-tuple-element.41.plan, bf16[512,640]{1,0:T(8,128)(2,1)S(1)} %copy-done, bf16[512,640]{1,0:T(8,128)(2,1)S(1)} %copy-done.1, f32[1,640]{1,0:T(1,128)S(1)} %reshape.20.q_gain_ref, f32[1,640]{1,0:T(1,128)S(1)} %reshape.21.k_gain_ref, ...), custom_call_target="tpu_custom_call" | custom-call | tf_op jit(solution)/shard_map/merge/pallas_call | solution.py:479
  124.2 0.6 copy-done.15
  124.8 5.2 %exchange.3.back_ref = f32[8,512]{1,0:T(8,128)} custom-call(f32[8,512]{1,0:T(8,128)} %copy-done.15), custom_call_target="tpu_custom_call" | custom-call | tf_op jit(solution)/shard_map/exchange/pallas_call | solution.py:173
  130.0 1.3 copy-done.9
  131.3 0.7 copy-done.13
  132.0 1.7 %final.1 = (bf16[512,640]{1,0:T(8,128)(2,1)}, bf16[512,640]{1,0:T(8,128)(2,1)}) custom-call(f32[8,512]{1,0:T(8,128)S(1)} %copy-done.12, f32[8,512]{1,0:T(8,128)S(1)} %copy-done.13, bf16[512,640]{1,0:T(8,128)(2,1)S(1)} %copy-done, bf16[512,640]{1,0:T(8,128)(2,1)S(1)} %copy-done.1, f32[1,640]{1,0:T(1,128)S(1)} %reshape.20.q_gain_ref, ...), custom_call_target="tpu_custom_call" | custom-call | tf_op jit(solution)/shard_map/final/pallas_call | solution.py:491
  (32 shorter events, 0.1 us)
Async XLA Ops:
  0.6 13.9 %copy-start = (bf16[512,640]{1,0:T(8,128)(2,1)S(1)}, bf16[512,640]{1,0:T(8,128)(2,1)}, u32[]{:S(2)}) copy-start(bf16[512,640]{1,0:T(8,128)(2,1)} %q_ref.7) | copy-start | bytes 1966084
  0.6 13.9 %copy-start.1 = (bf16[512,640]{1,0:T(8,128)(2,1)S(1)}, bf16[512,640]{1,0:T(8,128)(2,1)}, u32[]{:S(2)}) copy-start(bf16[512,640]{1,0:T(8,128)(2,1)} %k_ref.7) | copy-start | bytes 1966084
  1.5 1.1 copy-start.2
  2.6 1.1 copy-start.4
  3.7 0.7 copy-start.16
  4.4 10.2 %copy-start.17 = (f32[640]{0:T(1024)S(1)}, f32[640]{0:T(1024)}, u32[]{:S(2)}) copy-start(f32[640]{0:T(1024)} %param.18) | copy-start | bytes 7684
  4.4 10.2 %copy-start.18 = (f32[640]{0:T(1024)S(1)}, f32[640]{0:T(1024)}, u32[]{:S(2)}) copy-start(f32[640]{0:T(1024)} %param.19) | copy-start | bytes 7684
  8.3 52.3 %collective-permute-start.2 = (bf16[512,640]{1,0:T(8,128)(2,1)S(1)}, bf16[512,640]{1,0:T(8,128)(2,1)}, u32[]{:S(2)}, u32[]{:S(2)}) collective-permute-start(bf16[512,640]{1,0:T(8,128)(2,1)S(1)} %get-tuple-element.48), channel_id=1, source_target_pairs={{0,4},{4,8},{8,12},{12,16},{16,20},{20,24},{24,28},{1,5},{5,9},{9,... | collective-permute-start | bytes 1966088 | tf_op jit(solution)/shard_map/ppermute | solution.py:36
  11.5 53.4 %collective-permute-start.3 = (bf16[512,640]{1,0:T(8,128)(2,1)S(1)}, bf16[512,640]{1,0:T(8,128)(2,1)}, u32[]{:S(2)}, u32[]{:S(2)}) collective-permute-start(bf16[512,640]{1,0:T(8,128)(2,1)S(1)} %get-tuple-element.49), channel_id=1, source_target_pairs={{4,0},{8,4},{12,8},{16,12},{20,16},{24,20},{28,24},{5,1},{9,5},{13... | collective-permute-start | bytes 1966088 | tf_op jit(solution)/shard_map/ppermute | solution.py:36
  14.6 1.1 copy-start.6
  15.7 1.1 copy-start.8
  16.8 7.5 %copy-start.7 = (bf16[512,640]{1,0:T(8,128)(2,1)S(1)}, bf16[512,640]{1,0:T(8,128)(2,1)}, u32[]{:S(2)}) copy-start(bf16[512,640]{1,0:T(8,128)(2,1)} %qt_ref.3) | copy-start | bytes 1966084
  17.4 0.6 copy-start.14
  24.2 0.7 copy-start.11
  25.0 39.9 %copy-start.10 = (bf16[512,640]{1,0:T(8,128)(2,1)S(1)}, bf16[512,640]{1,0:T(8,128)(2,1)}, u32[]{:S(2)}) copy-start(bf16[512,640]{1,0:T(8,128)(2,1)} %co_ref.5) | copy-start | bytes 1966084
  27.4 10.6 %collective-permute-start = (bf16[512,256]{1,0:T(8,128)(2,1)S(1)}, bf16[512,256]{1,0:T(8,128)(2,1)S(1)}, u32[]{:S(2)}, u32[]{:S(2)}) collective-permute-start(bf16[512,256]{1,0:T(8,128)(2,1)S(1)} %get-tuple-element.46), channel_id=1, source_target_pairs={{0,4},{4,8},{8,12},{12,16},{16,20},{20,24},{24,28},{1,5},{5,9},{9,... | collective-permute-start | bytes 786440 | tf_op jit(solution)/shard_map/ppermute | solution.py:36
  30.4 28.3 %collective-permute-start.1 = (bf16[512,256]{1,0:T(8,128)(2,1)S(1)}, bf16[512,256]{1,0:T(8,128)(2,1)S(1)}, u32[]{:S(2)}, u32[]{:S(2)}) collective-permute-start(bf16[512,256]{1,0:T(8,128)(2,1)S(1)} %get-tuple-element.47), channel_id=1, source_target_pairs={{4,0},{8,4},{12,8},{16,12},{20,16},{24,20},{28,24},{5,1},{9,5},{13... | collective-permute-start | bytes 786440 | tf_op jit(solution)/shard_map/ppermute | solution.py:36
  33.5 57.2 %collective-permute-start.4 = (bf16[512,256]{1,0:T(8,128)(2,1)S(1)}, bf16[512,256]{1,0:T(8,128)(2,1)S(1)}, u32[]{:S(2)}, u32[]{:S(2)}) collective-permute-start(bf16[512,256]{1,0:T(8,128)(2,1)S(1)} %get-tuple-element.51), channel_id=1, source_target_pairs={{0,4},{4,8},{8,12},{12,16},{16,20},{20,24},{24,28},{1,5},{5,9},{9,... | collective-permute-start | bytes 786440 | tf_op jit(solution)/shard_map/ppermute | solution.py:36
  38.0 52.8 %collective-permute-start.5 = (bf16[512,256]{1,0:T(8,128)(2,1)S(1)}, bf16[512,256]{1,0:T(8,128)(2,1)S(1)}, u32[]{:S(2)}, u32[]{:S(2)}) collective-permute-start(bf16[512,256]{1,0:T(8,128)(2,1)S(1)} %get-tuple-element.52), channel_id=1, source_target_pairs={{4,0},{8,4},{12,8},{16,12},{20,16},{24,20},{28,24},{5,1},{9,5},{13... | collective-permute-start | bytes 786440 | tf_op jit(solution)/shard_map/ppermute | solution.py:36
  58.7 19.5 %collective-permute-start.6 = (bf16[512,128]{1,0:T(8,128)(2,1)S(1)}, bf16[512,128]{1,0:T(8,128)(2,1)S(1)}, u32[]{:S(2)}, u32[]{:S(2)}) collective-permute-start(bf16[512,128]{1,0:T(8,128)(2,1)S(1)} %get-tuple-element.54), channel_id=1, source_target_pairs={{0,4},{4,8},{8,12},{12,16},{16,20},{20,24},{24,28},{1,5},{5,9},{9,... | collective-permute-start | bytes 393224 | tf_op jit(solution)/shard_map/ppermute | solution.py:36
  60.6 21.8 %collective-permute-start.7 = (bf16[512,128]{1,0:T(8,128)(2,1)S(1)}, bf16[512,128]{1,0:T(8,128)(2,1)S(1)}, u32[]{:S(2)}, u32[]{:S(2)}) collective-permute-start(bf16[512,128]{1,0:T(8,128)(2,1)S(1)} %get-tuple-element.55), channel_id=1, source_target_pairs={{4,0},{8,4},{12,8},{16,12},{20,16},{24,20},{28,24},{5,1},{9,5},{13... | collective-permute-start | bytes 393224 | tf_op jit(solution)/shard_map/ppermute | solution.py:36
  64.9 17.5 %copy-start.3 = (bf16[512,640]{1,0:T(8,128)(2,1)S(1)}, bf16[512,640]{1,0:T(8,128)(2,1)}, u32[]{:S(2)}) copy-start(bf16[512,640]{1,0:T(8,128)(2,1)} %v_ref.7) | copy-start | bytes 1966084
  64.9 17.5 %copy-start.5 = (bf16[512,640]{1,0:T(8,128)(2,1)S(1)}, bf16[512,640]{1,0:T(8,128)(2,1)}, u32[]{:S(2)}) copy-start(bf16[512,640]{1,0:T(8,128)(2,1)} %vt_ref.7) | copy-start | bytes 1966084
  76.2 38.8 %collective-permute-start.11 = (bf16[512,256]{1,0:T(8,128)(2,1)S(1)}, bf16[512,256]{1,0:T(8,128)(2,1)S(1)}, u32[]{:S(2)}, u32[]{:S(2)}) collective-permute-start(bf16[512,256]{1,0:T(8,128)(2,1)S(1)} %get-tuple-element.69), channel_id=1, source_target_pairs={{0,4},{4,8},{8,12},{12,16},{16,20},{20,24},{24,28},{1,5},{5,9},{9,... | collective-permute-start | bytes 786440 | tf_op jit(solution)/shard_map/ppermute | solution.py:36
  78.2 36.9 %collective-permute-start.8 = (bf16[512,256]{1,0:T(8,128)(2,1)S(1)}, bf16[512,256]{1,0:T(8,128)(2,1)S(1)}, u32[]{:S(2)}, u32[]{:S(2)}) collective-permute-start(bf16[512,256]{1,0:T(8,128)(2,1)S(1)} %get-tuple-element.66), channel_id=1, source_target_pairs={{4,0},{8,4},{12,8},{16,12},{20,16},{24,20},{28,24},{5,1},{9,5},{13... | collective-permute-start | bytes 786440 | tf_op jit(solution)/shard_map/ppermute | solution.py:36
  88.7 19.6 %collective-permute-start.10 = (bf16[512,128]{1,0:T(8,128)(2,1)S(1)}, bf16[512,128]{1,0:T(8,128)(2,1)S(1)}, u32[]{:S(2)}, u32[]{:S(2)}) collective-permute-start(bf16[512,128]{1,0:T(8,128)(2,1)S(1)} %get-tuple-element.68), channel_id=1, source_target_pairs={{4,0},{8,4},{12,8},{16,12},{20,16},{24,20},{28,24},{5,1},{9,5},{13... | collective-permute-start | bytes 393224 | tf_op jit(solution)/shard_map/ppermute | solution.py:36
  102.1 12.9 %collective-permute-start.12 = (bf16[512,256]{1,0:T(8,128)(2,1)S(1)}, bf16[512,256]{1,0:T(8,128)(2,1)S(1)}, u32[]{:S(2)}, u32[]{:S(2)}) collective-permute-start(bf16[512,256]{1,0:T(8,128)(2,1)S(1)} %get-tuple-element.70), channel_id=1, source_target_pairs={{0,4},{4,8},{8,12},{12,16},{16,20},{20,24},{24,28},{1,5},{5,9},{9,... | collective-permute-start | bytes 786440 | tf_op jit(solution)/shard_map/ppermute | solution.py:36
  105.5 16.1 %collective-permute-start.9 = (bf16[512,256]{1,0:T(8,128)(2,1)S(1)}, bf16[512,256]{1,0:T(8,128)(2,1)S(1)}, u32[]{:S(2)}, u32[]{:S(2)}) collective-permute-start(bf16[512,256]{1,0:T(8,128)(2,1)S(1)} %get-tuple-element.67), channel_id=1, source_target_pairs={{4,0},{8,4},{12,8},{16,12},{20,16},{24,20},{28,24},{5,1},{9,5},{13... | collective-permute-start | bytes 786440 | tf_op jit(solution)/shard_map/ppermute | solution.py:36
  108.3 6.7 %collective-permute-start.13 = (bf16[512,128]{1,0:T(8,128)(2,1)S(1)}, bf16[512,128]{1,0:T(8,128)(2,1)S(1)}, u32[]{:S(2)}, u32[]{:S(2)}) collective-permute-start(bf16[512,128]{1,0:T(8,128)(2,1)S(1)} %get-tuple-element.71), channel_id=1, source_target_pairs={{0,4},{4,8},{8,12},{12,16},{16,20},{20,24},{24,28},{1,5},{5,9},{9,... | collective-permute-start | bytes 393224 | tf_op jit(solution)/shard_map/ppermute | solution.py:36
  121.6 8.4 %copy-start.12 = (f32[8,512]{1,0:T(8,128)S(1)}, f32[8,512]{1,0:T(8,128)}, u32[]{:S(2)}) copy-start(f32[8,512]{1,0:T(8,128)} %exchange.2.totals_ref) | copy-start | bytes 49156
  124.2 0.6 copy-start.15
  130.0 1.3 copy-start.9
  131.3 0.7 copy-start.13

commit v3 on v2

--- a/solution.py
+++ b/solution.py
@@ -17,7 +17,7 @@
 SCALE = HEAD_DIM ** (-0.5)
 PACK = NEED * TILE
 VMEM_BYTES = 48 * 1024 * 1024
-CHUNKS = (2, 2, 1)
+CHUNKS = (3, 2)
 
 VMEM = pl.BlockSpec(memory_space=pltpu.VMEM)
 SMEM = pl.BlockSpec(memory_space=pltpu.SMEM)
@@ -255,7 +255,12 @@
     above_ref,
     remote,
     remote_sum,
-    local_sum,
+    prob_buf,
+    tangent_buf,
+    grad_buf,
+    probs_half,
+    prob_tangent,
+    score_grad,
 ):
     rows = tiles_here * TILE
     for base, kp_ref, vp_ref in ((0, kb_ref, vb_ref), (PACK, ka_ref, va_ref)):
@@ -264,47 +269,61 @@
         remote[base : base + PACK, 256:384] = vp_ref[:PACK, :]
         remote[base : base + PACK, 384:512] = vp_ref[PACK:, :]
     remote_sum[...] = jnp.zeros_like(remote_sum)
-    k_local = jnp.concatenate([k_ref[...], kt_ref[...]], axis=1)
-    v_local = jnp.concatenate([v_ref[...], vt_ref[...]], axis=1)
-    for tile in range(tiles_here):
-        here = slice(tile * TILE, (tile + 1) * TILE)
-        places = [
+    tiles = [slice(tile * TILE, (tile + 1) * TILE) for tile in range(tiles_here)]
+    places = [
+        [
             pl.ds(pl.multiple_of(plan[4 + tile * 2 + column] * TILE, TILE), TILE)
             for column in range(2)
         ]
-        keys = jnp.concatenate([k_local] + [remote[place, 0:256] for place in places], axis=0)
-        vals = jnp.concatenate([v_local] + [remote[place, 256:512] for place in places], axis=0)
-        query, moving, cotangent = q_ref[here, :], qt_ref[here, :], co_ref[here, :]
-        scores = dot(query, keys[:, :128], 1, 1)
+        for tile in range(tiles_here)
+    ]
+
+    def far(tile, start, stop):
+        return jnp.concatenate([remote[place, start:stop] for place in places[tile]], axis=0)
+
+    k_local = jnp.concatenate([k_ref[...], kt_ref[...]], axis=1)
+    v_local = jnp.concatenate([v_ref[...], vt_ref[...]], axis=1)
+    query, cotangent = q_ref[...], co_ref[...]
+    moving = jnp.concatenate([qt_ref[...], query], axis=1)
+    prob_buf[:, :rows] = dot(query, k_ref[...], 1, 1)
+    tangent_buf[:, :rows] = dot(moving, k_local, 1, 1)
+    grad_buf[:, :rows] = dot(cotangent, v_ref[...], 1, 1)
+    for tile, here in enumerate(tiles):
+        prob_buf[here, rows:] = dot(query[here], far(tile, 0, 128), 1, 1)
+        tangent_buf[here, rows:] = dot(moving[here], far(tile, 0, 256), 1, 1)
+        grad_buf[here, rows:] = dot(cotangent[here], far(tile, 256, 384), 1, 1)
+    for here in tiles:
+        scores = prob_buf[here, :]
         highest = jnp.max(scores, axis=1, keepdims=True)
         weights = jnp.exp((scores - highest) * SCALE)
         probs = weights * (1.0 / jnp.sum(weights, axis=1, keepdims=True))
-        probs_half = probs.astype(BF16)
-        both = dot(probs_half, vals, 1, 0)
-        output = both[:, :128].astype(BF16)
+        prob_buf[here, :] = probs
+        probs_half[here, :] = probs.astype(BF16)
+        score_tangent = tangent_buf[here, :] * SCALE
+        centre = jnp.sum(probs * score_tangent, axis=1, keepdims=True)
+        prob_tangent[here, :] = (probs * (score_tangent - centre)).astype(BF16)
+    both = dot(probs_half[:, :rows], v_local, 1, 0)
+    moved = dot(prob_tangent[:, :rows], v_ref[...], 1, 0)
+    for tile, here in enumerate(tiles):
+        pair = both[here] + dot(probs_half[here, rows:], far(tile, 256, 512), 1, 0)
+        output = pair[:, :128].astype(BF16)
         out_ref[here, :] = output
-        score_tangent = dot(jnp.concatenate([moving, query], axis=1), keys, 1, 1) * SCALE
-        centre = jnp.sum(probs * score_tangent, axis=1, keepdims=True)
-        prob_tangent = (probs * (score_tangent - centre)).astype(BF16)
-        ot_ref[here, :] = (dot(prob_tangent, vals[:, :128], 1, 0) + both[:, 128:]).astype(BF16)
-        prob_grad = dot(cotangent, vals[:, :128], 1, 1)
-        delta = jnp.sum(cotangent.astype(F32) * output.astype(F32), axis=1, keepdims=True)
-        score_grad = (probs * (prob_grad - delta)).astype(BF16)
-        qg_ref[here, :] = dot(score_grad, keys[:, :128], 1, 0) * SCALE
-        key_grad = dot(score_grad, query, 0, 0)
-        value_grad = dot(probs_half, cotangent, 0, 0)
-        if tile == 0:
-            local_sum[:, :128] = key_grad[:rows]
-            local_sum[:, 128:] = value_grad[:rows]
-        else:
-            local_sum[:, :128] += key_grad[:rows]
-            local_sum[:, 128:] += value_grad[:rows]
-        for column, place in enumerate(places):
-            piece = slice(rows + column * TILE, rows + (column + 1) * TILE)
+        ot_ref[here, :] = (
+            moved[here] + dot(prob_tangent[here, rows:], far(tile, 256, 384), 1, 0) + pair[:, 128:]
+        ).astype(BF16)
+        delta = jnp.sum(cotangent[here].astype(F32) * output.astype(F32), axis=1, keepdims=True)
+        score_grad[here, :] = (prob_buf[here, :] * (grad_buf[here, :] - delta)).astype(BF16)
+    near = dot(score_grad[:, :rows], k_ref[...], 1, 0)
+    for tile, here in enumerate(tiles):
+        qg_ref[here, :] = (near[here] + dot(score_grad[here, rows:], far(tile, 0, 128), 1, 0)) * SCALE
+        key_grad = dot(score_grad[here, rows:], query[here], 0, 0)
+        value_grad = dot(probs_half[here, rows:], cotangent[here], 0, 0)
+        for column, place in enumerate(places[tile]):
+            piece = slice(column * TILE, (column + 1) * TILE)
             remote_sum[place, :128] += key_grad[piece]
             remote_sum[place, 128:] += value_grad[piece]
-    local_ref[:rows, :] = (local_sum[:, :128] * SCALE).astype(BF16)
-    local_ref[rows:, :] = local_sum[:, 128:].astype(BF16)
+    local_ref[:rows, :] = (dot(score_grad[:, :rows], query, 0, 0) * SCALE).astype(BF16)
+    local_ref[rows:, :] = dot(probs_half[:, :rows], cotangent, 0, 0).astype(BF16)
     for base, part_ref in ((0, below_ref), (PACK, above_ref)):
         part_ref[:PACK, :] = (remote_sum[base : base + PACK, :128] * SCALE).astype(BF16)
         part_ref[PACK:, :] = remote_sum[base : base + PACK, 128:].astype(BF16)
@@ -449,8 +468,9 @@
                     scratch_shapes=[
                         pltpu.VMEM((2 * PACK, 4 * HEAD_DIM), BF16),
                         pltpu.VMEM((2 * PACK, 2 * HEAD_DIM), F32),
-                        pltpu.VMEM((rows, 2 * HEAD_DIM), F32),
-                    ],
+                    ]
+                    + [pltpu.VMEM((rows, KSEL * TILE), F32)] * 3
+                    + [pltpu.VMEM((rows, KSEL * TILE), BF16)] * 3,
                 ),
                 out_shape=[
                     struct((rows, size * HEAD_DIM), BF16),

time: 135 us -> 120 us (0.89)
  Pallas kernels: 51.5 us -> 41.2 us
  starting transfers between devices: 53.8 us -> 44.1 us
  waiting for transfers between devices: 16.4 us -> 22.4 us
    pallas_call x3 -> x2, Pallas kernels: 28.8 us -> 17.6 us  [per_device(): pl.pallas_call(functools.partial(attend_kernel, tiles_here), grid_spec=pl...]
    ppermute x14 -> x10, starting transfers between devices: 53.8 us -> 44.1 us  [shifted(): lax.ppermute(value, axis, [(source, source + steps) for source in range(l...]
    ppermute x14 -> x10, waiting for transfers between devices: 16.4 us -> 22.4 us  [shifted(): lax.ppermute(value, axis, [(source, source + steps) for source in range(l...]
  transfers between devices with their start and end apart: 14 -> 10, of which waited for: 4 -> 3; matrix products, arithmetic and copies ran while one was open for 1% -> 1% of each run, Pallas kernels for 28% -> 22%
where the time goes in v3:
time: 120 us
  starting transfers between devices  44.1 us (37%)
  Pallas kernels  41.2 us (34%)
  waiting for transfers between devices  22.4 us (19%)
  local copies, waits for them, and re-layouts  9.86 us (8%)
    ppermute x10, starting transfers between devices, shifted(): lax.ppermute(value, axis, [(source, source + steps) for source in range(l...  44.1 us
    ppermute x10, waiting for transfers between devices, shifted(): lax.ppermute(value, axis, [(source, source + steps) for source in range(l...  22.4 us
    pallas_call x2, Pallas kernels, per_device(): pl.pallas_call(functools.partial(attend_kernel, tiles_here), grid_spec=pl...  17.6 us
    pallas_call x2, Pallas kernels, head_total(): pl.pallas_call(functools.partial(exchange_kernel, count), out_shape=jax.S...  12.4 us
    unnamed x39, local copies, waits for them, and re-layouts  9.86 us
    pallas_call x1, Pallas kernels, per_device(): pl.pallas_call(functools.partial(prepare_kernel, devices, tiles_here), ou...  3.96 us
    pallas_call x1, Pallas kernels, per_device(): pl.pallas_call(functools.partial(merge_kernel, bounds), out_shape=[struct...  2.58 us
  transfers between devices with their start and end apart: 10, of which 3 were waited for; matrix products, arithmetic and copies ran while one was open for 1% of the time, Pallas kernels for 22%

profile of v3, /device:TPU:25, one launch (start us, length us, event | category | flops | bytes accessed | tf_op | source)
XLA Modules:
  0.0 119.6 jit_solution(3764111304779777963)
XLA Ops:
  0.7 0.9 copy.16.key_tiles
  1.5 1.1 copy-done.8
  2.6 1.1 copy-done.9
  3.7 0.7 copy-done.15
  4.4 4.0 %prepare.1 = (s32[16]{0:T(128)S(1)}, bf16[512,640]{1,0:T(8,128)(2,1)S(1)}, bf16[512,640]{1,0:T(8,128)(2,1)S(1)}) custom-call(s32[1]{0:T(128)} %bitcast.position_ref, s32[32]{0:T(128)S(1)} %copy-done.15, s32[32,6]{1,0:T(8,128)S(1)} %copy.16.key_tiles, bf16[512,640]{1,0:T(8,128)(2,1)S(1)} %copy-done.8, bf16[512,640]{1,0:T(8,128)(2,1)S(1)} %copy-done.9), custom_call_target="tpu_custom_call" | custom-call | tf_op jit(solution)/shard_map/prepare/pallas_call | solution.py:406
  8.3 3.1 %collective-permute-start.2 = (bf16[512,640]{1,0:T(8,128)(2,1)S(1)}, bf16[512,640]{1,0:T(8,128)(2,1)}, u32[]{:S(2)}, u32[]{:S(2)}) collective-permute-start(bf16[512,640]{1,0:T(8,128)(2,1)S(1)} %get-tuple-element.40), channel_id=1, source_target_pairs={{0,4},{4,8},{8,12},{12,16},{16,20},{20,24},{24,28},{1,5},{5,9},{9,... | collective-permute-start | bytes 1966088 | tf_op jit(solution)/shard_map/ppermute | solution.py:36
  11.5 3.1 %collective-permute-start.3 = (bf16[512,640]{1,0:T(8,128)(2,1)S(1)}, bf16[512,640]{1,0:T(8,128)(2,1)}, u32[]{:S(2)}, u32[]{:S(2)}) collective-permute-start(bf16[512,640]{1,0:T(8,128)(2,1)S(1)} %get-tuple-element.41), channel_id=1, source_target_pairs={{4,0},{8,4},{12,8},{16,12},{20,16},{24,20},{28,24},{5,1},{9,5},{13... | collective-permute-start | bytes 1966088 | tf_op jit(solution)/shard_map/ppermute | solution.py:36
  14.6 0.0 copy-start.3
  14.6 1.1 copy-done.3
  15.7 1.1 copy-done.5
  16.8 0.6 sums.1.part_ref
  17.4 0.6 copy-done.13
  18.0 6.2 %exchange.2.totals_ref = f32[8,512]{1,0:T(8,128)} custom-call(f32[8,512]{1,0:T(8,128)} %copy-done.13), custom_call_target="tpu_custom_call" | custom-call | tf_op jit(solution)/shard_map/exchange/pallas_call | solution.py:173
  24.2 0.0 copy-done.4
  24.2 0.0 copy-start.10
  24.2 0.7 copy-done.10
  25.0 2.4 %norm.1 = (bf16[512,640]{1,0:T(8,128)(2,1)S(1)}, bf16[512,640]{1,0:T(8,128)(2,1)S(1)}, bf16[512,640]{1,0:T(8,128)(2,1)S(1)}, bf16[512,640]{1,0:T(8,128)(2,1)S(1)...) custom-call(s32[16]{0:T(128)S(1)} %get-tuple-element.33.plan, ...), custom_call_target="tpu_custom_call" | custom-call | tf_op jit(solution)/shard_map/norm/pallas_call | solution.py:436
  27.3 3.0 %collective-permute-start = (bf16[512,384]{1,0:T(8,128)(2,1)S(1)}, bf16[512,384]{1,0:T(8,128)(2,1)S(1)}, u32[]{:S(2)}, u32[]{:S(2)}) collective-permute-start(bf16[512,384]{1,0:T(8,128)(2,1)S(1)} %get-tuple-element.38), channel_id=1, source_target_pairs={{0,4},{4,8},{8,12},{12,16},{16,20},{20,24},{24,28},{1,5},{5,9},{9,... | collective-permute-start | bytes 1179656 | tf_op jit(solution)/shard_map/ppermute | solution.py:36
  30.4 3.2 %collective-permute-start.1 = (bf16[512,384]{1,0:T(8,128)(2,1)S(1)}, bf16[512,384]{1,0:T(8,128)(2,1)S(1)}, u32[]{:S(2)}, u32[]{:S(2)}) collective-permute-start(bf16[512,384]{1,0:T(8,128)(2,1)S(1)} %get-tuple-element.39), channel_id=1, source_target_pairs={{4,0},{8,4},{12,8},{16,12},{20,16},{24,20},{28,24},{5,1},{9,5},{13... | collective-permute-start | bytes 1179656 | tf_op jit(solution)/shard_map/ppermute | solution.py:36
  33.5 2.1 %collective-permute-start.4 = (bf16[512,256]{1,0:T(8,128)(2,1)S(1)}, bf16[512,256]{1,0:T(8,128)(2,1)S(1)}, u32[]{:S(2)}, u32[]{:S(2)}) collective-permute-start(bf16[512,256]{1,0:T(8,128)(2,1)S(1)} %get-tuple-element.43), channel_id=1, source_target_pairs={{0,4},{4,8},{8,12},{12,16},{16,20},{20,24},{24,28},{1,5},{5,9},{9,... | collective-permute-start | bytes 786440 | tf_op jit(solution)/shard_map/ppermute | solution.py:36
  35.7 5.1 %collective-permute-done.kb_ref = bf16[512,384]{1,0:T(8,128)(2,1)S(1)} collective-permute-done((bf16[512,384]{1,0:T(8,128)(2,1)S(1)}, bf16[512,384]{1,0:T(8,128)(2,1)S(1)}, u32[]{:S(2)}, u32[]{:S(2)}) %collective-permute-start) | collective-permute-done | bytes 393248 | tf_op jit(solution)/shard_map/ppermute | solution.py:36
  40.8 19.0 %collective-permute-start.5 = (bf16[512,256]{1,0:T(8,128)(2,1)S(1)}, bf16[512,256]{1,0:T(8,128)(2,1)S(1)}, u32[]{:S(2)}, u32[]{:S(2)}) collective-permute-start(bf16[512,256]{1,0:T(8,128)(2,1)S(1)} %get-tuple-element.44), channel_id=1, source_target_pairs={{4,0},{8,4},{12,8},{16,12},{20,16},{24,20},{28,24},{5,1},{9,5},{13... | collective-permute-start | bytes 786440 | tf_op jit(solution)/shard_map/ppermute | solution.py:36
  59.7 4.6 %collective-permute-done.1.ka_ref = bf16[512,384]{1,0:T(8,128)(2,1)S(1)} collective-permute-done((bf16[512,384]{1,0:T(8,128)(2,1)S(1)}, bf16[512,384]{1,0:T(8,128)(2,1)S(1)}, u32[]{:S(2)}, u32[]{:S(2)}) %collective-permute-start.1) | collective-permute-done | bytes 393248 | tf_op jit(solution)/shard_map/ppermute | solution.py:36
  64.3 0.0 collective-permute-done.2.vb_ref
  64.3 0.0 collective-permute-done.3.va_ref
  64.3 0.0 copy-done.16
  64.3 10.5 %attend.2 = (bf16[512,384]{1,0:T(8,128)(2,1)S(1)}, bf16[512,384]{1,0:T(8,128)(2,1)S(1)}, f32[512,384]{1,0:T(8,128)}, bf16[1024,384]{1,0:T(8,128)(2,1)}, bf16[512...) custom-call(s32[16]{0:T(128)S(1)} %get-tuple-element.33.plan, bf16[512,640]{1,0:T(8,128)(2,1)S(1)} %get-tuple-element.34.q_ref, ...), custom_call_target="tpu_custom_call" | custom-call | flops 3019898880 | bytes 4718592 | tf_op jit(solution)/shard_map/attend/pallas_call | solution.py:457
  74.8 1.9 %collective-permute-start.6 = (bf16[512,384]{1,0:T(8,128)(2,1)S(1)}, bf16[512,384]{1,0:T(8,128)(2,1)S(1)}, u32[]{:S(2)}, u32[]{:S(2)}) collective-permute-start(bf16[512,384]{1,0:T(8,128)(2,1)S(1)} %get-tuple-element.52), channel_id=1, source_target_pairs={{4,0},{8,4},{12,8},{16,12},{20,16},{24,20},{28,24},{5,1},{9,5},{13... | collective-permute-start | bytes 1179656 | tf_op jit(solution)/shard_map/ppermute | solution.py:36
  76.7 3.4 %collective-permute-start.8 = (bf16[512,384]{1,0:T(8,128)(2,1)S(1)}, bf16[512,384]{1,0:T(8,128)(2,1)S(1)}, u32[]{:S(2)}, u32[]{:S(2)}) collective-permute-start(bf16[512,384]{1,0:T(8,128)(2,1)S(1)} %get-tuple-element.54), channel_id=1, source_target_pairs={{0,4},{4,8},{8,12},{12,16},{16,20},{20,24},{24,28},{1,5},{5,9},{9,... | collective-permute-start | bytes 1179656 | tf_op jit(solution)/shard_map/ppermute | solution.py:36
  80.1 0.0 collective-permute-done.4.kb_ref
  80.1 0.0 collective-permute-done.5.ka_ref
  80.1 7.1 %attend.3 = (bf16[512,256]{1,0:T(8,128)(2,1)S(1)}, bf16[512,256]{1,0:T(8,128)(2,1)S(1)}, f32[512,256]{1,0:T(8,128)S(1)}, bf16[1024,256]{1,0:T(8,128)(2,1)S(1)}, ...) custom-call(s32[16]{0:T(128)S(1)} %get-tuple-element.33.plan, bf16[512,640]{1,0:T(8,128)(2,1)S(1)} %get-tuple-element.34.q_ref, ...), custom_call_target="tpu_custom_call" | custom-call | flops 2013265920 | bytes 3145728 | tf_op jit(solution)/shard_map/attend/pallas_call | solution.py:457
  87.2 2.8 %collective-permute-start.7 = (bf16[512,256]{1,0:T(8,128)(2,1)S(1)}, bf16[512,256]{1,0:T(8,128)(2,1)S(1)}, u32[]{:S(2)}, u32[]{:S(2)}) collective-permute-start(bf16[512,256]{1,0:T(8,128)(2,1)S(1)} %get-tuple-element.53), channel_id=1, source_target_pairs={{4,0},{8,4},{12,8},{16,12},{20,16},{24,20},{28,24},{5,1},{9,5},{13... | collective-permute-start | bytes 786440 | tf_op jit(solution)/shard_map/ppermute | solution.py:36
  90.0 2.5 %collective-permute-start.9 = (bf16[512,256]{1,0:T(8,128)(2,1)S(1)}, bf16[512,256]{1,0:T(8,128)(2,1)S(1)}, u32[]{:S(2)}, u32[]{:S(2)}) collective-permute-start(bf16[512,256]{1,0:T(8,128)(2,1)S(1)} %get-tuple-element.55), channel_id=1, source_target_pairs={{0,4},{4,8},{8,12},{12,16},{16,20},{20,24},{24,28},{1,5},{5,9},{9,... | collective-permute-start | bytes 786440 | tf_op jit(solution)/shard_map/ppermute | solution.py:36
  92.6 1.2 pad_maximum_fusion
  93.8 12.7 %collective-permute-done.7.refs_5_ = bf16[512,256]{1,0:T(8,128)(2,1)S(1)} collective-permute-done((bf16[512,256]{1,0:T(8,128)(2,1)S(1)}, bf16[512,256]{1,0:T(8,128)(2,1)S(1)}, u32[]{:S(2)}, u32[]{:S(2)}) %collective-permute-start.7) | collective-permute-done | bytes 262176 | tf_op jit(solution)/shard_map/ppermute | solution.py:36
  106.5 0.0 collective-permute-done.9.refs_7_
  106.5 0.0 collective-permute-done.6.refs_4_
  106.5 0.0 collective-permute-done.8.refs_6_
  106.5 0.0 copy-done.2
  106.5 0.0 copy-done.7
  106.5 0.0 copy-start.11
  106.5 2.6 %merge.1 = (bf16[512,640]{1,0:T(8,128)(2,1)}, f32[512,640]{1,0:T(8,128)}, f32[8,512]{1,0:T(8,128)S(1)}) custom-call(s32[16]{0:T(128)S(1)} %get-tuple-element.33.plan, bf16[512,640]{1,0:T(8,128)(2,1)S(1)} %copy-done, bf16[512,640]{1,0:T(8,128)(2,1)S(1)} %copy-done.1, f32[1,640]{1,0:T(1,128)S(1)} %reshape.20.q_gain_ref, f32[1,640]{1,0:T(1,128)S(1)} %reshape.21.k_gain_ref, ...), custom_call_target="tpu_custom_call" | custom-call | tf_op jit(solution)/shard_map/merge/pallas_call | solution.py:499
  109.1 0.6 copy-done.14
  109.7 6.2 %exchange.3.back_ref = f32[8,512]{1,0:T(8,128)} custom-call(f32[8,512]{1,0:T(8,128)} %copy-done.14), custom_call_target="tpu_custom_call" | custom-call | tf_op jit(solution)/shard_map/exchange/pallas_call | solution.py:173
  115.9 1.3 %copy-done.6 = f32[512,640]{1,0:T(8,128)S(1)} copy-done((f32[512,640]{1,0:T(8,128)S(1)}, f32[512,640]{1,0:T(8,128)}, u32[]{:S(2)}) %copy-start.6) | copy-done | bytes 1310744
  117.2 0.7 copy-done.12
  117.9 1.7 %final.1 = (bf16[512,640]{1,0:T(8,128)(2,1)}, bf16[512,640]{1,0:T(8,128)(2,1)}) custom-call(f32[8,512]{1,0:T(8,128)S(1)} %copy-done.11, f32[8,512]{1,0:T(8,128)S(1)} %copy-done.12, bf16[512,640]{1,0:T(8,128)(2,1)S(1)} %copy-done, bf16[512,640]{1,0:T(8,128)(2,1)S(1)} %copy-done.1, f32[1,640]{1,0:T(1,128)S(1)} %reshape.20.q_gain_ref, ...), custom_call_target="tpu_custom_call" | custom-call | tf_op jit(solution)/shard_map/final/pallas_call | solution.py:511
  (23 shorter events, 0.0 us)
Async XLA Ops:
  0.6 13.9 %copy-start = (bf16[512,640]{1,0:T(8,128)(2,1)S(1)}, bf16[512,640]{1,0:T(8,128)(2,1)}, u32[]{:S(2)}) copy-start(bf16[512,640]{1,0:T(8,128)(2,1)} %q_ref.7) | copy-start | bytes 1966084
  0.6 13.9 %copy-start.1 = (bf16[512,640]{1,0:T(8,128)(2,1)S(1)}, bf16[512,640]{1,0:T(8,128)(2,1)}, u32[]{:S(2)}) copy-start(bf16[512,640]{1,0:T(8,128)(2,1)} %k_ref.7) | copy-start | bytes 1966084
  1.5 1.1 copy-start.8
  2.6 1.1 copy-start.9
  3.7 0.7 copy-start.15
  4.4 10.2 %copy-start.17 = (f32[640]{0:T(1024)S(1)}, f32[640]{0:T(1024)}, u32[]{:S(2)}) copy-start(f32[640]{0:T(1024)} %param.18) | copy-start | bytes 7684
  4.4 10.2 %copy-start.18 = (f32[640]{0:T(1024)S(1)}, f32[640]{0:T(1024)}, u32[]{:S(2)}) copy-start(f32[640]{0:T(1024)} %param.19) | copy-start | bytes 7684
  8.3 56.0 %collective-permute-start.2 = (bf16[512,640]{1,0:T(8,128)(2,1)S(1)}, bf16[512,640]{1,0:T(8,128)(2,1)}, u32[]{:S(2)}, u32[]{:S(2)}) collective-permute-start(bf16[512,640]{1,0:T(8,128)(2,1)S(1)} %get-tuple-element.40), channel_id=1, source_target_pairs={{0,4},{4,8},{8,12},{12,16},{16,20},{20,24},{24,28},{1,5},{5,9},{9,... | collective-permute-start | bytes 1966088 | tf_op jit(solution)/shard_map/ppermute | solution.py:36
  11.5 52.8 %collective-permute-start.3 = (bf16[512,640]{1,0:T(8,128)(2,1)S(1)}, bf16[512,640]{1,0:T(8,128)(2,1)}, u32[]{:S(2)}, u32[]{:S(2)}) collective-permute-start(bf16[512,640]{1,0:T(8,128)(2,1)S(1)} %get-tuple-element.41), channel_id=1, source_target_pairs={{4,0},{8,4},{12,8},{16,12},{20,16},{24,20},{28,24},{5,1},{9,5},{13... | collective-permute-start | bytes 1966088 | tf_op jit(solution)/shard_map/ppermute | solution.py:36
  14.6 1.1 copy-start.3
  15.7 1.1 copy-start.5
  16.8 7.5 %copy-start.4 = (bf16[512,640]{1,0:T(8,128)(2,1)S(1)}, bf16[512,640]{1,0:T(8,128)(2,1)}, u32[]{:S(2)}) copy-start(bf16[512,640]{1,0:T(8,128)(2,1)} %qt_ref.3) | copy-start | bytes 1966084
  17.4 0.6 copy-start.13
  24.2 0.7 copy-start.10
  25.0 39.3 %copy-start.16 = (bf16[512,640]{1,0:T(8,128)(2,1)S(1)}, bf16[512,640]{1,0:T(8,128)(2,1)}, u32[]{:S(2)}) copy-start(bf16[512,640]{1,0:T(8,128)(2,1)} %co_ref.3) | copy-start | bytes 1966084
  27.3 13.4 %collective-permute-start = (bf16[512,384]{1,0:T(8,128)(2,1)S(1)}, bf16[512,384]{1,0:T(8,128)(2,1)S(1)}, u32[]{:S(2)}, u32[]{:S(2)}) collective-permute-start(bf16[512,384]{1,0:T(8,128)(2,1)S(1)} %get-tuple-element.38), channel_id=1, source_target_pairs={{0,4},{4,8},{8,12},{12,16},{16,20},{20,24},{24,28},{1,5},{5,9},{9,... | collective-permute-start | bytes 1179656 | tf_op jit(solution)/shard_map/ppermute | solution.py:36
  30.4 33.9 %collective-permute-start.1 = (bf16[512,384]{1,0:T(8,128)(2,1)S(1)}, bf16[512,384]{1,0:T(8,128)(2,1)S(1)}, u32[]{:S(2)}, u32[]{:S(2)}) collective-permute-start(bf16[512,384]{1,0:T(8,128)(2,1)S(1)} %get-tuple-element.39), channel_id=1, source_target_pairs={{4,0},{8,4},{12,8},{16,12},{20,16},{24,20},{28,24},{5,1},{9,5},{13... | collective-permute-start | bytes 1179656 | tf_op jit(solution)/shard_map/ppermute | solution.py:36
  33.5 46.6 %collective-permute-start.4 = (bf16[512,256]{1,0:T(8,128)(2,1)S(1)}, bf16[512,256]{1,0:T(8,128)(2,1)S(1)}, u32[]{:S(2)}, u32[]{:S(2)}) collective-permute-start(bf16[512,256]{1,0:T(8,128)(2,1)S(1)} %get-tuple-element.43), channel_id=1, source_target_pairs={{0,4},{4,8},{8,12},{12,16},{16,20},{20,24},{24,28},{1,5},{5,9},{9,... | collective-permute-start | bytes 786440 | tf_op jit(solution)/shard_map/ppermute | solution.py:36
  40.8 39.4 %collective-permute-start.5 = (bf16[512,256]{1,0:T(8,128)(2,1)S(1)}, bf16[512,256]{1,0:T(8,128)(2,1)S(1)}, u32[]{:S(2)}, u32[]{:S(2)}) collective-permute-start(bf16[512,256]{1,0:T(8,128)(2,1)S(1)} %get-tuple-element.44), channel_id=1, source_target_pairs={{4,0},{8,4},{12,8},{16,12},{20,16},{24,20},{28,24},{5,1},{9,5},{13... | collective-permute-start | bytes 786440 | tf_op jit(solution)/shard_map/ppermute | solution.py:36
  74.8 31.6 %collective-permute-start.6 = (bf16[512,384]{1,0:T(8,128)(2,1)S(1)}, bf16[512,384]{1,0:T(8,128)(2,1)S(1)}, u32[]{:S(2)}, u32[]{:S(2)}) collective-permute-start(bf16[512,384]{1,0:T(8,128)(2,1)S(1)} %get-tuple-element.52), channel_id=1, source_target_pairs={{4,0},{8,4},{12,8},{16,12},{20,16},{24,20},{28,24},{5,1},{9,5},{13... | collective-permute-start | bytes 1179656 | tf_op jit(solution)/shard_map/ppermute | solution.py:36
  76.7 29.7 %collective-permute-start.8 = (bf16[512,384]{1,0:T(8,128)(2,1)S(1)}, bf16[512,384]{1,0:T(8,128)(2,1)S(1)}, u32[]{:S(2)}, u32[]{:S(2)}) collective-permute-start(bf16[512,384]{1,0:T(8,128)(2,1)S(1)} %get-tuple-element.54), channel_id=1, source_target_pairs={{0,4},{4,8},{8,12},{12,16},{16,20},{20,24},{24,28},{1,5},{5,9},{9,... | collective-permute-start | bytes 1179656 | tf_op jit(solution)/shard_map/ppermute | solution.py:36
  87.2 19.2 %collective-permute-start.7 = (bf16[512,256]{1,0:T(8,128)(2,1)S(1)}, bf16[512,256]{1,0:T(8,128)(2,1)S(1)}, u32[]{:S(2)}, u32[]{:S(2)}) collective-permute-start(bf16[512,256]{1,0:T(8,128)(2,1)S(1)} %get-tuple-element.53), channel_id=1, source_target_pairs={{4,0},{8,4},{12,8},{16,12},{20,16},{24,20},{28,24},{5,1},{9,5},{13... | collective-permute-start | bytes 786440 | tf_op jit(solution)/shard_map/ppermute | solution.py:36
  90.0 16.4 %collective-permute-start.9 = (bf16[512,256]{1,0:T(8,128)(2,1)S(1)}, bf16[512,256]{1,0:T(8,128)(2,1)S(1)}, u32[]{:S(2)}, u32[]{:S(2)}) collective-permute-start(bf16[512,256]{1,0:T(8,128)(2,1)S(1)} %get-tuple-element.55), channel_id=1, source_target_pairs={{0,4},{4,8},{8,12},{12,16},{16,20},{20,24},{24,28},{1,5},{5,9},{9,... | collective-permute-start | bytes 786440 | tf_op jit(solution)/shard_map/ppermute | solution.py:36
  92.5 13.9 %copy-start.2 = (f32[512,384]{1,0:T(8,128)S(1)}, f32[512,384]{1,0:T(8,128)}, u32[]{:S(2)}) copy-start(f32[512,384]{1,0:T(8,128)} %get-tuple-element.48.refs_0_) | copy-start | bytes 2359300
  92.6 13.9 %copy-start.7 = (bf16[1024,384]{1,0:T(8,128)(2,1)S(1)}, bf16[1024,384]{1,0:T(8,128)(2,1)}, u32[]{:S(2)}) copy-start(bf16[1024,384]{1,0:T(8,128)(2,1)} %get-tuple-element.50.refs_2_) | copy-start | bytes 2359300
  106.5 9.4 %copy-start.11 = (f32[8,512]{1,0:T(8,128)S(1)}, f32[8,512]{1,0:T(8,128)}, u32[]{:S(2)}) copy-start(f32[8,512]{1,0:T(8,128)} %exchange.2.totals_ref) | copy-start | bytes 49156
  109.1 0.6 copy-start.14
  115.9 1.3 %copy-start.6 = (f32[512,640]{1,0:T(8,128)S(1)}, f32[512,640]{1,0:T(8,128)}, u32[]{:S(2)}) copy-start(f32[512,640]{1,0:T(8,128)} %get-tuple-element.57.key_ref) | copy-start | bytes 3932164
  117.2 0.7 copy-start.12

commit v4 on v3

--- a/solution.py
+++ b/solution.py
@@ -16,12 +16,12 @@
 NORM_EPS = 1e-06
 SCALE = HEAD_DIM ** (-0.5)
 PACK = NEED * TILE
-VMEM_BYTES = 48 * 1024 * 1024
-CHUNKS = (3, 2)
+VMEM_BYTES = 24 * 1024 * 1024
+CHUNKS = (2, 3)
 
 VMEM = pl.BlockSpec(memory_space=pltpu.VMEM)
 SMEM = pl.BlockSpec(memory_space=pltpu.SMEM)
-HBM = pl.BlockSpec(memory_space=pltpu.HBM)
+HBM = pl.BlockSpec(memory_space=pl.ANY)
 F32 = jnp.float32
 BF16 = jnp.bfloat16
 
@@ -181,7 +181,9 @@
             pltpu.SemaphoreType.DMA((count - 1,)),
         ],
         compiler_params=pltpu.CompilerParams(
-            collective_id=collective_id, has_side_effects=True
+            collective_id=collective_id,
+            has_side_effects=True,
+            vmem_limit_bytes=2 * 1024 * 1024,
         ),
         name="exchange",
     )(part)

time: 120 us -> 115 us (0.958)
  Pallas kernels: 41.2 us -> 36 us
  local copies, waits for them, and re-layouts: 9.86 us -> 5.91 us
  starting transfers between devices: 44.1 us -> 47.2 us
    unnamed x39 -> x27, local copies, waits for them, and re-layouts: 9.86 us -> 5.9 us
    ppermute x10, starting transfers between devices: 44.1 us -> 47.2 us  [shifted(): lax.ppermute(value, axis, [(source, source + steps) for source in range(l...]
    pallas_call x2, Pallas kernels: 12.4 us -> 9.69 us  [head_total(): pl.pallas_call(functools.partial(exchange_kernel, count), out_shape=jax.S...]
    pallas_call x2, Pallas kernels: 17.6 us -> 15.9 us  [per_device(): pl.pallas_call(functools.partial(attend_kernel, tiles_here), grid_spec=pl...]
  transfers between devices with their start and end apart: 10 -> 10, of which waited for: 3 -> 3; matrix products, arithmetic and copies ran while one was open for 1% -> 1% of each run, Pallas kernels for 22% -> 20%
where the time goes in v4:
time: 115 us; the launch traced here: 114 us
  starting transfers between devices  47.2 us (41%)
  Pallas kernels  36 us (31%)
  waiting for transfers between devices  23.1 us (20%)
  local copies, waits for them, and re-layouts  5.91 us (5%)
  other arithmetic  1.17 us (1%)
    ppermute x10, starting transfers between devices, shifted(): lax.ppermute(value, axis, [(source, source + steps) for source in range(l...  47.2 us
    ppermute x10, waiting for transfers between devices, shifted(): lax.ppermute(value, axis, [(source, source + steps) for source in range(l...  23.1 us
    pallas_call x2, Pallas kernels, per_device(): pl.pallas_call(functools.partial(attend_kernel, tiles_here), grid_spec=pl...  15.9 us
    pallas_call x2, Pallas kernels, head_total(): pl.pallas_call(functools.partial(exchange_kernel, count), out_shape=jax.S...  9.69 us
    unnamed x27, local copies, waits for them, and re-layouts  5.9 us
    pallas_call x1, Pallas kernels, per_device(): pl.pallas_call(functools.partial(prepare_kernel, devices, tiles_here), ou...  3.96 us
  transfers between devices with their start and end apart: 10, of which 3 were waited for; matrix products, arithmetic and copies ran while one was open for 1% of the time, Pallas kernels for 20%

profile of v4, /device:TPU:25, one launch (start us, length us, event | category | flops | bytes accessed | tf_op | source)
XLA Modules:
  0.0 114.3 jit_solution(7629702046000118700)
XLA Ops:
  0.6 0.0 copy-start
  0.6 0.0 copy-start.1
  0.7 0.9 copy.16.key_tiles
  1.5 1.1 copy-done.5
  2.6 1.1 copy-done.7
  3.7 0.7 copy-done.9
  4.4 4.0 %prepare.1 = (s32[16]{0:T(128)S(1)}, bf16[512,640]{1,0:T(8,128)(2,1)S(1)}, bf16[512,640]{1,0:T(8,128)(2,1)S(1)}) custom-call(s32[1]{0:T(128)} %bitcast.position_ref, s32[32]{0:T(128)S(1)} %copy-done.9, s32[32,6]{1,0:T(8,128)S(1)} %copy.16.key_tiles, bf16[512,640]{1,0:T(8,128)(2,1)S(1)} %copy-done.5, bf16[512,640]{1,0:T(8,128)(2,1)S(1)} %copy-done.7), custom_call_target="tpu_custom_call" | custom-call | tf_op jit(solution)/shard_map/prepare/pallas_call | solution.py:408
  8.3 3.1 %collective-permute-start.2 = (bf16[512,640]{1,0:T(8,128)(2,1)S(1)}, bf16[512,640]{1,0:T(8,128)(2,1)S(1)}, u32[]{:S(2)}, u32[]{:S(2)}) collective-permute-start(bf16[512,640]{1,0:T(8,128)(2,1)S(1)} %get-tuple-element.40), channel_id=1, source_target_pairs={{0,4},{4,8},{8,12},{12,16},{16,20},{20,24},{24,28},{1,5},{5,9},{9,... | collective-permute-start | bytes 1966088 | tf_op jit(solution)/shard_map/ppermute | solution.py:36
  11.5 3.1 %collective-permute-start.3 = (bf16[512,640]{1,0:T(8,128)(2,1)S(1)}, bf16[512,640]{1,0:T(8,128)(2,1)S(1)}, u32[]{:S(2)}, u32[]{:S(2)}) collective-permute-start(bf16[512,640]{1,0:T(8,128)(2,1)S(1)} %get-tuple-element.41), channel_id=1, source_target_pairs={{4,0},{8,4},{12,8},{16,12},{20,16},{24,20},{28,24},{5,1},{9,5},{13... | collective-permute-start | bytes 1966088 | tf_op jit(solution)/shard_map/ppermute | solution.py:36
  14.5 0.0 copy-done
  14.5 0.0 copy-done.1
  14.5 0.0 copy-start.2
  14.6 1.1 copy-done.2
  15.6 1.1 copy-done.4
  16.7 0.6 sums.1.part_ref
  17.3 4.8 %exchange.2.totals_ref = f32[8,512]{1,0:T(8,128)S(1)} custom-call(f32[8,512]{1,0:T(8,128)S(1)} %sums.1.part_ref), custom_call_target="tpu_custom_call" | custom-call | tf_op jit(solution)/shard_map/exchange/pallas_call | solution.py:173
  22.2 0.0 copy-done.11
  22.2 0.0 copy-done.12
  22.2 0.0 copy-start.6
  22.2 0.0 copy-start.8
  22.2 0.0 copy-start.10
  22.3 1.8 %norm.1 = (bf16[512,640]{1,0:T(8,128)(2,1)S(1)}, bf16[512,640]{1,0:T(8,128)(2,1)S(1)}, bf16[512,640]{1,0:T(8,128)(2,1)S(1)}, bf16[512,640]{1,0:T(8,128)(2,1)S(1)...) custom-call(s32[16]{0:T(128)S(1)} %get-tuple-element.33.plan, ...), custom_call_target="tpu_custom_call" | custom-call | tf_op jit(solution)/shard_map/norm/pallas_call | solution.py:438
  24.0 2.3 %collective-permute-start.4 = (bf16[512,384]{1,0:T(8,128)(2,1)S(1)}, bf16[512,384]{1,0:T(8,128)(2,1)S(1)}, u32[]{:S(2)}, u32[]{:S(2)}) collective-permute-start(bf16[512,384]{1,0:T(8,128)(2,1)S(1)} %get-tuple-element.43), channel_id=1, source_target_pairs={{0,4},{4,8},{8,12},{12,16},{16,20},{20,24},{24,28},{1,5},{5,9},{9,... | collective-permute-start | bytes 1179656 | tf_op jit(solution)/shard_map/ppermute | solution.py:36
  26.3 3.9 %collective-permute-start.5 = (bf16[512,384]{1,0:T(8,128)(2,1)S(1)}, bf16[512,384]{1,0:T(8,128)(2,1)S(1)}, u32[]{:S(2)}, u32[]{:S(2)}) collective-permute-start(bf16[512,384]{1,0:T(8,128)(2,1)S(1)} %get-tuple-element.44), channel_id=1, source_target_pairs={{4,0},{8,4},{12,8},{16,12},{20,16},{24,20},{28,24},{5,1},{9,5},{13... | collective-permute-start | bytes 1179656 | tf_op jit(solution)/shard_map/ppermute | solution.py:36
  30.2 1.9 %collective-permute-start = (bf16[512,256]{1,0:T(8,128)(2,1)S(1)}, bf16[512,256]{1,0:T(8,128)(2,1)S(1)}, u32[]{:S(2)}, u32[]{:S(2)}) collective-permute-start(bf16[512,256]{1,0:T(8,128)(2,1)S(1)} %get-tuple-element.38), channel_id=1, source_target_pairs={{0,4},{4,8},{8,12},{12,16},{16,20},{20,24},{24,28},{1,5},{5,9},{9,... | collective-permute-start | bytes 786440 | tf_op jit(solution)/shard_map/ppermute | solution.py:36
  32.2 5.2 %collective-permute-done.4.kb_ref = bf16[512,384]{1,0:T(8,128)(2,1)S(1)} collective-permute-done((bf16[512,384]{1,0:T(8,128)(2,1)S(1)}, bf16[512,384]{1,0:T(8,128)(2,1)S(1)}, u32[]{:S(2)}, u32[]{:S(2)}) %collective-permute-start.4) | collective-permute-done | bytes 393248 | tf_op jit(solution)/shard_map/ppermute | solution.py:36
  37.4 22.4 %collective-permute-start.1 = (bf16[512,256]{1,0:T(8,128)(2,1)S(1)}, bf16[512,256]{1,0:T(8,128)(2,1)S(1)}, u32[]{:S(2)}, u32[]{:S(2)}) collective-permute-start(bf16[512,256]{1,0:T(8,128)(2,1)S(1)} %get-tuple-element.39), channel_id=1, source_target_pairs={{4,0},{8,4},{12,8},{16,12},{20,16},{24,20},{28,24},{5,1},{9,5},{13... | collective-permute-start | bytes 786440 | tf_op jit(solution)/shard_map/ppermute | solution.py:36
  59.7 4.6 %collective-permute-done.5.ka_ref = bf16[512,384]{1,0:T(8,128)(2,1)S(1)} collective-permute-done((bf16[512,384]{1,0:T(8,128)(2,1)S(1)}, bf16[512,384]{1,0:T(8,128)(2,1)S(1)}, u32[]{:S(2)}, u32[]{:S(2)}) %collective-permute-start.5) | collective-permute-done | bytes 393248 | tf_op jit(solution)/shard_map/ppermute | solution.py:36
  64.3 0.0 collective-permute-done.2.vb_ref
  64.3 0.0 collective-permute-done.3.va_ref
  64.3 0.0 copy-done.8
  64.3 0.0 copy-done.10
  64.3 9.4 %attend.3 = (bf16[512,384]{1,0:T(8,128)(2,1)S(1)}, bf16[512,384]{1,0:T(8,128)(2,1)S(1)}, f32[512,384]{1,0:T(8,128)S(1)}, bf16[1024,384]{1,0:T(8,128)(2,1)S(1)}, ...) custom-call(s32[16]{0:T(128)S(1)} %get-tuple-element.33.plan, bf16[512,640]{1,0:T(8,128)(2,1)S(1)} %get-tuple-element.34.q_ref, ...), custom_call_target="tpu_custom_call" | custom-call | flops 3019898880 | bytes 4718592 | tf_op jit(solution)/shard_map/attend/pallas_call | solution.py:459
  73.8 1.9 %collective-permute-start.7 = (bf16[512,384]{1,0:T(8,128)(2,1)S(1)}, bf16[512,384]{1,0:T(8,128)(2,1)S(1)}, u32[]{:S(2)}, u32[]{:S(2)}) collective-permute-start(bf16[512,384]{1,0:T(8,128)(2,1)S(1)} %get-tuple-element.53), channel_id=1, source_target_pairs={{4,0},{8,4},{12,8},{16,12},{20,16},{24,20},{28,24},{5,1},{9,5},{13... | collective-permute-start | bytes 1179656 | tf_op jit(solution)/shard_map/ppermute | solution.py:36
  75.7 3.4 %collective-permute-start.9 = (bf16[512,384]{1,0:T(8,128)(2,1)S(1)}, bf16[512,384]{1,0:T(8,128)(2,1)S(1)}, u32[]{:S(2)}, u32[]{:S(2)}) collective-permute-start(bf16[512,384]{1,0:T(8,128)(2,1)S(1)} %get-tuple-element.55), channel_id=1, source_target_pairs={{0,4},{4,8},{8,12},{12,16},{16,20},{20,24},{24,28},{1,5},{5,9},{9,... | collective-permute-start | bytes 1179656 | tf_op jit(solution)/shard_map/ppermute | solution.py:36
  79.1 0.0 collective-permute-done.kb_ref
  79.1 0.0 collective-permute-done.1.ka_ref
  79.1 6.5 %attend.2 = (bf16[512,256]{1,0:T(8,128)(2,1)S(1)}, bf16[512,256]{1,0:T(8,128)(2,1)S(1)}, f32[512,256]{1,0:T(8,128)S(1)}, bf16[1024,256]{1,0:T(8,128)(2,1)S(1)}, ...) custom-call(s32[16]{0:T(128)S(1)} %get-tuple-element.33.plan, bf16[512,640]{1,0:T(8,128)(2,1)S(1)} %get-tuple-element.34.q_ref, ...), custom_call_target="tpu_custom_call" | custom-call | flops 2013265920 | bytes 3145728 | tf_op jit(solution)/shard_map/attend/pallas_call | solution.py:459
  85.6 2.8 %collective-permute-start.6 = (bf16[512,256]{1,0:T(8,128)(2,1)S(1)}, bf16[512,256]{1,0:T(8,128)(2,1)S(1)}, u32[]{:S(2)}, u32[]{:S(2)}) collective-permute-start(bf16[512,256]{1,0:T(8,128)(2,1)S(1)} %get-tuple-element.52), channel_id=1, source_target_pairs={{4,0},{8,4},{12,8},{16,12},{20,16},{24,20},{28,24},{5,1},{9,5},{13... | collective-permute-start | bytes 786440 | tf_op jit(solution)/shard_map/ppermute | solution.py:36
  88.4 2.5 %collective-permute-start.8 = (bf16[512,256]{1,0:T(8,128)(2,1)S(1)}, bf16[512,256]{1,0:T(8,128)(2,1)S(1)}, u32[]{:S(2)}, u32[]{:S(2)}) collective-permute-start(bf16[512,256]{1,0:T(8,128)(2,1)S(1)} %get-tuple-element.54), channel_id=1, source_target_pairs={{0,4},{4,8},{8,12},{12,16},{16,20},{20,24},{24,28},{1,5},{5,9},{9,... | collective-permute-start | bytes 786440 | tf_op jit(solution)/shard_map/ppermute | solution.py:36
  90.9 1.2 %pad_maximum_fusion = (bf16[512,640]{1,0:T(8,128)(2,1)}, bf16[512,640]{1,0:T(8,128)(2,1)}) fusion(bf16[512,384]{1,0:T(8,128)(2,1)S(1)} %get-tuple-element.45, bf16[512,256]{1,0:T(8,128)(2,1)S(1)} %get-tuple-element.42, bf16[512,384]{1,0:T(8,128)(2,1)S(1)} %get-tuple-element.47, bf16[512,256]{1,0:T(8,128)(2,1)S(1)} %get-tuple-element.46), kind=kLoop, calls=%fused_computation | loop fusion | flops 2621440 | bytes 2621440 | tf_op jit(solution)/shard_map/concatenate | solution.py:522
  92.1 13.3 %collective-permute-done.6.refs_4_ = bf16[512,256]{1,0:T(8,128)(2,1)S(1)} collective-permute-done((bf16[512,256]{1,0:T(8,128)(2,1)S(1)}, bf16[512,256]{1,0:T(8,128)(2,1)S(1)}, u32[]{:S(2)}, u32[]{:S(2)}) %collective-permute-start.6) | collective-permute-done | bytes 262176 | tf_op jit(solution)/shard_map/ppermute | solution.py:36
  105.4 0.0 collective-permute-done.8.refs_6_
  105.4 0.0 collective-permute-done.7.refs_5_
  105.4 0.0 collective-permute-done.9.refs_7_
  105.4 2.3 %merge.1 = (bf16[512,640]{1,0:T(8,128)(2,1)}, f32[512,640]{1,0:T(8,128)S(1)}, f32[8,512]{1,0:T(8,128)S(1)}) custom-call(s32[16]{0:T(128)S(1)} %get-tuple-element.33.plan, bf16[512,640]{1,0:T(8,128)(2,1)S(1)} %copy-done, bf16[512,640]{1,0:T(8,128)(2,1)S(1)} %copy-done.1, f32[1,640]{1,0:T(1,128)S(1)} %reshape.20.q_gain_ref, f32[1,640]{1,0:T(1,128)S(1)} %reshape.21.k_gain_ref, ...), custom_call_target="tpu_custom_call" | custom-call | tf_op jit(solution)/shard_map/merge/pallas_call | solution.py:501
  107.7 4.9 %exchange.3.back_ref = f32[8,512]{1,0:T(8,128)S(1)} custom-call(f32[8,512]{1,0:T(8,128)S(1)} %get-tuple-element.56.part_ref), custom_call_target="tpu_custom_call" | custom-call | tf_op jit(solution)/shard_map/exchange/pallas_call | solution.py:173
  112.6 1.7 %final.1 = (bf16[512,640]{1,0:T(8,128)(2,1)}, bf16[512,640]{1,0:T(8,128)(2,1)}) custom-call(f32[8,512]{1,0:T(8,128)S(1)} %exchange.2.totals_ref, f32[8,512]{1,0:T(8,128)S(1)} %exchange.3.back_ref, bf16[512,640]{1,0:T(8,128)(2,1)S(1)} %copy-done, bf16[512,640]{1,0:T(8,128)(2,1)S(1)} %copy-done.1, f32[1,640]{1,0:T(1,128)S(1)} %reshape.20.q_gain_ref, ...), custom_call_target="tpu_custom_call" | custom-call | tf_op jit(solution)/shard_map/final/pallas_call | solution.py:513
  (11 shorter events, 0.0 us)
Async XLA Ops:
  0.6 13.9 %copy-start = (bf16[512,640]{1,0:T(8,128)(2,1)S(1)}, bf16[512,640]{1,0:T(8,128)(2,1)}, u32[]{:S(2)}) copy-start(bf16[512,640]{1,0:T(8,128)(2,1)} %q_ref.7) | copy-start | bytes 1966084
  0.6 13.9 %copy-start.1 = (bf16[512,640]{1,0:T(8,128)(2,1)S(1)}, bf16[512,640]{1,0:T(8,128)(2,1)}, u32[]{:S(2)}) copy-start(bf16[512,640]{1,0:T(8,128)(2,1)} %k_ref.7) | copy-start | bytes 1966084
  1.5 1.1 copy-start.5
  2.6 1.1 copy-start.7
  3.7 0.7 copy-start.9
  8.3 56.0 %collective-permute-start.2 = (bf16[512,640]{1,0:T(8,128)(2,1)S(1)}, bf16[512,640]{1,0:T(8,128)(2,1)S(1)}, u32[]{:S(2)}, u32[]{:S(2)}) collective-permute-start(bf16[512,640]{1,0:T(8,128)(2,1)S(1)} %get-tuple-element.40), channel_id=1, source_target_pairs={{0,4},{4,8},{8,12},{12,16},{16,20},{20,24},{24,28},{1,5},{5,9},{9,... | collective-permute-start | bytes 1966088 | tf_op jit(solution)/shard_map/ppermute | solution.py:36
  11.5 52.8 %collective-permute-start.3 = (bf16[512,640]{1,0:T(8,128)(2,1)S(1)}, bf16[512,640]{1,0:T(8,128)(2,1)S(1)}, u32[]{:S(2)}, u32[]{:S(2)}) collective-permute-start(bf16[512,640]{1,0:T(8,128)(2,1)S(1)} %get-tuple-element.41), channel_id=1, source_target_pairs={{4,0},{8,4},{12,8},{16,12},{20,16},{24,20},{28,24},{5,1},{9,5},{13... | collective-permute-start | bytes 1966088 | tf_op jit(solution)/shard_map/ppermute | solution.py:36
  14.5 1.1 copy-start.2
  15.6 1.1 copy-start.4
  16.7 5.4 %copy-start.11 = (f32[640]{0:T(1024)S(1)}, f32[640]{0:T(1024)}, u32[]{:S(2)}) copy-start(f32[640]{0:T(1024)} %param.18) | copy-start | bytes 7684
  16.7 5.5 %copy-start.12 = (f32[640]{0:T(1024)S(1)}, f32[640]{0:T(1024)}, u32[]{:S(2)}) copy-start(f32[640]{0:T(1024)} %param.19) | copy-start | bytes 7684
  16.7 5.5 %copy-start.3 = (bf16[512,640]{1,0:T(8,128)(2,1)S(1)}, bf16[512,640]{1,0:T(8,128)(2,1)}, u32[]{:S(2)}) copy-start(bf16[512,640]{1,0:T(8,128)(2,1)} %qt_ref.3) | copy-start | bytes 1966084
  22.2 42.1 %copy-start.6 = (bf16[512,640]{1,0:T(8,128)(2,1)S(1)}, bf16[512,640]{1,0:T(8,128)(2,1)}, u32[]{:S(2)}) copy-start(bf16[512,640]{1,0:T(8,128)(2,1)} %v_ref.5) | copy-start | bytes 1966084
  22.2 42.1 %copy-start.8 = (bf16[512,640]{1,0:T(8,128)(2,1)S(1)}, bf16[512,640]{1,0:T(8,128)(2,1)}, u32[]{:S(2)}) copy-start(bf16[512,640]{1,0:T(8,128)(2,1)} %vt_ref.5) | copy-start | bytes 1966084
  22.2 42.1 %copy-start.10 = (bf16[512,640]{1,0:T(8,128)(2,1)S(1)}, bf16[512,640]{1,0:T(8,128)(2,1)}, u32[]{:S(2)}) copy-start(bf16[512,640]{1,0:T(8,128)(2,1)} %co_ref.3) | copy-start | bytes 1966084
  24.0 13.3 %collective-permute-start.4 = (bf16[512,384]{1,0:T(8,128)(2,1)S(1)}, bf16[512,384]{1,0:T(8,128)(2,1)S(1)}, u32[]{:S(2)}, u32[]{:S(2)}) collective-permute-start(bf16[512,384]{1,0:T(8,128)(2,1)S(1)} %get-tuple-element.43), channel_id=1, source_target_pairs={{0,4},{4,8},{8,12},{12,16},{16,20},{20,24},{24,28},{1,5},{5,9},{9,... | collective-permute-start | bytes 1179656 | tf_op jit(solution)/shard_map/ppermute | solution.py:36
  26.3 38.0 %collective-permute-start.5 = (bf16[512,384]{1,0:T(8,128)(2,1)S(1)}, bf16[512,384]{1,0:T(8,128)(2,1)S(1)}, u32[]{:S(2)}, u32[]{:S(2)}) collective-permute-start(bf16[512,384]{1,0:T(8,128)(2,1)S(1)} %get-tuple-element.44), channel_id=1, source_target_pairs={{4,0},{8,4},{12,8},{16,12},{20,16},{24,20},{28,24},{5,1},{9,5},{13... | collective-permute-start | bytes 1179656 | tf_op jit(solution)/shard_map/ppermute | solution.py:36
  30.2 48.9 %collective-permute-start = (bf16[512,256]{1,0:T(8,128)(2,1)S(1)}, bf16[512,256]{1,0:T(8,128)(2,1)S(1)}, u32[]{:S(2)}, u32[]{:S(2)}) collective-permute-start(bf16[512,256]{1,0:T(8,128)(2,1)S(1)} %get-tuple-element.38), channel_id=1, source_target_pairs={{0,4},{4,8},{8,12},{12,16},{16,20},{20,24},{24,28},{1,5},{5,9},{9,... | collective-permute-start | bytes 786440 | tf_op jit(solution)/shard_map/ppermute | solution.py:36
  37.4 41.7 %collective-permute-start.1 = (bf16[512,256]{1,0:T(8,128)(2,1)S(1)}, bf16[512,256]{1,0:T(8,128)(2,1)S(1)}, u32[]{:S(2)}, u32[]{:S(2)}) collective-permute-start(bf16[512,256]{1,0:T(8,128)(2,1)S(1)} %get-tuple-element.39), channel_id=1, source_target_pairs={{4,0},{8,4},{12,8},{16,12},{20,16},{24,20},{28,24},{5,1},{9,5},{13... | collective-permute-start | bytes 786440 | tf_op jit(solution)/shard_map/ppermute | solution.py:36
  73.8 31.6 %collective-permute-start.7 = (bf16[512,384]{1,0:T(8,128)(2,1)S(1)}, bf16[512,384]{1,0:T(8,128)(2,1)S(1)}, u32[]{:S(2)}, u32[]{:S(2)}) collective-permute-start(bf16[512,384]{1,0:T(8,128)(2,1)S(1)} %get-tuple-element.53), channel_id=1, source_target_pairs={{4,0},{8,4},{12,8},{16,12},{20,16},{24,20},{28,24},{5,1},{9,5},{13... | collective-permute-start | bytes 1179656 | tf_op jit(solution)/shard_map/ppermute | solution.py:36
  75.7 29.7 %collective-permute-start.9 = (bf16[512,384]{1,0:T(8,128)(2,1)S(1)}, bf16[512,384]{1,0:T(8,128)(2,1)S(1)}, u32[]{:S(2)}, u32[]{:S(2)}) collective-permute-start(bf16[512,384]{1,0:T(8,128)(2,1)S(1)} %get-tuple-element.55), channel_id=1, source_target_pairs={{0,4},{4,8},{8,12},{12,16},{16,20},{20,24},{24,28},{1,5},{5,9},{9,... | collective-permute-start | bytes 1179656 | tf_op jit(solution)/shard_map/ppermute | solution.py:36
  85.6 19.8 %collective-permute-start.6 = (bf16[512,256]{1,0:T(8,128)(2,1)S(1)}, bf16[512,256]{1,0:T(8,128)(2,1)S(1)}, u32[]{:S(2)}, u32[]{:S(2)}) collective-permute-start(bf16[512,256]{1,0:T(8,128)(2,1)S(1)} %get-tuple-element.52), channel_id=1, source_target_pairs={{4,0},{8,4},{12,8},{16,12},{20,16},{24,20},{28,24},{5,1},{9,5},{13... | collective-permute-start | bytes 786440 | tf_op jit(solution)/shard_map/ppermute | solution.py:36
  88.4 17.0 %collective-permute-start.8 = (bf16[512,256]{1,0:T(8,128)(2,1)S(1)}, bf16[512,256]{1,0:T(8,128)(2,1)S(1)}, u32[]{:S(2)}, u32[]{:S(2)}) collective-permute-start(bf16[512,256]{1,0:T(8,128)(2,1)S(1)} %get-tuple-element.54), channel_id=1, source_target_pairs={{0,4},{4,8},{8,12},{12,16},{16,20},{20,24},{24,28},{1,5},{5,9},{9,... | collective-permute-start | bytes 786440 | tf_op jit(solution)/shard_map/ppermute | solution.py:36

commit v5 on v4

--- a/solution.py
+++ b/solution.py
@@ -331,6 +331,10 @@
         part_ref[PACK:, :] = remote_sum[base : base + PACK, 128:].astype(BF16)
 
 
+def chained_attend_kernel(tiles_here, plan, *refs):
+    attend_kernel(tiles_here, plan, *refs[:11], *refs[12:])
+
+
 def merge_kernel(bounds, plan, q_ref, k_ref, q_gain_ref, k_gain_ref, *refs):
     count = len(bounds)
     qg, local, from_above, from_below = (refs[index * count : (index + 1) * count] for index in range(4))
@@ -455,15 +459,18 @@
             return (0, head)
 
         full_spec = pl.BlockSpec((rows, HEAD_DIM), whole)
+        earlier = [results[-1][4]] if results else []
+        body = chained_attend_kernel if results else attend_kernel
         results.append(
             pl.pallas_call(
-                functools.partial(attend_kernel, tiles_here),
+                functools.partial(body, tiles_here),
                 grid_spec=pltpu.PrefetchScalarGridSpec(
                     num_scalar_prefetch=1,
                     grid=(size,),
                     in_specs=[full_spec] * 7
                     + [pl.BlockSpec((2 * PACK, HEAD_DIM), part)] * 2
-                    + [pl.BlockSpec((2 * PACK, HEAD_DIM), whole)] * 2,
+                    + [pl.BlockSpec((2 * PACK, HEAD_DIM), whole)] * 2
+                    + [HBM] * len(earlier),
                     out_specs=[pl.BlockSpec((rows, HEAD_DIM), part)] * 3
                     + [pl.BlockSpec((2 * rows, HEAD_DIM), part)]
                     + [pl.BlockSpec((2 * PACK, HEAD_DIM), part)] * 2,
@@ -491,7 +498,7 @@
                 name="attend",
             )(
                 plan, qn, qnt, out_cotangent, kn, knt, values, v_tangent,
-                k_below[index], k_above[index], v_below, v_above,
+                k_below[index], k_above[index], v_below, v_above, *earlier,
             )
         )
     outs, tangents, query_grads, locals_, to_below, to_above = zip(*results)

time: 115 us -> 120 us (1.043)
  waiting for transfers between devices: 23.1 us -> 30.7 us
  starting transfers between devices: 47.2 us -> 45.3 us
    ppermute x10, waiting for transfers between devices: 23.1 us -> 30.7 us  [shifted(): lax.ppermute(value, axis, [(source, source + steps) for source in range(l...]
    ppermute x10, starting transfers between devices: 47.2 us -> 45.3 us  [shifted(): lax.ppermute(value, axis, [(source, source + steps) for source in range(l...]
  transfers between devices with their start and end apart: 10 -> 10, of which waited for: 3 -> 5; matrix products, arithmetic and copies ran while one was open for 1% -> 1% of each run, Pallas kernels for 20% -> 11%
where the time goes in v5:
time: 120 us
  starting transfers between devices  45.3 us (38%)
  Pallas kernels  35.8 us (30%)
  waiting for transfers between devices  30.7 us (26%)
  local copies, waits for them, and re-layouts  5.91 us (5%)
    ppermute x10, starting transfers between devices, shifted(): lax.ppermute(value, axis, [(source, source + steps) for source in range(l...  45.3 us
    ppermute x10, waiting for transfers between devices, shifted(): lax.ppermute(value, axis, [(source, source + steps) for source in range(l...  30.7 us
    pallas_call x2, Pallas kernels, per_device(): pl.pallas_call(functools.partial(body, tiles_here), grid_spec=pltpu.Prefe...  15.9 us
    pallas_call x2, Pallas kernels, head_total(): pl.pallas_call(functools.partial(exchange_kernel, count), out_shape=jax.S...  9.58 us
    unnamed x27, local copies, waits for them, and re-layouts  5.9 us
    pallas_call x1, Pallas kernels, per_device(): pl.pallas_call(functools.partial(prepare_kernel, devices, tiles_here), ou...  3.96 us
  transfers between devices with their start and end apart: 10, of which 5 were waited for; matrix products, arithmetic and copies ran while one was open for 1% of the time, Pallas kernels for 11%

profile of v5, /device:TPU:25, one launch (start us, length us, event | category | flops | bytes accessed | tf_op | source)
XLA Modules:
  0.0 119.9 jit_solution(12640040302039458984)
XLA Ops:
  0.6 0.0 copy-start.1
  0.6 0.0 copy-start
  0.7 0.9 copy.16.key_tiles
  1.5 1.1 copy-done.5
  2.6 1.1 copy-done.7
  3.7 0.7 copy-done.9
  4.4 4.0 %prepare.1 = (s32[16]{0:T(128)S(1)}, bf16[512,640]{1,0:T(8,128)(2,1)S(1)}, bf16[512,640]{1,0:T(8,128)(2,1)S(1)}) custom-call(s32[1]{0:T(128)} %bitcast.position_ref, s32[32]{0:T(128)S(1)} %copy-done.9, s32[32,6]{1,0:T(8,128)S(1)} %copy.16.key_tiles, bf16[512,640]{1,0:T(8,128)(2,1)S(1)} %copy-done.5, bf16[512,640]{1,0:T(8,128)(2,1)S(1)} %copy-done.7), custom_call_target="tpu_custom_call" | custom-call | tf_op jit(solution)/shard_map/prepare/pallas_call | solution.py:412
  8.3 3.1 %collective-permute-start.2 = (bf16[512,640]{1,0:T(8,128)(2,1)S(1)}, bf16[512,640]{1,0:T(8,128)(2,1)S(1)}, u32[]{:S(2)}, u32[]{:S(2)}) collective-permute-start(bf16[512,640]{1,0:T(8,128)(2,1)S(1)} %get-tuple-element.40), channel_id=1, source_target_pairs={{0,4},{4,8},{8,12},{12,16},{16,20},{20,24},{24,28},{1,5},{5,9},{9,... | collective-permute-start | bytes 1966088 | tf_op jit(solution)/shard_map/ppermute | solution.py:36
  11.5 3.1 %collective-permute-start.3 = (bf16[512,640]{1,0:T(8,128)(2,1)S(1)}, bf16[512,640]{1,0:T(8,128)(2,1)S(1)}, u32[]{:S(2)}, u32[]{:S(2)}) collective-permute-start(bf16[512,640]{1,0:T(8,128)(2,1)S(1)} %get-tuple-element.41), channel_id=1, source_target_pairs={{4,0},{8,4},{12,8},{16,12},{20,16},{24,20},{28,24},{5,1},{9,5},{13... | collective-permute-start | bytes 1966088 | tf_op jit(solution)/shard_map/ppermute | solution.py:36
  14.5 0.0 copy-done.11
  14.6 0.0 copy-done.12
  14.6 0.0 copy-done.1
  14.6 0.0 copy-done
  14.6 0.0 copy-start.2
  14.6 1.1 copy-done.2
  15.7 1.1 copy-done.4
  16.8 0.6 sums.1.part_ref
  17.4 4.8 %exchange.2.totals_ref = f32[8,512]{1,0:T(8,128)S(1)} custom-call(f32[8,512]{1,0:T(8,128)S(1)} %sums.1.part_ref), custom_call_target="tpu_custom_call" | custom-call | tf_op jit(solution)/shard_map/exchange/pallas_call | solution.py:173
  22.2 0.0 copy-done.3
  22.2 0.0 copy-start.6
  22.2 0.0 copy-start.8
  22.2 0.0 copy-start.10
  22.3 1.8 %norm.1 = (bf16[512,640]{1,0:T(8,128)(2,1)S(1)}, bf16[512,640]{1,0:T(8,128)(2,1)S(1)}, bf16[512,640]{1,0:T(8,128)(2,1)S(1)}, bf16[512,640]{1,0:T(8,128)(2,1)S(1)...) custom-call(s32[16]{0:T(128)S(1)} %get-tuple-element.33.plan, ...), custom_call_target="tpu_custom_call" | custom-call | tf_op jit(solution)/shard_map/norm/pallas_call | solution.py:442
  24.0 2.3 %collective-permute-start = (bf16[512,256]{1,0:T(8,128)(2,1)S(1)}, bf16[512,256]{1,0:T(8,128)(2,1)S(1)}, u32[]{:S(2)}, u32[]{:S(2)}) collective-permute-start(bf16[512,256]{1,0:T(8,128)(2,1)S(1)} %get-tuple-element.38), channel_id=1, source_target_pairs={{0,4},{4,8},{8,12},{12,16},{16,20},{20,24},{24,28},{1,5},{5,9},{9,... | collective-permute-start | bytes 786440 | tf_op jit(solution)/shard_map/ppermute | solution.py:36
  26.3 3.9 %collective-permute-start.1 = (bf16[512,256]{1,0:T(8,128)(2,1)S(1)}, bf16[512,256]{1,0:T(8,128)(2,1)S(1)}, u32[]{:S(2)}, u32[]{:S(2)}) collective-permute-start(bf16[512,256]{1,0:T(8,128)(2,1)S(1)} %get-tuple-element.39), channel_id=1, source_target_pairs={{4,0},{8,4},{12,8},{16,12},{20,16},{24,20},{28,24},{5,1},{9,5},{13... | collective-permute-start | bytes 786440 | tf_op jit(solution)/shard_map/ppermute | solution.py:36
  30.2 1.9 %collective-permute-start.4 = (bf16[512,384]{1,0:T(8,128)(2,1)S(1)}, bf16[512,384]{1,0:T(8,128)(2,1)S(1)}, u32[]{:S(2)}, u32[]{:S(2)}) collective-permute-start(bf16[512,384]{1,0:T(8,128)(2,1)S(1)} %get-tuple-element.43), channel_id=1, source_target_pairs={{0,4},{4,8},{8,12},{12,16},{16,20},{20,24},{24,28},{1,5},{5,9},{9,... | collective-permute-start | bytes 1179656 | tf_op jit(solution)/shard_map/ppermute | solution.py:36
  32.2 2.4 %collective-permute-done.kb_ref = bf16[512,256]{1,0:T(8,128)(2,1)S(1)} collective-permute-done((bf16[512,256]{1,0:T(8,128)(2,1)S(1)}, bf16[512,256]{1,0:T(8,128)(2,1)S(1)}, u32[]{:S(2)}, u32[]{:S(2)}) %collective-permute-start) | collective-permute-done | bytes 262176 | tf_op jit(solution)/shard_map/ppermute | solution.py:36
  34.6 19.5 %collective-permute-start.5 = (bf16[512,384]{1,0:T(8,128)(2,1)S(1)}, bf16[512,384]{1,0:T(8,128)(2,1)S(1)}, u32[]{:S(2)}, u32[]{:S(2)}) collective-permute-start(bf16[512,384]{1,0:T(8,128)(2,1)S(1)} %get-tuple-element.44), channel_id=1, source_target_pairs={{4,0},{8,4},{12,8},{16,12},{20,16},{24,20},{28,24},{5,1},{9,5},{13... | collective-permute-start | bytes 1179656 | tf_op jit(solution)/shard_map/ppermute | solution.py:36
  54.1 7.4 %collective-permute-done.1.ka_ref = bf16[512,256]{1,0:T(8,128)(2,1)S(1)} collective-permute-done((bf16[512,256]{1,0:T(8,128)(2,1)S(1)}, bf16[512,256]{1,0:T(8,128)(2,1)S(1)}, u32[]{:S(2)}, u32[]{:S(2)}) %collective-permute-start.1) | collective-permute-done | bytes 262176 | tf_op jit(solution)/shard_map/ppermute | solution.py:36
  61.5 0.0 collective-permute-done.2.vb_ref.refs_9_
  61.5 0.0 collective-permute-done.3.va_ref.refs_10_
  61.5 0.0 copy-done.6
  61.5 6.5 %attend.2 = (bf16[512,256]{1,0:T(8,128)(2,1)S(1)}, bf16[512,256]{1,0:T(8,128)(2,1)S(1)}, f32[512,256]{1,0:T(8,128)S(1)}, bf16[1024,256]{1,0:T(8,128)(2,1)S(1)}, ...) custom-call(s32[16]{0:T(128)S(1)} %get-tuple-element.33.plan, ...), custom_call_target="tpu_custom_call" | custom-call | flops 2013265920 | bytes 3145728 | tf_op jit(solution)/shard_map/attend/pallas_call | solution.py:465
  68.0 0.0 collective-permute-done.4.refs_7_
  68.0 1.9 %collective-permute-done.5.refs_8_ = bf16[512,384]{1,0:T(8,128)(2,1)S(1)} collective-permute-done((bf16[512,384]{1,0:T(8,128)(2,1)S(1)}, bf16[512,384]{1,0:T(8,128)(2,1)S(1)}, u32[]{:S(2)}, u32[]{:S(2)}) %collective-permute-start.5) | collective-permute-done | bytes 393248 | tf_op jit(solution)/shard_map/ppermute | solution.py:36
  69.9 9.4 %attend.3 = (bf16[512,384]{1,0:T(8,128)(2,1)S(1)}, bf16[512,384]{1,0:T(8,128)(2,1)S(1)}, f32[512,384]{1,0:T(8,128)S(1)}, bf16[1024,384]{1,0:T(8,128)(2,1)S(1)}, ...) custom-call(s32[16]{0:T(128)S(1)} %get-tuple-element.33.plan, ...), custom_call_target="tpu_custom_call" | custom-call | flops 3019898880 | bytes 4718592 | tf_op jit(solution)/shard_map/attend/pallas_call | solution.py:465
  79.3 1.9 %collective-permute-start.7 = (bf16[512,384]{1,0:T(8,128)(2,1)S(1)}, bf16[512,384]{1,0:T(8,128)(2,1)S(1)}, u32[]{:S(2)}, u32[]{:S(2)}) collective-permute-start(bf16[512,384]{1,0:T(8,128)(2,1)S(1)} %get-tuple-element.53), channel_id=1, source_target_pairs={{4,0},{8,4},{12,8},{16,12},{20,16},{24,20},{28,24},{5,1},{9,5},{13... | collective-permute-start | bytes 1179656 | tf_op jit(solution)/shard_map/ppermute | solution.py:36
  81.3 3.4 %collective-permute-start.9 = (bf16[512,384]{1,0:T(8,128)(2,1)S(1)}, bf16[512,384]{1,0:T(8,128)(2,1)S(1)}, u32[]{:S(2)}, u32[]{:S(2)}) collective-permute-start(bf16[512,384]{1,0:T(8,128)(2,1)S(1)} %get-tuple-element.55), channel_id=1, source_target_pairs={{0,4},{4,8},{8,12},{12,16},{16,20},{20,24},{24,28},{1,5},{5,9},{9,... | collective-permute-start | bytes 1179656 | tf_op jit(solution)/shard_map/ppermute | solution.py:36
  84.7 1.9 %collective-permute-start.8 = (bf16[512,256]{1,0:T(8,128)(2,1)S(1)}, bf16[512,256]{1,0:T(8,128)(2,1)S(1)}, u32[]{:S(2)}, u32[]{:S(2)}) collective-permute-start(bf16[512,256]{1,0:T(8,128)(2,1)S(1)} %get-tuple-element.54), channel_id=1, source_target_pairs={{0,4},{4,8},{8,12},{12,16},{16,20},{20,24},{24,28},{1,5},{5,9},{9,... | collective-permute-start | bytes 786440 | tf_op jit(solution)/shard_map/ppermute | solution.py:36
  86.6 4.3 %collective-permute-start.6 = (bf16[512,256]{1,0:T(8,128)(2,1)S(1)}, bf16[512,256]{1,0:T(8,128)(2,1)S(1)}, u32[]{:S(2)}, u32[]{:S(2)}) collective-permute-start(bf16[512,256]{1,0:T(8,128)(2,1)S(1)} %get-tuple-element.45.refs_11_), channel_id=1, source_target_pairs={{4,0},{8,4},{12,8},{16,12},{20,16},{24,20},{28,24},{5,1},{9,5},{13... | collective-permute-start | bytes 786440 | tf_op jit(solution)/shard_map/ppermute | solution.py:36
  90.9 1.2 pad_maximum_fusion
  92.0 7.4 %collective-permute-done.8.refs_6_ = bf16[512,256]{1,0:T(8,128)(2,1)S(1)} collective-permute-done((bf16[512,256]{1,0:T(8,128)(2,1)S(1)}, bf16[512,256]{1,0:T(8,128)(2,1)S(1)}, u32[]{:S(2)}, u32[]{:S(2)}) %collective-permute-start.8) | collective-permute-done | bytes 262176 | tf_op jit(solution)/shard_map/ppermute | solution.py:36
  99.4 11.7 %collective-permute-done.6.refs_4_ = bf16[512,256]{1,0:T(8,128)(2,1)S(1)} collective-permute-done((bf16[512,256]{1,0:T(8,128)(2,1)S(1)}, bf16[512,256]{1,0:T(8,128)(2,1)S(1)}, u32[]{:S(2)}, u32[]{:S(2)}) %collective-permute-start.6) | collective-permute-done | bytes 262176 | tf_op jit(solution)/shard_map/ppermute | solution.py:36
  111.1 0.0 collective-permute-done.7.refs_5_
  111.1 0.0 collective-permute-done.9.refs_7_
  111.1 2.3 %merge.1 = (bf16[512,640]{1,0:T(8,128)(2,1)}, f32[512,640]{1,0:T(8,128)S(1)}, f32[8,512]{1,0:T(8,128)S(1)}) custom-call(s32[16]{0:T(128)S(1)} %get-tuple-element.33.plan, bf16[512,640]{1,0:T(8,128)(2,1)S(1)} %copy-done, bf16[512,640]{1,0:T(8,128)(2,1)S(1)} %copy-done.1, f32[1,640]{1,0:T(1,128)S(1)} %reshape.20.q_gain_ref, f32[1,640]{1,0:T(1,128)S(1)} %reshape.21.k_gain_ref, ...), custom_call_target="tpu_custom_call" | custom-call | tf_op jit(solution)/shard_map/merge/pallas_call | solution.py:508
  113.4 4.7 %exchange.3.back_ref = f32[8,512]{1,0:T(8,128)S(1)} custom-call(f32[8,512]{1,0:T(8,128)S(1)} %get-tuple-element.56.part_ref), custom_call_target="tpu_custom_call" | custom-call | tf_op jit(solution)/shard_map/exchange/pallas_call | solution.py:173
  118.1 1.7 %final.1 = (bf16[512,640]{1,0:T(8,128)(2,1)}, bf16[512,640]{1,0:T(8,128)(2,1)}) custom-call(f32[8,512]{1,0:T(8,128)S(1)} %exchange.2.totals_ref, f32[8,512]{1,0:T(8,128)S(1)} %exchange.3.back_ref, bf16[512,640]{1,0:T(8,128)(2,1)S(1)} %copy-done, bf16[512,640]{1,0:T(8,128)(2,1)S(1)} %copy-done.1, f32[1,640]{1,0:T(1,128)S(1)} %reshape.20.q_gain_ref, ...), custom_call_target="tpu_custom_call" | custom-call | tf_op jit(solution)/shard_map/final/pallas_call | solution.py:520
  (11 shorter events, 0.0 us)
Async XLA Ops:
  0.6 13.9 %copy-start.1 = (bf16[512,640]{1,0:T(8,128)(2,1)S(1)}, bf16[512,640]{1,0:T(8,128)(2,1)}, u32[]{:S(2)}) copy-start(bf16[512,640]{1,0:T(8,128)(2,1)} %k_ref.7) | copy-start | bytes 1966084
  0.6 13.9 %copy-start = (bf16[512,640]{1,0:T(8,128)(2,1)S(1)}, bf16[512,640]{1,0:T(8,128)(2,1)}, u32[]{:S(2)}) copy-start(bf16[512,640]{1,0:T(8,128)(2,1)} %q_ref.7) | copy-start | bytes 1966084
  1.5 1.1 copy-start.5
  2.6 1.1 copy-start.7
  3.7 0.7 copy-start.9
  4.4 10.2 %copy-start.11 = (f32[640]{0:T(1024)S(1)}, f32[640]{0:T(1024)}, u32[]{:S(2)}) copy-start(f32[640]{0:T(1024)} %param.18) | copy-start | bytes 7684
  4.4 10.2 %copy-start.12 = (f32[640]{0:T(1024)S(1)}, f32[640]{0:T(1024)}, u32[]{:S(2)}) copy-start(f32[640]{0:T(1024)} %param.19) | copy-start | bytes 7684
  8.3 53.2 %collective-permute-start.2 = (bf16[512,640]{1,0:T(8,128)(2,1)S(1)}, bf16[512,640]{1,0:T(8,128)(2,1)S(1)}, u32[]{:S(2)}, u32[]{:S(2)}) collective-permute-start(bf16[512,640]{1,0:T(8,128)(2,1)S(1)} %get-tuple-element.40), channel_id=1, source_target_pairs={{0,4},{4,8},{8,12},{12,16},{16,20},{20,24},{24,28},{1,5},{5,9},{9,... | collective-permute-start | bytes 1966088 | tf_op jit(solution)/shard_map/ppermute | solution.py:36
  11.5 50.0 %collective-permute-start.3 = (bf16[512,640]{1,0:T(8,128)(2,1)S(1)}, bf16[512,640]{1,0:T(8,128)(2,1)S(1)}, u32[]{:S(2)}, u32[]{:S(2)}) collective-permute-start(bf16[512,640]{1,0:T(8,128)(2,1)S(1)} %get-tuple-element.41), channel_id=1, source_target_pairs={{4,0},{8,4},{12,8},{16,12},{20,16},{24,20},{28,24},{5,1},{9,5},{13... | collective-permute-start | bytes 1966088 | tf_op jit(solution)/shard_map/ppermute | solution.py:36
  14.6 1.1 copy-start.2
  15.7 1.1 copy-start.4
  16.8 5.4 %copy-start.3 = (bf16[512,640]{1,0:T(8,128)(2,1)S(1)}, bf16[512,640]{1,0:T(8,128)(2,1)}, u32[]{:S(2)}) copy-start(bf16[512,640]{1,0:T(8,128)(2,1)} %qt_ref.3) | copy-start | bytes 1966084
  22.2 39.3 %copy-start.6 = (bf16[512,640]{1,0:T(8,128)(2,1)S(1)}, bf16[512,640]{1,0:T(8,128)(2,1)}, u32[]{:S(2)}) copy-start(bf16[512,640]{1,0:T(8,128)(2,1)} %refs_5_.1) | copy-start | bytes 1966084
  22.2 39.3 %copy-start.8 = (bf16[512,640]{1,0:T(8,128)(2,1)S(1)}, bf16[512,640]{1,0:T(8,128)(2,1)}, u32[]{:S(2)}) copy-start(bf16[512,640]{1,0:T(8,128)(2,1)} %refs_6_.1) | copy-start | bytes 1966084
  22.2 39.3 %copy-start.10 = (bf16[512,640]{1,0:T(8,128)(2,1)S(1)}, bf16[512,640]{1,0:T(8,128)(2,1)}, u32[]{:S(2)}) copy-start(bf16[512,640]{1,0:T(8,128)(2,1)} %refs_2_.1) | copy-start | bytes 1966084
  24.0 10.5 %collective-permute-start = (bf16[512,256]{1,0:T(8,128)(2,1)S(1)}, bf16[512,256]{1,0:T(8,128)(2,1)S(1)}, u32[]{:S(2)}, u32[]{:S(2)}) collective-permute-start(bf16[512,256]{1,0:T(8,128)(2,1)S(1)} %get-tuple-element.38), channel_id=1, source_target_pairs={{0,4},{4,8},{8,12},{12,16},{16,20},{20,24},{24,28},{1,5},{5,9},{9,... | collective-permute-start | bytes 786440 | tf_op jit(solution)/shard_map/ppermute | solution.py:36
  26.3 35.2 %collective-permute-start.1 = (bf16[512,256]{1,0:T(8,128)(2,1)S(1)}, bf16[512,256]{1,0:T(8,128)(2,1)S(1)}, u32[]{:S(2)}, u32[]{:S(2)}) collective-permute-start(bf16[512,256]{1,0:T(8,128)(2,1)S(1)} %get-tuple-element.39), channel_id=1, source_target_pairs={{4,0},{8,4},{12,8},{16,12},{20,16},{24,20},{28,24},{5,1},{9,5},{13... | collective-permute-start | bytes 786440 | tf_op jit(solution)/shard_map/ppermute | solution.py:36
  30.2 37.8 %collective-permute-start.4 = (bf16[512,384]{1,0:T(8,128)(2,1)S(1)}, bf16[512,384]{1,0:T(8,128)(2,1)S(1)}, u32[]{:S(2)}, u32[]{:S(2)}) collective-permute-start(bf16[512,384]{1,0:T(8,128)(2,1)S(1)} %get-tuple-element.43), channel_id=1, source_target_pairs={{0,4},{4,8},{8,12},{12,16},{16,20},{20,24},{24,28},{1,5},{5,9},{9,... | collective-permute-start | bytes 1179656 | tf_op jit(solution)/shard_map/ppermute | solution.py:36
  34.6 35.4 %collective-permute-start.5 = (bf16[512,384]{1,0:T(8,128)(2,1)S(1)}, bf16[512,384]{1,0:T(8,128)(2,1)S(1)}, u32[]{:S(2)}, u32[]{:S(2)}) collective-permute-start(bf16[512,384]{1,0:T(8,128)(2,1)S(1)} %get-tuple-element.44), channel_id=1, source_target_pairs={{4,0},{8,4},{12,8},{16,12},{20,16},{24,20},{28,24},{5,1},{9,5},{13... | collective-permute-start | bytes 1179656 | tf_op jit(solution)/shard_map/ppermute | solution.py:36
  79.3 31.7 %collective-permute-start.7 = (bf16[512,384]{1,0:T(8,128)(2,1)S(1)}, bf16[512,384]{1,0:T(8,128)(2,1)S(1)}, u32[]{:S(2)}, u32[]{:S(2)}) collective-permute-start(bf16[512,384]{1,0:T(8,128)(2,1)S(1)} %get-tuple-element.53), channel_id=1, source_target_pairs={{4,0},{8,4},{12,8},{16,12},{20,16},{24,20},{28,24},{5,1},{9,5},{13... | collective-permute-start | bytes 1179656 | tf_op jit(solution)/shard_map/ppermute | solution.py:36
  81.3 29.8 %collective-permute-start.9 = (bf16[512,384]{1,0:T(8,128)(2,1)S(1)}, bf16[512,384]{1,0:T(8,128)(2,1)S(1)}, u32[]{:S(2)}, u32[]{:S(2)}) collective-permute-start(bf16[512,384]{1,0:T(8,128)(2,1)S(1)} %get-tuple-element.55), channel_id=1, source_target_pairs={{0,4},{4,8},{8,12},{12,16},{16,20},{20,24},{24,28},{1,5},{5,9},{9,... | collective-permute-start | bytes 1179656 | tf_op jit(solution)/shard_map/ppermute | solution.py:36
  84.7 14.8 %collective-permute-start.8 = (bf16[512,256]{1,0:T(8,128)(2,1)S(1)}, bf16[512,256]{1,0:T(8,128)(2,1)S(1)}, u32[]{:S(2)}, u32[]{:S(2)}) collective-permute-start(bf16[512,256]{1,0:T(8,128)(2,1)S(1)} %get-tuple-element.54), channel_id=1, source_target_pairs={{0,4},{4,8},{8,12},{12,16},{16,20},{20,24},{24,28},{1,5},{5,9},{9,... | collective-permute-start | bytes 786440 | tf_op jit(solution)/shard_map/ppermute | solution.py:36
  86.6 24.5 %collective-permute-start.6 = (bf16[512,256]{1,0:T(8,128)(2,1)S(1)}, bf16[512,256]{1,0:T(8,128)(2,1)S(1)}, u32[]{:S(2)}, u32[]{:S(2)}) collective-permute-start(bf16[512,256]{1,0:T(8,128)(2,1)S(1)} %get-tuple-element.45.refs_11_), channel_id=1, source_target_pairs={{4,0},{8,4},{12,8},{16,12},{20,16},{24,20},{28,24},{5,1},{9,5},{13... | collective-permute-start | bytes 786440 | tf_op jit(solution)/shard_map/ppermute | solution.py:36
